TPU v7x, 32 devices: a whole 2x2x4 slice. The times are simulated.
32 devices in a mesh: groups: 2 (over x), node: 16 (over z, y, core).
Axes of the slice: x: 2, y: 2, z: 4, core: 2. Of those that a mesh axis runs over, the one named last changes fastest.
Arguments:
- hidden: bfloat16 [4096, 4096], P(('groups', 'node')), parts along dimension 0, may hold values from -6 to 6
- queries: bfloat16 [4096, 4096], P(('groups', 'node')), parts along dimension 0, may hold values from -64 to 64
- kv_weight: bfloat16 [4096, 1024], P(None, 'node'), may hold values from -0.09375 to 0.09375
- doc_ids: int32 [4096], P('groups'), parts along dimension 0, may hold values from 0 to 2, never falling along the last dimension, each value on 1 to 1536 neighbouring positions
Outputs:
- attended: bfloat16 [4096, 4096], P(('groups', 'node')), parts along dimension 0
There are 2 independent parts, one for each index of `groups`. A program takes and returns all parts, laid end to end along the dimension named above; an argument that names none is the same for every part. Nothing has to cross between parts.
All inputs are finite; a program needn't handle non-finite values.
Results may differ from a plain program's by a relative error of at most 0.0035.
The roundings to bfloat16 on the way count: a program that leaves them out, or rounds other values in their place, can miss the bound.
Values may be sent and summed in bfloat16 or wider, within the bound.
No kernel may reach another device: no remote copies, remote signals or barrier semaphores. Data moves between devices by JAX's collectives and lax.ppermute only.
A program may use at most 128 MiB of HBM per device.

v0:
```python
import math

import jax
import jax.numpy as jnp
import numpy as np
from jax import lax
from jax.experimental import pallas as pl
from jax.experimental.pallas import tpu as pltpu
from jax.sharding import PartitionSpec as P

KVH = 4
QPK = 8
HD = 128
AXES = ("groups", "node")
MASKED = -1e30
EXP2_SCALE = HD ** (-0.5) * math.log2(math.e)
VMEM_LIMIT = 28 * 1024 * 1024

ANY = pl.BlockSpec(memory_space=pl.ANY)
IN_SMEM = pl.BlockSpec(memory_space=pltpu.SMEM)
IN_VMEM = pl.BlockSpec(memory_space=pltpu.VMEM)


def scalars(*values):
    return jnp.stack([jnp.asarray(v).astype(jnp.int32) for v in values])


def rope_tables(positions):
    half = HD // 2
    freqs = 500000.0 ** (-(jnp.arange(half).astype(jnp.float32) * 2.0) / HD)
    angle = positions.astype(jnp.float32)[:, None] * freqs[None, :]
    return jnp.cos(angle), jnp.sin(angle)


def attend_kernel(rows, chunk, n_q, n_kv, resumed, last, place_ref, start_ref, starts_ref, *refs):
    queries, refs = refs[:n_q], refs[n_q:]
    arrays, refs = refs[: 2 * n_kv], refs[2 * n_kv :]
    state, refs = (refs[:3], refs[3:]) if resumed else ((), refs)
    if last:
        outs, refs = refs[:n_q], refs[n_q:]
        kv, qv, stacked, bias, sem, qsem, ssem, stat_m, stat_l, acc = refs
    else:
        stat_m, stat_l, acc, kv, qv, stacked, bias, sem, qsem, ssem = refs
    part_rows = queries[0].shape[0]
    chunks = arrays[0].shape[0] // chunk

    def q_copy(i):
        column = pl.multiple_of(place_ref[2 + 2 * i], HD)
        return pltpu.make_async_copy(
            queries[i].at[:, pl.ds(column, QPK * HD)],
            qv.at[pl.ds(pl.multiple_of(place_ref[1 + 2 * i], part_rows), part_rows)],
            qsem.at[i],
        )

    def kv_copy(i):
        kind = place_ref[1 + 2 * n_q + n_kv + i // 2]
        kind = kind if i % 2 == 0 else 1 - kind
        return pltpu.make_async_copy(arrays[i], kv.at[i // 2, kind], sem.at[i])

    for i in range(n_q):
        q_copy(i).start()
    running = [
        pltpu.make_async_copy(old, new, ssem.at[i])
        for i, (old, new) in enumerate(zip(state, (stat_m, stat_l, acc)))
    ]
    for copy in running:
        copy.start()
    for i in range(2 * n_kv):
        kv_copy(i).start()
    if not resumed:
        stat_m[...] = jnp.full_like(stat_m, MASKED)
        stat_l[...] = jnp.zeros_like(stat_l)
        acc[...] = jnp.zeros_like(acc)
    for i in range(n_q):
        q_copy(i).wait()
    for h in range(QPK):
        stacked[h * rows : (h + 1) * rows, :] = qv[:, h * HD : (h + 1) * HD]
    for copy in running:
        copy.wait()
    for i in range(2 * n_kv):
        kv_copy(i).wait()

    lanes = chunk // HD
    starts = jnp.concatenate([starts_ref[...]] * lanes, axis=1)
    q_pos = place_ref[0] + lax.broadcasted_iota(jnp.int32, (rows, chunk), 0)
    first_chunk = start_ref[0] // chunk
    end_chunk = (place_ref[0] + rows + chunk - 1) // chunk

    def attend_chunk(i, j, t):
        k_pos = t * chunk + lax.broadcasted_iota(jnp.int32, (rows, chunk), 1)
        bias[...] = jnp.where((k_pos <= q_pos) & (k_pos >= starts), 0.0, MASKED)
        here = pl.ds(pl.multiple_of(j * chunk, chunk), chunk)
        score = lax.dot_general(
            stacked[...],
            kv[i, 0, here, :],
            (((1,), (1,)), ((), ())),
            preferred_element_type=jnp.float32,
        )
        score = (score.reshape(QPK, rows, chunk) + bias[...][None]).reshape(QPK * rows, chunk)
        old = stat_m[...]
        top = jnp.maximum(old, jnp.max(score, axis=1, keepdims=True))
        expo = jnp.exp2((score - jnp.concatenate([top] * lanes, axis=1)) * EXP2_SCALE)
        factor = jnp.exp2((old - top) * EXP2_SCALE)
        stat_m[...] = top
        sums = expo[:, :HD]
        for lane in range(1, lanes):
            sums = sums + expo[:, lane * HD : (lane + 1) * HD]
        stat_l[...] = stat_l[...] * factor + sums
        part = jnp.dot(
            expo.astype(jnp.bfloat16),
            kv[i, 1, here, :],
            preferred_element_type=jnp.float32,
        )
        acc[...] = acc[...] * factor + part

    @pl.loop(0, n_kv * chunks)
    def _(step):
        i, j = step // chunks, step % chunks
        t = place_ref[1 + 2 * n_q + i] * chunks + j

        @pl.when((t >= first_chunk) & (t < end_chunk))
        def _():
            attend_chunk(i, j, t)

    if not last:
        return
    for h in range(QPK):
        at = slice(h * rows, (h + 1) * rows)
        done = acc[at, :] / jnp.sum(stat_l[at, :], axis=1, keepdims=True)
        qv[:, h * HD : (h + 1) * HD] = done.astype(jnp.bfloat16)
    for i in range(n_q):
        at = pl.multiple_of(place_ref[1 + 2 * i], part_rows)
        outs[i][...] = qv[pl.ds(at, part_rows), :]


def attend_starts(doc_ids, first_row, rows):
    docs = lax.dynamic_slice_in_dim(doc_ids, first_row, rows)
    starts = jnp.sum((doc_ids[None, :] < docs[:, None]).astype(jnp.int32), axis=1)
    return starts


def attend(place, starts, queries, arrays, tokens, chunk, state=(), last=True):
    rows = starts.shape[0]
    n_q, n_kv = len(queries), len(arrays) // 2
    part_rows = queries[0].shape[0]
    running = (QPK * rows, HD)
    if last:
        out_shape = [jax.ShapeDtypeStruct((part_rows, QPK * HD), jnp.bfloat16)] * n_q
    else:
        out_shape = [jax.ShapeDtypeStruct(running, jnp.float32)] * 3
    return pl.pallas_call(
        lambda *refs: attend_kernel(rows, chunk, n_q, n_kv, bool(state), last, *refs),
        out_shape=out_shape,
        in_specs=[IN_SMEM, IN_SMEM, IN_VMEM] + [ANY] * (n_q + 2 * n_kv + len(state)),
        out_specs=[IN_VMEM] * len(out_shape),
        scratch_shapes=[
            pltpu.VMEM((n_kv, 2, *arrays[0].shape), jnp.bfloat16),
            pltpu.VMEM((rows, QPK * HD), jnp.bfloat16),
            pltpu.VMEM((QPK * rows, HD), jnp.bfloat16),
            pltpu.VMEM((rows, chunk), jnp.float32),
            pltpu.SemaphoreType.DMA((2 * n_kv,)),
            pltpu.SemaphoreType.DMA((n_q,)),
            pltpu.SemaphoreType.DMA((3,)),
        ]
        + [pltpu.VMEM(running, jnp.float32)] * (3 if last else 0),
        compiler_params=pltpu.CompilerParams(vmem_limit_bytes=VMEM_LIMIT),
        cost_estimate=pl.CostEstimate(
            flops=rows * tokens * HD,
            bytes_accessed=rows * tokens,
            transcendentals=0,
        ),
        name="attend",
    )(
        place,
        starts[:1],
        jnp.broadcast_to(starts[:, None], (rows, HD)),
        *queries,
        *arrays,
        *state,
    )


def project_kernel(rows, n_hidden, n_pieces, place_ref, cos_ref, sin_ref, *refs):
    hidden = refs[:n_hidden]
    pieces = refs[n_hidden : n_hidden + n_pieces]
    out_ref = refs[n_hidden + n_pieces]
    hbuf, wbuf, hsem, wsem = refs[n_hidden + n_pieces + 1 :]

    def w_copy(i):
        size = pieces[i].shape[0]
        at = pl.multiple_of(place_ref[2 + n_hidden + 2 * i], size)
        return pltpu.make_async_copy(pieces[i], wbuf.at[pl.ds(at, size)], wsem.at[i])

    def h_copy(i):
        at = pl.multiple_of(place_ref[1 + i] * rows, rows)
        return pltpu.make_async_copy(hidden[i], hbuf.at[pl.ds(at, rows)], hsem.at[i])

    for i in range(n_pieces):

        @pl.when(place_ref[1 + n_hidden + 2 * i] == 1)
        def _():
            w_copy(i).start()

    for i in range(n_hidden):
        h_copy(i).start()
    for i in range(n_pieces):

        @pl.when(place_ref[1 + n_hidden + 2 * i] == 1)
        def _():
            w_copy(i).wait()

    for i in range(n_hidden):
        h_copy(i).wait()
    head = lax.dot_general(
        hbuf[...], wbuf[...], (((1,), (1,)), ((), ())), preferred_element_type=jnp.float32
    )
    turned = head * cos_ref[...] + pltpu.roll(head, HD // 2, 1) * sin_ref[...]
    out_ref[...] = jnp.where(place_ref[0] == 1, turned, head).astype(jnp.bfloat16)


def project(place, cos, sin, hidden, pieces):
    rows, depth = hidden[0].shape
    n = len(hidden)
    return pl.pallas_call(
        lambda *refs: project_kernel(rows, n, len(pieces), *refs),
        out_shape=jax.ShapeDtypeStruct((n * rows, HD), jnp.bfloat16),
        in_specs=[IN_SMEM, IN_VMEM, IN_VMEM] + [ANY] * (n + len(pieces)),
        out_specs=IN_VMEM,
        scratch_shapes=[
            pltpu.VMEM((n * rows, depth), jnp.bfloat16),
            pltpu.VMEM((HD, depth), jnp.bfloat16),
            pltpu.SemaphoreType.DMA((n,)),
            pltpu.SemaphoreType.DMA((len(pieces),)),
        ],
        compiler_params=pltpu.CompilerParams(vmem_limit_bytes=VMEM_LIMIT),
        cost_estimate=pl.CostEstimate(
            flops=rows * depth * HD,
            bytes_accessed=rows * depth,
            transcendentals=0,
        ),
        name="project",
    )(place, cos, sin, *hidden, *pieces)


def join_kernel(place_ref, *refs):
    n = len(refs) - 4
    out_ref, whole, sem, out_sem = refs[n:]
    copies = []
    for i in range(n):
        height, width = refs[i].shape
        at = pl.multiple_of(place_ref[2 * i + 1], width)
        row = pl.multiple_of(place_ref[2 * i], height)
        copies.append(
            pltpu.make_async_copy(
                refs[i], whole.at[pl.ds(row, height), pl.ds(at, width)], sem.at[i]
            )
        )
    for c in copies:
        c.start()
    for c in copies:
        c.wait()
    copy = pltpu.make_async_copy(whole, out_ref, out_sem)
    copy.start()
    copy.wait()


def join(place, parts, shape):
    return pl.pallas_call(
        join_kernel,
        out_shape=jax.ShapeDtypeStruct(shape, parts[0].dtype),
        in_specs=[IN_SMEM] + [ANY] * len(parts),
        out_specs=ANY,
        scratch_shapes=[
            pltpu.VMEM(shape, parts[0].dtype),
            pltpu.SemaphoreType.DMA((len(parts),)),
            pltpu.SemaphoreType.DMA,
        ],
        compiler_params=pltpu.CompilerParams(vmem_limit_bytes=VMEM_LIMIT),
        name="join",
    )(place, *parts)


def by_planes(hidden, queries, kv_weight, doc_ids):
    rows = hidden.shape[0]
    tokens = doc_ids.shape[0]
    width = kv_weight.shape[1]
    part = width // 2
    columns = QPK * HD
    x = lax.axis_index("groups")
    node = lax.axis_index("node")
    z, y, c = node // 4, (node // 2) % 2, node % 2

    def hop(fn):
        pairs = []
        for i in range(32):
            to = fn(i // 16, (i // 4) % 4, (i // 2) % 2, i % 2)
            if to is not None:
                pairs.append((i, ((to[0] * 4 + to[1]) * 2 + to[2]) * 2 + to[3]))
        return lambda v: lax.ppermute(v, AXES, pairs)

    to_core = hop(lambda x, z, y, c: (x, z, y, 1 - c))
    to_y = hop(lambda x, z, y, c: (x, z, 1 - y, c))
    to_both = hop(lambda x, z, y, c: (x, z, 1 - y, 1 - c))
    to_x = hop(lambda x, z, y, c: (1 - x, z, y, c))
    near = hop(lambda x, z, y, c: (x, z ^ 1, y, c))
    far = hop(lambda x, z, y, c: (x, z ^ (2 + c), y, z % 2))
    up_near = hop(lambda x, z, y, c: (x, z + 1, y, c) if z % 2 == 0 else None)
    up_far = hop(lambda x, z, y, c: (x, z + 2, y, c) if z < 2 else None)
    swap_high = hop(lambda x, z, y, c: (x, z ^ 1, y, c) if z >= 2 else None)

    chunk = math.gcd(tokens, 512)
    tables = [[] for _ in range(9)]
    for i in range(32):
        ix, iz, iy, ic = i // 16, (i // 4) % 4, (i // 2) % 2, i % 2
        blocks = [2 * iy + ic, 2 * iy + 1 - ic, 2 * (1 - iy) + ic, 2 * (1 - iy) + 1 - ic]
        own = int(ic == iz % 2)
        tables[0].append(
            [int(iz < 2), *blocks]
            + [own, ic * width, 1 - own, ic * width, 1, (1 - ic) * width]
        )
        side = (1 - own) * width
        tables[6].append(
            [int(iz >= 2), *blocks]
            + [1, side + ix * part, 1, side + (1 - ix) * part]
            + [1, width - side + ix * part, 1, width - side + (1 - ix) * part]
        )
        planes = [iz, iz - 1 if iz % 2 else -1, iz - 2, (iz ^ 1) - 2 if iz >= 2 else -1]
        for t, block in enumerate((2 * (1 - iy), 2 * iy + 1 - ic, 2 * iy + ic)):
            first = (4 * iz + block) * rows
            q_rows = [ic * rows, 0, (1 - ic) * rows, 0] if t == 0 else [0, 0]
            calls = (
                [(1, planes[:1]), (4, planes[1:3]), (2, planes[3:])],
                [(3, planes[:1]), (7, planes[1:])],
                [(8, planes)],
            )[t]
            for at, some in calls:
                kinds = [max(plane, 0) // 2 for plane in some]
                tables[at].append([first] + q_rows + some + kinds)
        heads = [iy + 2 * ic, iy + 2 * (1 - ic), iy + 2 * (1 - ic)]
        heads += [1 - iy + 2 * ic, 1 - iy + 2 * (1 - ic)]
        tops = [0, 0, rows // 2, 0, 0]
        tables[5].append([v for top, h in zip(tops, heads) for v in (top, h * columns)])
    widths = [len(t[0]) for t in tables]
    whole = np.concatenate([np.asarray(t, np.int32) for t in tables], axis=1)
    place = lax.dynamic_slice_in_dim(jnp.asarray(whole), x * 16 + node, 1, 0)[0]
    at, places = 0, []
    for w in widths:
        places.append(place[at : at + w])
        at += w

    weight = kv_weight.T
    far_0 = far(lax.dynamic_slice_in_dim(weight, x * part, part, 0))
    near_0 = near(weight)
    hidden_y = to_y(hidden)
    hidden_c = to_core(hidden)

    positions = z * 4 * rows + jnp.arange(4 * rows)
    cosine, sine = rope_tables(positions)
    cos = jnp.concatenate([cosine, cosine], axis=1)
    sin = jnp.concatenate([-sine, sine], axis=1)
    starts = [
        attend_starts(doc_ids, (4 * z + block) * rows, size)
        for block, size in ((2 * (1 - y), 2 * rows), (2 * y + 1 - c, rows), (2 * y + c, rows))
    ]
    q_own, *q_away = [
        lax.dynamic_slice_in_dim(queries, h * columns, columns, 1)
        for h in (y + 2 * c, y + 2 * (1 - c), 1 - y + 2 * c, 1 - y + 2 * (1 - c))
    ]
    far_0, cos, sin, starts, places, q_own, q_away = lax.optimization_barrier(
        (far_0, cos, sin, starts, places, q_own, q_away)
    )
    far_1, far_0x = near(far_0), to_x(far_0)
    far_1, far_0x = lax.optimization_barrier((far_1, far_0x))
    far_1x = to_x(far_1)
    near_c = to_core(jnp.where(c == z % 2, near_0, weight))
    q_core = to_core(q_away[0])
    hidden_y, far_1, q_away, q_core = lax.optimization_barrier((hidden_y, far_1, q_away, q_core))
    hidden_yc = to_core(hidden_y)
    q_y, q_both = to_y(q_away[1]), to_both(q_away[2])

    plane_hidden = [hidden, hidden_c, hidden_y, hidden_yc]
    kv_a = project(places[0], cos, sin, plane_hidden, [weight, near_0, near_c])
    kv_a, places[6] = lax.optimization_barrier((kv_a, places[6]))
    kv_b = project(places[6], cos, sin, plane_hidden, [far_0, far_0x, far_1, far_1x])

    a_near, a_far = up_near(kv_a), up_far(kv_a)
    b_near, b_far = up_near(kv_b), up_far(kv_b)
    own, near_below = [kv_a, kv_b], [a_near, b_near]
    q_partner = [q_y, q_both]
    begun = attend(places[1], starts[0], q_partner, own, tokens, chunk, last=False)
    begun_beside = attend(places[3], starts[1], [q_core], own, tokens, chunk, last=False)
    begun, begun_beside, a_far = lax.optimization_barrier((begun, begun_beside, a_far))
    other = [swap_high(a_far), swap_high(b_far)]
    below = near_below + [a_far, b_far]
    begun = attend(places[4], starts[0], q_partner, below, tokens, chunk, begun, last=False)
    across = attend(places[2], starts[0], q_partner, other, tokens, chunk, begun)
    back = [to_y(across[0]), to_both(across[1])]
    below += other
    across, places[7] = lax.optimization_barrier((across, places[7]))
    beside = attend(places[7], starts[1], [q_core], below, tokens, chunk, begun_beside)
    beside, places[8] = lax.optimization_barrier((beside, places[8]))
    here = attend(places[8], starts[2], [q_own], own + below, tokens, chunk)
    parts = [here[0], to_core(beside[0][: rows // 2]), to_core(beside[0][rows // 2 :])] + back
    return join(places[5], parts, queries.shape)


def by_gathers(hidden, queries, kv_weight, doc_ids):
    rows = hidden.shape[0]
    tokens = doc_ids.shape[0]
    me = lax.axis_index("node")
    whole = lax.all_gather(kv_weight, "node", axis=1, tiled=True)
    projected = jnp.dot(hidden, whole, preferred_element_type=jnp.float32)
    split = whole.shape[1] // 2
    cosine, sine = rope_tables(me * rows + jnp.arange(rows))
    keys = projected[:, :split].reshape(rows, KVH, HD)
    a, b = keys[..., : HD // 2], keys[..., HD // 2 :]
    cosine, sine = cosine[:, None, :], sine[:, None, :]
    keys = jnp.concatenate([a * cosine - b * sine, b * cosine + a * sine], axis=-1)
    both = jnp.concatenate([keys, projected[:, split:].reshape(rows, KVH, HD)], axis=1)
    both = both.astype(jnp.bfloat16).transpose(1, 0, 2)
    whole = lax.all_gather(both, "node", axis=1, tiled=True)
    chunk = math.gcd(tokens, 512)
    starts = attend_starts(doc_ids, me * rows, rows)
    outs = []
    for g in range(KVH):
        place = scalars(me * rows, 0, g * QPK * HD, 0, 0)
        pair = [whole[g], whole[KVH + g]]
        outs += attend(place, starts, [queries], pair, tokens, chunk)
    return jnp.concatenate(outs, axis=1)


def solution(mesh):
    planes = mesh.shape["groups"] == 2 and mesh.shape["node"] == 16
    in_specs = (P(AXES, None), P(AXES, None), P(None, "node"), P("groups"))
    return jax.shard_map(
        by_planes if planes else by_gathers,
        mesh=mesh,
        in_specs=in_specs,
        out_specs=P(AXES, None),
        check_vma=False,
    )
```

profile of v0, /device:TPU:17, one launch (start us, length us, event | category | flops | bytes accessed | tf_op | source)
XLA Modules:
  0.0 83.2 jit_solution(8301214791471768009)
XLA Ops:
  0.0 1.7 %dynamic-slice_bitcast_fusion = bf16[32,4096]{1,0:T(8,128)(2,1)} fusion(bf16[4096,64]{0,1:T(8,128)(2,1)} %param.7, s32[]{:T(128)S(6)} %select_n.57), kind=kLoop, calls=%fused_computation.8 | loop fusion | bytes 524292 | tf_op jit(solution)/shard_map/dynamic_slice | solution.py:352
  2.4 1.2 %collective-permute-start.1 = (bf16[128,4096]{1,0:T(8,128)(2,1)}, bf16[128,4096]{1,0:T(8,128)(2,1)S(1)}, u32[]{:S(2)}, u32[]{:S(2)}) collective-permute-start(bf16[128,4096]{1,0:T(8,128)(2,1)} %refs_3_.3), channel_id=1, source_target_pairs={{0,2},{1,3},{2,0},{3,1},{4,6},{5,7},{6,4},{7,5},{8,10},{9,11},{10,... | collective-permute-start | bytes 3145736 | tf_op jit(solution)/shard_map/ppermute | solution.py:299
  6.0 1.0 %convert_reduce_fusion = s32[256]{0:T(256)S(1)} fusion(s32[2048]{0:T(1024)} %param.8, s32[256]{0:T(256)S(1)} %dynamic_slice.28), kind=kLoop, calls=%fused_computation | loop fusion | flops 1572608 | bytes 10240 | tf_op jit(solution)/shard_map/reduce_sum | solution.py:138
  7.9 1.0 %convert_reduce_fusion.1 = (s32[128]{0:T(128)S(1)}, s32[128]{0:T(128)S(1)}) fusion(s32[2048]{0:T(1024)} %param.8, s32[128]{0:T(128)S(1)} %get-tuple-element.112, s32[128]{0:T(128)S(1)} %get-tuple-element.111), kind=kLoop, calls=%fused_computation.1 | loop fusion | flops 1572608 | bytes 10240 | tf_op jit(solution)/shard_map/reduce_sum | solution.py:138
  9.0 2.1 %constant_dynamic-slice_fusion = (bf16[128,1024]{1,0:T(8,128)(2,1)}, bf16[128,1024]{1,0:T(8,128)(2,1)}, bf16[128,1024]{1,0:T(8,128)(2,1)S(1)}, bf16[128,1024]{1,0:T(8,128)(2,1)}) fusion(bf16[128,4096]{1,0:T(8,128)(2,1)} %param.6, s32[]{:T(128)S(6)} %select_n.69, s32[]{:T(128)S(6)} %select_n.67, s32[]{:T(128)S(6)} %select_n.66, s32[]{:T(128)S(6)} %select_n.68), kind=kLoop, calls=%fused_computation.11 | loop fusion | bytes 2097168 | tf_op jit(solution)/shard_map/dynamic_slice | solution.py:366
  11.2 1.0 %fusion = (f32[512,64]{1,0:T(8,128)S(1)}, f32[512,64]{1,0:T(8,128)S(1)}, f32[512,64]{1,0:T(8,128)S(1)}) fusion(f32[64]{0:T(128)S(1)} %multiply_power_fusion, f32[512]{0:T(512)S(1)} %add_convert_fusion), kind=kLoop, calls=%fused_computation.9 | loop fusion | flops 65536 | bytes 395520 | tf_op jit(solution)/shard_map/neg | solution.py:360
  12.4 1.9 %collective-permute-done.refs_7_ = bf16[32,4096]{1,0:T(8,128)(2,1)} collective-permute-done((bf16[32,4096]{1,0:T(8,128)(2,1)}, bf16[32,4096]{1,0:T(8,128)(2,1)}, u32[]{:S(2)}, u32[]{:S(2)}) %collective-permute-start) | collective-permute-done | bytes 262176 | tf_op jit(solution)/shard_map/ppermute | solution.py:299
  14.3 2.5 %collective-permute-start.2 = (bf16[32,4096]{1,0:T(8,128)(2,1)}, bf16[32,4096]{1,0:T(8,128)(2,1)}, u32[]{:S(2)}, u32[]{:S(2)}) collective-permute-start(bf16[32,4096]{1,0:T(8,128)(2,1)} %collective-permute-done.refs_7_), channel_id=1, source_target_pairs={{0,4},{1,5},{2,6},{3,7},{4,0},{5,1},{6,2},{7,3},{8,12},{9,13},{10,... | collective-permute-start | bytes 786440 | tf_op jit(solution)/shard_map/ppermute | solution.py:299
  16.9 1.2 %collective-permute-start.3 = (bf16[32,4096]{1,0:T(8,128)(2,1)}, bf16[32,4096]{1,0:T(8,128)(2,1)}, u32[]{:S(2)}, u32[]{:S(2)}) collective-permute-start(bf16[32,4096]{1,0:T(8,128)(2,1)} %collective-permute-done.refs_7_), channel_id=1, source_target_pairs={{0,16},{1,17},{2,18},{3,19},{4,20},{5,21},{6,22},{7,23},{8,24},{9,... | collective-permute-start | bytes 786440 | tf_op jit(solution)/shard_map/ppermute | solution.py:299
  18.1 8.3 %collective-permute-done.2.refs_9_ = bf16[32,4096]{1,0:T(8,128)(2,1)} collective-permute-done((bf16[32,4096]{1,0:T(8,128)(2,1)}, bf16[32,4096]{1,0:T(8,128)(2,1)}, u32[]{:S(2)}, u32[]{:S(2)}) %collective-permute-start.2) | collective-permute-done | bytes 262176 | tf_op jit(solution)/shard_map/ppermute | solution.py:299
  26.4 1.5 %collective-permute-start.7 = (bf16[128,4096]{1,0:T(8,128)(2,1)S(1)}, bf16[128,4096]{1,0:T(8,128)(2,1)S(1)}, u32[]{:S(2)}, u32[]{:S(2)}) collective-permute-start(bf16[128,4096]{1,0:T(8,128)(2,1)S(1)} %copy-done), channel_id=1, source_target_pairs={{0,1},{1,0},{2,3},{3,2},{4,5},{5,4},{6,7},{7,6},{8,9},{9,8},{10,11... | collective-permute-start | bytes 3145736 | tf_op jit(solution)/shard_map/ppermute | solution.py:299
  28.3 1.4 %collective-permute-start.10 = (bf16[64,4096]{1,0:T(8,128)(2,1)S(1)}, bf16[64,4096]{1,0:T(8,128)(2,1)S(1)}, u32[]{:S(2)}, u32[]{:S(2)}) collective-permute-start(bf16[64,4096]{1,0:T(8,128)(2,1)S(1)} %broadcast_select_fusion), channel_id=1, source_target_pairs={{0,1},{1,0},{2,3},{3,2},{4,5},{5,4},{6,7},{7,6},{8,9},{9,8},{10,11... | collective-permute-start | bytes 1572872 | tf_op jit(solution)/shard_map/ppermute | solution.py:299
  29.7 1.2 %collective-permute-start.11 = (bf16[32,4096]{1,0:T(8,128)(2,1)}, bf16[32,4096]{1,0:T(8,128)(2,1)S(1)}, u32[]{:S(2)}, u32[]{:S(2)}) collective-permute-start(bf16[32,4096]{1,0:T(8,128)(2,1)} %collective-permute-done.2.refs_9_), channel_id=1, source_target_pairs={{0,16},{1,17},{2,18},{3,19},{4,20},{5,21},{6,22},{7,23},{8,24},{9,... | collective-permute-start | bytes 786440 | tf_op jit(solution)/shard_map/ppermute | solution.py:299
  30.9 0.9 %collective-permute-start.5 = (bf16[128,1024]{1,0:T(8,128)(2,1)S(1)}, bf16[128,1024]{1,0:T(8,128)(2,1)S(1)}, u32[]{:S(2)}, u32[]{:S(2)}) collective-permute-start(bf16[128,1024]{1,0:T(8,128)(2,1)S(1)} %copy-done.3), channel_id=1, source_target_pairs={{0,2},{1,3},{2,0},{3,1},{4,6},{5,7},{6,4},{7,5},{8,10},{9,11},{10,... | collective-permute-start | bytes 786440 | tf_op jit(solution)/shard_map/ppermute | solution.py:299
  32.5 1.0 %collective-permute-start.6 = (bf16[128,1024]{1,0:T(8,128)(2,1)S(1)}, bf16[128,1024]{1,0:T(8,128)(2,1)S(1)}, u32[]{:S(2)}, u32[]{:S(2)}) collective-permute-start(bf16[128,1024]{1,0:T(8,128)(2,1)S(1)} %copy-done.2), channel_id=1, source_target_pairs={{0,3},{1,2},{2,1},{3,0},{4,7},{5,6},{6,5},{7,4},{8,11},{9,10},{10,... | collective-permute-start | bytes 786440 | tf_op jit(solution)/shard_map/ppermute | solution.py:299
  33.5 3.0 %project.2.refs_5_.refs_4_ = bf16[512,128]{1,0:T(8,128)(2,1)S(1)} custom-call(s32[11]{0:T(128)S(1)} %get-tuple-element.65.refs_0_, f32[512,128]{1,0:T(8,128)S(1)} %get-tuple-element.66.refs_1_, f32[512,128]{1,0:T(8,128)S(1)} %get-tuple-element.67.refs_2_, bf16[128,4096]{1,0:T(8,128)(2,1)S(1)} %copy-done, ...), custom_call_target="tpu_custom_call" | custom-call | flops 67108864 | bytes 524288 | tf_op jit(solution)/shard_map/project/pallas_call | solution.py:224
  36.5 1.3 %collective-permute-start.12 = (bf16[512,128]{1,0:T(8,128)(2,1)S(1)}, bf16[512,128]{1,0:T(8,128)(2,1)S(1)}, u32[]{:S(2)}, u32[]{:S(2)}) collective-permute-start(bf16[512,128]{1,0:T(8,128)(2,1)S(1)} %project.2.refs_5_.refs_4_), channel_id=1, source_target_pairs={{0,8},{1,9},{2,10},{3,11},{4,12},{5,13},{6,14},{7,15},{16,24},{17,... | collective-permute-start | bytes 393224 | tf_op jit(solution)/shard_map/ppermute | solution.py:299
  37.8 3.1 %project.3.refs_6_.refs_5_ = bf16[512,128]{1,0:T(8,128)(2,1)S(1)} custom-call(s32[13]{0:T(128)S(1)} %slice_bitcast_fusion.2.refs_0_, f32[512,128]{1,0:T(8,128)S(1)} %get-tuple-element.66.refs_1_, f32[512,128]{1,0:T(8,128)S(1)} %get-tuple-element.67.refs_2_, bf16[128,4096]{1,0:T(8,128)(2,1)S(1)} %copy-done, ...), custom_call_target="tpu_custom_call" | custom-call | flops 67108864 | bytes 524288 | tf_op jit(solution)/shard_map/project/pallas_call | solution.py:224
  40.9 1.3 %collective-permute-start.14 = (bf16[512,128]{1,0:T(8,128)(2,1)S(1)}, bf16[512,128]{1,0:T(8,128)(2,1)S(1)}, u32[]{:S(2)}, u32[]{:S(2)}) collective-permute-start(bf16[512,128]{1,0:T(8,128)(2,1)S(1)} %project.3.refs_6_.refs_5_), channel_id=1, source_target_pairs={{0,8},{1,9},{2,10},{3,11},{4,12},{5,13},{6,14},{7,15},{16,24},{17,... | collective-permute-start | bytes 393224 | tf_op jit(solution)/shard_map/ppermute | solution.py:299
  42.7 3.2 %collective-permute-start.17 = (bf16[512,128]{1,0:T(8,128)(2,1)S(1)}, bf16[512,128]{1,0:T(8,128)(2,1)S(1)}, u32[]{:S(2)}, u32[]{:S(2)}) collective-permute-start(bf16[512,128]{1,0:T(8,128)(2,1)S(1)} %project.3.refs_6_.refs_5_), channel_id=1, source_target_pairs={{0,4},{1,5},{2,6},{3,7},{8,12},{9,13},{10,14},{11,15},{16,20},{17,... | collective-permute-start | bytes 393224 | tf_op jit(solution)/shard_map/ppermute | solution.py:299
  46.0 2.6 %attend.7 = (f32[1024,128]{1,0:T(8,128)S(1)}, f32[1024,128]{1,0:T(8,128)S(1)}, f32[1024,128]{1,0:T(8,128)S(1)}) custom-call(s32[5]{0:T(128)S(1)} %slice_bitcast_fusion.5.refs_0_, s32[1]{0:T(128)S(1)} %bitcast.26, s32[128,128]{1,0:T(8,128)S(1)} %broadcast_in_dim.7.refs_2_, bf16[128,1024]{1,0:T(8,128)(2,1)} %collective-permute-done.4.refs_3_, ...), custom_call_target="tpu_custom_call" | custom-call | flops 33554432 | bytes 262144 | tf_op jit(solution)/shard_map/attend/pallas_call | solution.py:151
  48.7 1.3 %collective-permute-start.16 = (bf16[512,128]{1,0:T(8,128)(2,1)S(1)}, bf16[512,128]{1,0:T(8,128)(2,1)S(1)}, u32[]{:S(2)}, u32[]{:S(2)}) collective-permute-start(bf16[512,128]{1,0:T(8,128)(2,1)S(1)} %project.2.refs_5_.refs_4_), channel_id=1, source_target_pairs={{0,4},{1,5},{2,6},{3,7},{8,12},{9,13},{10,14},{11,15},{16,20},{17,... | collective-permute-start | bytes 393224 | tf_op jit(solution)/shard_map/ppermute | solution.py:299
  50.1 3.7 %attend.6 = (f32[2048,128]{1,0:T(8,128)S(1)}, f32[2048,128]{1,0:T(8,128)S(1)}, f32[2048,128]{1,0:T(8,128)S(1)}) custom-call(s32[7]{0:T(128)S(1)} %get-tuple-element.64.refs_0_, s32[1]{0:T(128)} %slice.90.refs_1_, s32[256,128]{1,0:T(8,128)S(1)} %broadcast_in_dim.6.refs_2_, bf16[128,1024]{1,0:T(8,128)(2,1)S(1)} %collective-permute-done.5.refs_3_, ...), custom_call_target="tpu_custom_call" | custom-call | flops 67108864 | bytes 524288 | tf_op jit(solution)/shard_map/attend/pallas_call | solution.py:151
  53.8 1.9 %collective-permute-start.13 = (bf16[512,128]{1,0:T(8,128)(2,1)S(1)}, bf16[512,128]{1,0:T(8,128)(2,1)S(1)}, u32[]{:S(2)}, u32[]{:S(2)}) collective-permute-start(bf16[512,128]{1,0:T(8,128)(2,1)S(1)} %collective-permute-done.12.refs_7_.refs_6_.refs_8_), channel_id=1, source_target_pairs={{8,12},{9,13},{10,14},{11,15},{12,8},{13,9},{14,10},{15,11},{24,28... | collective-permute-start | bytes 393224 | tf_op jit(solution)/shard_map/ppermute | solution.py:299
  55.8 3.4 %collective-permute-start.15 = (bf16[512,128]{1,0:T(8,128)(2,1)S(1)}, bf16[512,128]{1,0:T(8,128)(2,1)S(1)}, u32[]{:S(2)}, u32[]{:S(2)}) collective-permute-start(bf16[512,128]{1,0:T(8,128)(2,1)S(1)} %collective-permute-done.14.refs_8_.refs_7_.refs_9_), channel_id=1, source_target_pairs={{8,12},{9,13},{10,14},{11,15},{12,8},{13,9},{14,10},{15,11},{24,28... | collective-permute-start | bytes 393224 | tf_op jit(solution)/shard_map/ppermute | solution.py:299
  59.1 4.1 %attend.8 = (f32[2048,128]{1,0:T(8,128)S(1)}, f32[2048,128]{1,0:T(8,128)S(1)}, f32[2048,128]{1,0:T(8,128)S(1)}) custom-call(s32[9]{0:T(128)S(1)} %get-tuple-element.84.refs_0_, s32[1]{0:T(128)} %slice.90.refs_1_, s32[256,128]{1,0:T(8,128)S(1)} %broadcast_in_dim.6.refs_2_, bf16[128,1024]{1,0:T(8,128)(2,1)S(1)} %collective-permute-done.5.refs_3_, ...), custom_call_target="tpu_custom_call" | custom-call | flops 67108864 | bytes 524288 | tf_op jit(solution)/shard_map/attend/pallas_call | solution.py:151
  63.3 4.1 %attend.9 = (bf16[128,1024]{1,0:T(8,128)(2,1)S(1)}, bf16[128,1024]{1,0:T(8,128)(2,1)S(1)}) custom-call(s32[7]{0:T(128)S(1)} %get-tuple-element.55.refs_0_, s32[1]{0:T(128)} %slice.90.refs_1_, s32[256,128]{1,0:T(8,128)S(1)} %broadcast_in_dim.6.refs_2_, bf16[128,1024]{1,0:T(8,128)(2,1)S(1)} %collective-permute-done.5.refs_3_, ...), custom_call_target="tpu_custom_call" | custom-call | flops 67108864 | bytes 524288 | tf_op jit(solution)/shard_map/attend/pallas_call | solution.py:151
  67.5 1.0 %collective-permute-start.20 = (bf16[128,1024]{1,0:T(8,128)(2,1)S(1)}, bf16[128,1024]{1,0:T(8,128)(2,1)S(1)}, u32[]{:S(2)}, u32[]{:S(2)}) collective-permute-start(bf16[128,1024]{1,0:T(8,128)(2,1)S(1)} %get-tuple-element.91), channel_id=1, source_target_pairs={{0,2},{1,3},{2,0},{3,1},{4,6},{5,7},{6,4},{7,5},{8,10},{9,11},{10,... | collective-permute-start | bytes 786440 | tf_op jit(solution)/shard_map/ppermute | solution.py:299
  68.4 2.8 %collective-permute-start.21 = (bf16[128,1024]{1,0:T(8,128)(2,1)S(1)}, bf16[128,1024]{1,0:T(8,128)(2,1)S(1)}, u32[]{:S(2)}, u32[]{:S(2)}) collective-permute-start(bf16[128,1024]{1,0:T(8,128)(2,1)S(1)} %get-tuple-element.92), channel_id=1, source_target_pairs={{0,3},{1,2},{2,1},{3,0},{4,7},{5,6},{6,5},{7,4},{8,11},{9,10},{10,... | collective-permute-start | bytes 786440 | tf_op jit(solution)/shard_map/ppermute | solution.py:299
  71.3 4.0 %attend.10 = bf16[128,1024]{1,0:T(8,128)(2,1)S(1)} custom-call(s32[9]{0:T(128)S(1)} %get-tuple-element.94.refs_0_, s32[1]{0:T(128)S(1)} %bitcast.27, s32[128,128]{1,0:T(8,128)S(1)} %broadcast_in_dim.7.refs_2_, bf16[128,1024]{1,0:T(8,128)(2,1)} %collective-permute-done.4.refs_3_, bf16[512,128]{1,0:T(8,128)(2,1)S(1)} %collective-permute-done.16.refs_5_.refs_4_.refs_6_, ...), custom_call_target="tpu_custom_call" | custom-call | flops 33554432 | bytes 262144 | tf_op jit(solution)/shard_map/attend/pallas_call | solution.py:151
  76.0 5.3 %attend.11.refs_0_ = bf16[128,1024]{1,0:T(8,128)(2,1)S(1)} custom-call(s32[11]{0:T(128)S(1)} %get-tuple-element.99.refs_0_, s32[1]{0:T(128)S(1)} %bitcast.28, s32[128,128]{1,0:T(8,128)S(1)} %broadcast_in_dim.8.refs_2_, bf16[128,1024]{1,0:T(8,128)(2,1)S(1)} %get-tuple-element.101.refs_3_, bf16[512,128]{1,0:T(8,128)(2,1)S(1)} %project.2.refs_5_.refs_4_, ...), custom_call_target="tpu_custom_call" | custom-call | flops 33554432 | bytes 262144 | tf_op jit(solution)/shard_map/attend/pallas_call | solution.py:151
  81.4 1.7 %join.1 = bf16[128,4096]{1,0:T(8,128)(2,1)} custom-call(s32[10]{0:T(128)S(1)} %slice_bitcast_fusion.3.place_ref, bf16[128,1024]{1,0:T(8,128)(2,1)S(1)} %attend.11.refs_0_, bf16[64,1024]{1,0:T(8,128)(2,1)S(1)} %collective-permute-done.18.refs_1_, bf16[64,1024]{1,0:T(8,128)(2,1)S(1)} %collective-permute-done.19.refs_2_, ...), custom_call_target="tpu_custom_call" | custom-call | tf_op jit(solution)/shard_map/join/pallas_call | solution.py:268
  (52 shorter events, 6.6 us)
Async XLA Ops:
  1.7 12.7 %collective-permute-start = (bf16[32,4096]{1,0:T(8,128)(2,1)}, bf16[32,4096]{1,0:T(8,128)(2,1)}, u32[]{:S(2)}, u32[]{:S(2)}) collective-permute-start(bf16[32,4096]{1,0:T(8,128)(2,1)} %dynamic-slice_bitcast_fusion), channel_id=1, source_target_pairs={{0,8},{1,12},{2,10},{3,14},{4,13},{5,9},{6,15},{7,11},{8,0},{9,4},... | collective-permute-start | bytes 786440 | tf_op jit(solution)/shard_map/ppermute | solution.py:299
  2.4 25.5 %collective-permute-start.1 = (bf16[128,4096]{1,0:T(8,128)(2,1)}, bf16[128,4096]{1,0:T(8,128)(2,1)S(1)}, u32[]{:S(2)}, u32[]{:S(2)}) collective-permute-start(bf16[128,4096]{1,0:T(8,128)(2,1)} %refs_3_.3), channel_id=1, source_target_pairs={{0,2},{1,3},{2,0},{3,1},{4,6},{5,7},{6,4},{7,5},{8,10},{9,11},{10,... | collective-permute-start | bytes 3145736 | tf_op jit(solution)/shard_map/ppermute | solution.py:299
  3.7 24.5 %collective-permute-start.9 = (bf16[64,4096]{1,0:T(8,128)(2,1)}, bf16[64,4096]{1,0:T(8,128)(2,1)}, u32[]{:S(2)}, u32[]{:S(2)}) collective-permute-start(bf16[64,4096]{1,0:T(8,128)(2,1)} %bitcast.24), channel_id=1, source_target_pairs={{0,4},{1,5},{2,6},{3,7},{4,0},{5,1},{6,2},{7,3},{8,12},{9,13},{10,... | collective-permute-start | bytes 1572872 | tf_op jit(solution)/shard_map/ppermute | solution.py:299
  11.2 15.2 %copy-start = (bf16[128,4096]{1,0:T(8,128)(2,1)S(1)}, bf16[128,4096]{1,0:T(8,128)(2,1)}, u32[]{:S(2)}) copy-start(bf16[128,4096]{1,0:T(8,128)(2,1)} %refs_3_.3) | copy-start | bytes 3145732
  11.2 17.1 %copy-start.1 = (bf16[4096,64]{0,1:T(8,128)(2,1)S(1)}, bf16[4096,64]{0,1:T(8,128)(2,1)}, u32[]{:S(2)}) copy-start(bf16[4096,64]{0,1:T(8,128)(2,1)} %param.7) | copy-start | bytes 1572868
  14.3 12.0 %collective-permute-start.2 = (bf16[32,4096]{1,0:T(8,128)(2,1)}, bf16[32,4096]{1,0:T(8,128)(2,1)}, u32[]{:S(2)}, u32[]{:S(2)}) collective-permute-start(bf16[32,4096]{1,0:T(8,128)(2,1)} %collective-permute-done.refs_7_), channel_id=1, source_target_pairs={{0,4},{1,5},{2,6},{3,7},{4,0},{5,1},{6,2},{7,3},{8,12},{9,13},{10,... | collective-permute-start | bytes 786440 | tf_op jit(solution)/shard_map/ppermute | solution.py:299
  16.9 11.0 %collective-permute-start.3 = (bf16[32,4096]{1,0:T(8,128)(2,1)}, bf16[32,4096]{1,0:T(8,128)(2,1)}, u32[]{:S(2)}, u32[]{:S(2)}) collective-permute-start(bf16[32,4096]{1,0:T(8,128)(2,1)} %collective-permute-done.refs_7_), channel_id=1, source_target_pairs={{0,16},{1,17},{2,18},{3,19},{4,20},{5,21},{6,22},{7,23},{8,24},{9,... | collective-permute-start | bytes 786440 | tf_op jit(solution)/shard_map/ppermute | solution.py:299
  18.1 9.8 %collective-permute-start.4 = (bf16[128,1024]{1,0:T(8,128)(2,1)}, bf16[128,1024]{1,0:T(8,128)(2,1)}, u32[]{:S(2)}, u32[]{:S(2)}) collective-permute-start(bf16[128,1024]{1,0:T(8,128)(2,1)} %get-tuple-element.59), channel_id=1, source_target_pairs={{0,1},{1,0},{2,3},{3,2},{4,5},{5,4},{6,7},{7,6},{8,9},{9,8},{10,11... | collective-permute-start | bytes 786440 | tf_op jit(solution)/shard_map/ppermute | solution.py:299
  18.1 12.8 %copy-start.3 = (bf16[128,1024]{1,0:T(8,128)(2,1)S(1)}, bf16[128,1024]{1,0:T(8,128)(2,1)}, u32[]{:S(2)}) copy-start(bf16[128,1024]{1,0:T(8,128)(2,1)} %get-tuple-element.62) | copy-start | bytes 786436
  18.1 14.3 %copy-start.2 = (bf16[128,1024]{1,0:T(8,128)(2,1)S(1)}, bf16[128,1024]{1,0:T(8,128)(2,1)}, u32[]{:S(2)}) copy-start(bf16[128,1024]{1,0:T(8,128)(2,1)} %get-tuple-element.63) | copy-start | bytes 786436
  26.4 7.1 %collective-permute-start.7 = (bf16[128,4096]{1,0:T(8,128)(2,1)S(1)}, bf16[128,4096]{1,0:T(8,128)(2,1)S(1)}, u32[]{:S(2)}, u32[]{:S(2)}) collective-permute-start(bf16[128,4096]{1,0:T(8,128)(2,1)S(1)} %copy-done), channel_id=1, source_target_pairs={{0,1},{1,0},{2,3},{3,2},{4,5},{5,4},{6,7},{7,6},{8,9},{9,8},{10,11... | collective-permute-start | bytes 3145736 | tf_op jit(solution)/shard_map/ppermute | solution.py:299
  27.9 5.6 %collective-permute-start.8 = (bf16[128,4096]{1,0:T(8,128)(2,1)S(1)}, bf16[128,4096]{1,0:T(8,128)(2,1)S(1)}, u32[]{:S(2)}, u32[]{:S(2)}) collective-permute-start(bf16[128,4096]{1,0:T(8,128)(2,1)S(1)} %collective-permute-done.1.refs_5_), channel_id=1, source_target_pairs={{0,1},{1,0},{2,3},{3,2},{4,5},{5,4},{6,7},{7,6},{8,9},{9,8},{10,11... | collective-permute-start | bytes 3145736 | tf_op jit(solution)/shard_map/ppermute | solution.py:299
  28.3 4.2 %collective-permute-start.10 = (bf16[64,4096]{1,0:T(8,128)(2,1)S(1)}, bf16[64,4096]{1,0:T(8,128)(2,1)S(1)}, u32[]{:S(2)}, u32[]{:S(2)}) collective-permute-start(bf16[64,4096]{1,0:T(8,128)(2,1)S(1)} %broadcast_select_fusion), channel_id=1, source_target_pairs={{0,1},{1,0},{2,3},{3,2},{4,5},{5,4},{6,7},{7,6},{8,9},{9,8},{10,11... | collective-permute-start | bytes 1572872 | tf_op jit(solution)/shard_map/ppermute | solution.py:299
  29.7 8.1 %collective-permute-start.11 = (bf16[32,4096]{1,0:T(8,128)(2,1)}, bf16[32,4096]{1,0:T(8,128)(2,1)S(1)}, u32[]{:S(2)}, u32[]{:S(2)}) collective-permute-start(bf16[32,4096]{1,0:T(8,128)(2,1)} %collective-permute-done.2.refs_9_), channel_id=1, source_target_pairs={{0,16},{1,17},{2,18},{3,19},{4,20},{5,21},{6,22},{7,23},{8,24},{9,... | collective-permute-start | bytes 786440 | tf_op jit(solution)/shard_map/ppermute | solution.py:299
  30.9 17.7 %collective-permute-start.5 = (bf16[128,1024]{1,0:T(8,128)(2,1)S(1)}, bf16[128,1024]{1,0:T(8,128)(2,1)S(1)}, u32[]{:S(2)}, u32[]{:S(2)}) collective-permute-start(bf16[128,1024]{1,0:T(8,128)(2,1)S(1)} %copy-done.3), channel_id=1, source_target_pairs={{0,2},{1,3},{2,0},{3,1},{4,6},{5,7},{6,4},{7,5},{8,10},{9,11},{10,... | collective-permute-start | bytes 786440 | tf_op jit(solution)/shard_map/ppermute | solution.py:299
  32.5 17.5 %collective-permute-start.6 = (bf16[128,1024]{1,0:T(8,128)(2,1)S(1)}, bf16[128,1024]{1,0:T(8,128)(2,1)S(1)}, u32[]{:S(2)}, u32[]{:S(2)}) collective-permute-start(bf16[128,1024]{1,0:T(8,128)(2,1)S(1)} %copy-done.2), channel_id=1, source_target_pairs={{0,3},{1,2},{2,1},{3,0},{4,7},{5,6},{6,5},{7,4},{8,11},{9,10},{10,... | collective-permute-start | bytes 786440 | tf_op jit(solution)/shard_map/ppermute | solution.py:299
  36.5 17.3 %collective-permute-start.12 = (bf16[512,128]{1,0:T(8,128)(2,1)S(1)}, bf16[512,128]{1,0:T(8,128)(2,1)S(1)}, u32[]{:S(2)}, u32[]{:S(2)}) collective-permute-start(bf16[512,128]{1,0:T(8,128)(2,1)S(1)} %project.2.refs_5_.refs_4_), channel_id=1, source_target_pairs={{0,8},{1,9},{2,10},{3,11},{4,12},{5,13},{6,14},{7,15},{16,24},{17,... | collective-permute-start | bytes 393224 | tf_op jit(solution)/shard_map/ppermute | solution.py:299
  40.9 14.9 %collective-permute-start.14 = (bf16[512,128]{1,0:T(8,128)(2,1)S(1)}, bf16[512,128]{1,0:T(8,128)(2,1)S(1)}, u32[]{:S(2)}, u32[]{:S(2)}) collective-permute-start(bf16[512,128]{1,0:T(8,128)(2,1)S(1)} %project.3.refs_6_.refs_5_), channel_id=1, source_target_pairs={{0,8},{1,9},{2,10},{3,11},{4,12},{5,13},{6,14},{7,15},{16,24},{17,... | collective-permute-start | bytes 393224 | tf_op jit(solution)/shard_map/ppermute | solution.py:299
  42.7 16.4 %collective-permute-start.17 = (bf16[512,128]{1,0:T(8,128)(2,1)S(1)}, bf16[512,128]{1,0:T(8,128)(2,1)S(1)}, u32[]{:S(2)}, u32[]{:S(2)}) collective-permute-start(bf16[512,128]{1,0:T(8,128)(2,1)S(1)} %project.3.refs_6_.refs_5_), channel_id=1, source_target_pairs={{0,4},{1,5},{2,6},{3,7},{8,12},{9,13},{10,14},{11,15},{16,20},{17,... | collective-permute-start | bytes 393224 | tf_op jit(solution)/shard_map/ppermute | solution.py:299
  48.7 10.5 %collective-permute-start.16 = (bf16[512,128]{1,0:T(8,128)(2,1)S(1)}, bf16[512,128]{1,0:T(8,128)(2,1)S(1)}, u32[]{:S(2)}, u32[]{:S(2)}) collective-permute-start(bf16[512,128]{1,0:T(8,128)(2,1)S(1)} %project.2.refs_5_.refs_4_), channel_id=1, source_target_pairs={{0,4},{1,5},{2,6},{3,7},{8,12},{9,13},{10,14},{11,15},{16,20},{17,... | collective-permute-start | bytes 393224 | tf_op jit(solution)/shard_map/ppermute | solution.py:299
  53.8 9.5 %collective-permute-start.13 = (bf16[512,128]{1,0:T(8,128)(2,1)S(1)}, bf16[512,128]{1,0:T(8,128)(2,1)S(1)}, u32[]{:S(2)}, u32[]{:S(2)}) collective-permute-start(bf16[512,128]{1,0:T(8,128)(2,1)S(1)} %collective-permute-done.12.refs_7_.refs_6_.refs_8_), channel_id=1, source_target_pairs={{8,12},{9,13},{10,14},{11,15},{12,8},{13,9},{14,10},{15,11},{24,28... | collective-permute-start | bytes 393224 | tf_op jit(solution)/shard_map/ppermute | solution.py:299
  55.8 7.5 %collective-permute-start.15 = (bf16[512,128]{1,0:T(8,128)(2,1)S(1)}, bf16[512,128]{1,0:T(8,128)(2,1)S(1)}, u32[]{:S(2)}, u32[]{:S(2)}) collective-permute-start(bf16[512,128]{1,0:T(8,128)(2,1)S(1)} %collective-permute-done.14.refs_8_.refs_7_.refs_9_), channel_id=1, source_target_pairs={{8,12},{9,13},{10,14},{11,15},{12,8},{13,9},{14,10},{15,11},{24,28... | collective-permute-start | bytes 393224 | tf_op jit(solution)/shard_map/ppermute | solution.py:299
  67.5 13.9 %collective-permute-start.20 = (bf16[128,1024]{1,0:T(8,128)(2,1)S(1)}, bf16[128,1024]{1,0:T(8,128)(2,1)S(1)}, u32[]{:S(2)}, u32[]{:S(2)}) collective-permute-start(bf16[128,1024]{1,0:T(8,128)(2,1)S(1)} %get-tuple-element.91), channel_id=1, source_target_pairs={{0,2},{1,3},{2,0},{3,1},{4,6},{5,7},{6,4},{7,5},{8,10},{9,11},{10,... | collective-permute-start | bytes 786440 | tf_op jit(solution)/shard_map/ppermute | solution.py:299
  68.4 12.9 %collective-permute-start.21 = (bf16[128,1024]{1,0:T(8,128)(2,1)S(1)}, bf16[128,1024]{1,0:T(8,128)(2,1)S(1)}, u32[]{:S(2)}, u32[]{:S(2)}) collective-permute-start(bf16[128,1024]{1,0:T(8,128)(2,1)S(1)} %get-tuple-element.92), channel_id=1, source_target_pairs={{0,3},{1,2},{2,1},{3,0},{4,7},{5,6},{6,5},{7,4},{8,11},{9,10},{10,... | collective-permute-start | bytes 786440 | tf_op jit(solution)/shard_map/ppermute | solution.py:299
  75.3 6.0 %collective-permute-start.18 = (bf16[64,1024]{1,0:T(8,128)(2,1)S(1)}, bf16[64,1024]{1,0:T(8,128)(2,1)S(1)}, u32[]{:S(2)}, u32[]{:S(2)}) collective-permute-start(bf16[64,1024]{1,0:T(8,128)(2,1)S(1)} %get-tuple-element.110), channel_id=1, source_target_pairs={{0,1},{1,0},{2,3},{3,2},{4,5},{5,4},{6,7},{7,6},{8,9},{9,8},{10,11... | collective-permute-start | bytes 393224 | tf_op jit(solution)/shard_map/ppermute | solution.py:299
  75.4 5.9 %collective-permute-start.19 = (bf16[64,1024]{1,0:T(8,128)(2,1)S(1)}, bf16[64,1024]{1,0:T(8,128)(2,1)S(1)}, u32[]{:S(2)}, u32[]{:S(2)}) collective-permute-start(bf16[64,1024]{1,0:T(8,128)(2,1)S(1)} %get-tuple-element.109), channel_id=1, source_target_pairs={{0,1},{1,0},{2,3},{3,2},{4,5},{5,4},{6,7},{7,6},{8,9},{9,8},{10,11... | collective-permute-start | bytes 393224 | tf_op jit(solution)/shard_map/ppermute | solution.py:299
where the time goes:
time: 84.8 us; the launch traced here: 83.2 us
  Pallas kernels  31.7 us (37%)
  starting transfers between devices  29.5 us (35%)
  waiting for transfers between devices  10.8 us (13%)
  local copies, waits for them, and re-layouts  7.32 us (9%)
  other arithmetic  3.35 us (4%)
    ppermute x22, starting transfers between devices, hop(): return lambda v: lax.ppermute(v, AXES, pairs)  29.5 us
    pallas_call x6, Pallas kernels, attend(): pl.pallas_call(lambda *refs: attend_kernel(rows, chunk, n_q, n_kv, bool(s...  24 us
    ppermute x22, waiting for transfers between devices, hop(): return lambda v: lax.ppermute(v, AXES, pairs)  10.8 us
    pallas_call x2, Pallas kernels, project(): pl.pallas_call(lambda *refs: project_kernel(rows, n, len(pieces), *refs),...  6.04 us
    dynamic_slice x1, local copies, waits for them, and re-layouts, by_planes(): lax.dynamic_slice_in_dim(queries, h * columns, columns, 1)  2.12 us
    reduce_sum x2, other arithmetic, attend_starts(): jnp.sum((doc_ids[None, :] < docs[:, None]).astype(jnp.int32), axis=1)  2.09 us
  transfers between devices with their start and end apart: 22, of which 3 were waited for; matrix products, arithmetic and copies ran while one was open for 11% of the time, Pallas kernels for 31%

commit v1 on v0

--- a/solution.py
+++ b/solution.py
@@ -32,59 +32,48 @@
     return jnp.cos(angle), jnp.sin(angle)
 
 
-def attend_kernel(rows, chunk, n_q, n_kv, resumed, last, place_ref, start_ref, starts_ref, *refs):
+def attend_kernel(rows, chunk, n_q, n_kv, resumed, last, place_ref, starts_ref, *refs):
     queries, refs = refs[:n_q], refs[n_q:]
     arrays, refs = refs[: 2 * n_kv], refs[2 * n_kv :]
     state, refs = (refs[:3], refs[3:]) if resumed else ((), refs)
     if last:
         outs, refs = refs[:n_q], refs[n_q:]
-        kv, qv, stacked, bias, sem, qsem, ssem, stat_m, stat_l, acc = refs
+        kv, stacked, bias, stat_m, stat_l, acc = refs
     else:
-        stat_m, stat_l, acc, kv, qv, stacked, bias, sem, qsem, ssem = refs
-    part_rows = queries[0].shape[0]
+        stat_m, stat_l, acc, kv, stacked, bias = refs
+    part_rows = rows // n_q
     chunks = arrays[0].shape[0] // chunk
 
-    def q_copy(i):
-        column = pl.multiple_of(place_ref[2 + 2 * i], HD)
-        return pltpu.make_async_copy(
-            queries[i].at[:, pl.ds(column, QPK * HD)],
-            qv.at[pl.ds(pl.multiple_of(place_ref[1 + 2 * i], part_rows), part_rows)],
-            qsem.at[i],
-        )
-
-    def kv_copy(i):
-        kind = place_ref[1 + 2 * n_q + n_kv + i // 2]
-        kind = kind if i % 2 == 0 else 1 - kind
-        return pltpu.make_async_copy(arrays[i], kv.at[i // 2, kind], sem.at[i])
-
-    for i in range(n_q):
-        q_copy(i).start()
-    running = [
-        pltpu.make_async_copy(old, new, ssem.at[i])
-        for i, (old, new) in enumerate(zip(state, (stat_m, stat_l, acc)))
-    ]
-    for copy in running:
-        copy.start()
-    for i in range(2 * n_kv):
-        kv_copy(i).start()
-    if not resumed:
+    if resumed:
+        for old, new in zip(state, (stat_m, stat_l, acc)):
+            new[...] = old[...]
+    else:
         stat_m[...] = jnp.full_like(stat_m, MASKED)
         stat_l[...] = jnp.zeros_like(stat_l)
         acc[...] = jnp.zeros_like(acc)
-    for i in range(n_q):
-        q_copy(i).wait()
     for h in range(QPK):
-        stacked[h * rows : (h + 1) * rows, :] = qv[:, h * HD : (h + 1) * HD]
-    for copy in running:
-        copy.wait()
-    for i in range(2 * n_kv):
-        kv_copy(i).wait()
+        for i in range(n_q):
+            at = h * rows + i * part_rows
+            stacked[at : at + part_rows, :] = queries[i][:, h * HD : (h + 1) * HD]
+    for i in range(n_kv):
+        kind = place_ref[n_q + n_kv + i]
+        kv[i, kind] = arrays[2 * i][...]
+        kv[i, 1 - kind] = arrays[2 * i + 1][...]
 
     lanes = chunk // HD
     starts = jnp.concatenate([starts_ref[...]] * lanes, axis=1)
-    q_pos = place_ref[0] + lax.broadcasted_iota(jnp.int32, (rows, chunk), 0)
-    first_chunk = start_ref[0] // chunk
-    end_chunk = (place_ref[0] + rows + chunk - 1) // chunk
+    q_pos = jnp.concatenate(
+        [
+            place_ref[i] + lax.broadcasted_iota(jnp.int32, (part_rows, chunk), 0)
+            for i in range(n_q)
+        ],
+        axis=0,
+    )
+    first_chunk = place_ref[n_q + 2 * n_kv] // chunk
+    last_row = place_ref[0]
+    for i in range(1, n_q):
+        last_row = jnp.maximum(last_row, place_ref[i])
+    end_chunk = (last_row + part_rows + chunk - 1) // chunk
 
     def attend_chunk(i, j, t):
         k_pos = t * chunk + lax.broadcasted_iota(jnp.int32, (rows, chunk), 1)
@@ -116,7 +105,7 @@
     @pl.loop(0, n_kv * chunks)
     def _(step):
         i, j = step // chunks, step % chunks
-        t = place_ref[1 + 2 * n_q + i] * chunks + j
+        t = place_ref[n_q + i] * chunks + j
 
         @pl.when((t >= first_chunk) & (t < end_chunk))
         def _():
@@ -127,16 +116,17 @@
     for h in range(QPK):
         at = slice(h * rows, (h + 1) * rows)
         done = acc[at, :] / jnp.sum(stat_l[at, :], axis=1, keepdims=True)
-        qv[:, h * HD : (h + 1) * HD] = done.astype(jnp.bfloat16)
-    for i in range(n_q):
-        at = pl.multiple_of(place_ref[1 + 2 * i], part_rows)
-        outs[i][...] = qv[pl.ds(at, part_rows), :]
-
-
-def attend_starts(doc_ids, first_row, rows):
-    docs = lax.dynamic_slice_in_dim(doc_ids, first_row, rows)
+        for i in range(n_q):
+            outs[i][:, h * HD : (h + 1) * HD] = done[
+                i * part_rows : (i + 1) * part_rows
+            ].astype(jnp.bfloat16)
+
+
+def attend_starts(doc_ids, first_rows, rows):
+    docs = [lax.dynamic_slice_in_dim(doc_ids, first, rows) for first in first_rows]
+    docs = jnp.concatenate(docs)
     starts = jnp.sum((doc_ids[None, :] < docs[:, None]).astype(jnp.int32), axis=1)
-    return starts
+    return jnp.broadcast_to(starts[:, None], (starts.shape[0], HD)), jnp.min(starts)[None]
 
 
 def attend(place, starts, queries, arrays, tokens, chunk, state=(), last=True):
@@ -151,16 +141,12 @@
     return pl.pallas_call(
         lambda *refs: attend_kernel(rows, chunk, n_q, n_kv, bool(state), last, *refs),
         out_shape=out_shape,
-        in_specs=[IN_SMEM, IN_SMEM, IN_VMEM] + [ANY] * (n_q + 2 * n_kv + len(state)),
+        in_specs=[IN_SMEM] + [IN_VMEM] * (1 + n_q + 2 * n_kv + len(state)),
         out_specs=[IN_VMEM] * len(out_shape),
         scratch_shapes=[
             pltpu.VMEM((n_kv, 2, *arrays[0].shape), jnp.bfloat16),
-            pltpu.VMEM((rows, QPK * HD), jnp.bfloat16),
             pltpu.VMEM((QPK * rows, HD), jnp.bfloat16),
             pltpu.VMEM((rows, chunk), jnp.float32),
-            pltpu.SemaphoreType.DMA((2 * n_kv,)),
-            pltpu.SemaphoreType.DMA((n_q,)),
-            pltpu.SemaphoreType.DMA((3,)),
         ]
         + [pltpu.VMEM(running, jnp.float32)] * (3 if last else 0),
         compiler_params=pltpu.CompilerParams(vmem_limit_bytes=VMEM_LIMIT),
@@ -170,14 +156,7 @@
             transcendentals=0,
         ),
         name="attend",
-    )(
-        place,
-        starts[:1],
-        jnp.broadcast_to(starts[:, None], (rows, HD)),
-        *queries,
-        *arrays,
-        *state,
-    )
+    )(place, starts, *queries, *arrays, *state)
 
 
 def project_kernel(rows, n_hidden, n_pieces, place_ref, cos_ref, sin_ref, *refs):
@@ -309,7 +288,7 @@
     swap_high = hop(lambda x, z, y, c: (x, z ^ 1, y, c) if z >= 2 else None)
 
     chunk = math.gcd(tokens, 512)
-    tables = [[] for _ in range(9)]
+    tables = [[] for _ in range(7)]
     for i in range(32):
         ix, iz, iy, ic = i // 16, (i // 4) % 4, (i // 2) % 2, i % 2
         blocks = [2 * iy + ic, 2 * iy + 1 - ic, 2 * (1 - iy) + ic, 2 * (1 - iy) + 1 - ic]
@@ -325,17 +304,12 @@
             + [1, width - side + ix * part, 1, width - side + (1 - ix) * part]
         )
         planes = [iz, iz - 1 if iz % 2 else -1, iz - 2, (iz ^ 1) - 2 if iz >= 2 else -1]
-        for t, block in enumerate((2 * (1 - iy), 2 * iy + 1 - ic, 2 * iy + ic)):
-            first = (4 * iz + block) * rows
-            q_rows = [ic * rows, 0, (1 - ic) * rows, 0] if t == 0 else [0, 0]
-            calls = (
-                [(1, planes[:1]), (4, planes[1:3]), (2, planes[3:])],
-                [(3, planes[:1]), (7, planes[1:])],
-                [(8, planes)],
-            )[t]
-            for at, some in calls:
-                kinds = [max(plane, 0) // 2 for plane in some]
-                tables[at].append([first] + q_rows + some + kinds)
+        calls = [(1, 1 - iy, planes[:1]), (2, 1 - iy, planes[3:])]
+        calls += [(3, iy, planes), (4, 1 - iy, planes[1:3])]
+        for at, iy_rows, some in calls:
+            first = [(4 * iz + 2 * iy_rows + core) * rows for core in (ic, 1 - ic)]
+            kinds = [max(plane, 0) // 2 for plane in some]
+            tables[at].append(first + some + kinds)
         heads = [iy + 2 * ic, iy + 2 * (1 - ic), iy + 2 * (1 - ic)]
         heads += [1 - iy + 2 * ic, 1 - iy + 2 * (1 - ic)]
         tops = [0, 0, rows // 2, 0, 0]
@@ -358,10 +332,13 @@
     cosine, sine = rope_tables(positions)
     cos = jnp.concatenate([cosine, cosine], axis=1)
     sin = jnp.concatenate([-sine, sine], axis=1)
-    starts = [
-        attend_starts(doc_ids, (4 * z + block) * rows, size)
-        for block, size in ((2 * (1 - y), 2 * rows), (2 * y + 1 - c, rows), (2 * y + c, rows))
+    firsts = [
+        [(4 * z + 2 * (1 - y) + c) * rows, (4 * z + 2 * (1 - y) + 1 - c) * rows],
+        [(4 * z + 2 * y + c) * rows, (4 * z + 2 * y + 1 - c) * rows],
     ]
+    starts, lowest = zip(*[attend_starts(doc_ids, first, rows) for first in firsts])
+    for at, low in ((1, 0), (2, 0), (3, 1), (4, 0)):
+        places[at] = jnp.concatenate([places[at], lowest[low]])
     q_own, *q_away = [
         lax.dynamic_slice_in_dim(queries, h * columns, columns, 1)
         for h in (y + 2 * c, y + 2 * (1 - c), 1 - y + 2 * c, 1 - y + 2 * (1 - c))
@@ -388,19 +365,16 @@
     own, near_below = [kv_a, kv_b], [a_near, b_near]
     q_partner = [q_y, q_both]
     begun = attend(places[1], starts[0], q_partner, own, tokens, chunk, last=False)
-    begun_beside = attend(places[3], starts[1], [q_core], own, tokens, chunk, last=False)
-    begun, begun_beside, a_far = lax.optimization_barrier((begun, begun_beside, a_far))
+    begun, a_far = lax.optimization_barrier((begun, a_far))
     other = [swap_high(a_far), swap_high(b_far)]
     below = near_below + [a_far, b_far]
     begun = attend(places[4], starts[0], q_partner, below, tokens, chunk, begun, last=False)
     across = attend(places[2], starts[0], q_partner, other, tokens, chunk, begun)
     back = [to_y(across[0]), to_both(across[1])]
-    below += other
-    across, places[7] = lax.optimization_barrier((across, places[7]))
-    beside = attend(places[7], starts[1], [q_core], below, tokens, chunk, begun_beside)
-    beside, places[8] = lax.optimization_barrier((beside, places[8]))
-    here = attend(places[8], starts[2], [q_own], own + below, tokens, chunk)
-    parts = [here[0], to_core(beside[0][: rows // 2]), to_core(beside[0][rows // 2 :])] + back
+    stored = own + below + other
+    across, places[3] = lax.optimization_barrier((across, places[3]))
+    here, beside = attend(places[3], starts[1], [q_own, q_core], stored, tokens, chunk)
+    parts = [here, to_core(beside[: rows // 2]), to_core(beside[rows // 2 :])] + back
     return join(places[5], parts, queries.shape)
 
 
@@ -420,12 +394,13 @@
     both = both.astype(jnp.bfloat16).transpose(1, 0, 2)
     whole = lax.all_gather(both, "node", axis=1, tiled=True)
     chunk = math.gcd(tokens, 512)
-    starts = attend_starts(doc_ids, me * rows, rows)
+    starts, lowest = attend_starts(doc_ids, [me * rows], rows)
+    place = jnp.concatenate([scalars(me * rows, 0, 0), lowest])
     outs = []
     for g in range(KVH):
-        place = scalars(me * rows, 0, g * QPK * HD, 0, 0)
         pair = [whole[g], whole[KVH + g]]
-        outs += attend(place, starts, [queries], pair, tokens, chunk)
+        mine = queries[:, g * QPK * HD : (g + 1) * QPK * HD]
+        outs += attend(place, starts, [mine], pair, tokens, chunk)
     return jnp.concatenate(outs, axis=1)
 
 

time: 84.8 us -> 78.4 us (0.925)
  the two profiles are of different devices: /device:TPU:17 before, /device:TPU:29 now
where the time goes in v1:
time: 78.4 us; the launch traced here: 77.1 us
  waiting for transfers between devices  23.5 us (30%)
  starting transfers between devices  21.9 us (28%)
  Pallas kernels  15.4 us (20%)
  other arithmetic  8.16 us (10%)
  local copies, waits for them, and re-layouts  7.7 us (10%)
    ppermute x22, waiting for transfers between devices, hop(): return lambda v: lax.ppermute(v, AXES, pairs)  23.5 us
    ppermute x22, starting transfers between devices, hop(): return lambda v: lax.ppermute(v, AXES, pairs)  21.9 us
    pallas_call x4, Pallas kernels, attend(): pl.pallas_call(lambda *refs: attend_kernel(rows, chunk, n_q, n_kv, bool(s...  8.31 us
    pallas_call x2, Pallas kernels, project(): pl.pallas_call(lambda *refs: project_kernel(rows, n, len(pieces), *refs),...  5.4 us
    concatenate x4, other arithmetic, by_planes(): places[at] = jnp.concatenate([places[at], lowest[low]])  3.3 us
    broadcast_in_dim x2, local copies, waits for them, and re-layouts, attend_starts(): jnp.broadcast_to(starts[:, None], (starts.shape[0], HD))  2.12 us
    pallas_call x1, Pallas kernels, join(): pl.pallas_call(join_kernel, out_shape=jax.ShapeDtypeStruct(shape, parts[0...  1.68 us
    dynamic_slice x1, local copies, waits for them, and re-layouts, by_planes(): far_0 = far(lax.dynamic_slice_in_dim(weight, x * part, part, 0))  1.66 us
  transfers between devices with their start and end apart: 22, of which 10 were waited for; matrix products, arithmetic and copies ran while one was open for 18% of the time, Pallas kernels for 16%

profile of v1, /device:TPU:29, one launch (start us, length us, event | category | flops | bytes accessed | tf_op | source)
XLA Modules:
  0.0 77.1 jit_solution(6082616098576114476)
XLA Ops:
  0.0 1.7 %dynamic-slice_bitcast_fusion = bf16[32,4096]{1,0:T(8,128)(2,1)} fusion(bf16[4096,64]{0,1:T(8,128)(2,1)} %param.7, s32[]{:T(128)S(6)} %select_n.60), kind=kLoop, calls=%fused_computation.7 | loop fusion | bytes 524292 | tf_op jit(solution)/shard_map/dynamic_slice | solution.py:326
  3.6 0.9 %fusion.2 = (s32[128]{0:T(128)S(1)}, s32[128]{0:T(128)S(1)}, s32[128]{0:T(128)S(1)}, s32[128]{0:T(128)S(1)}) fusion(s32[2048]{0:T(1024)} %param.8, s32[]{:T(128)S(6)} %select_n.65, s32[]{:T(128)S(6)} %select_n.66, s32[]{:T(128)S(6)} %select_n.68, s32[]{:T(128)S(6)} %select_n.67), kind=kLoop, calls=%fused_computation.30 | loop fusion | bytes 4112 | tf_op jit(solution)/shard_map/dynamic_slice | solution.py:126
  4.6 1.2 %convert_reduce_fusion = (s32[256]{0:T(256)S(1)}, s32[256]{0:T(256)S(1)}) fusion(s32[2048]{0:T(1024)} %param.8, s32[256]{0:T(256)S(1)} %get-tuple-element.105, s32[256]{0:T(256)S(1)} %get-tuple-element.104), kind=kLoop, calls=%fused_computation | loop fusion | flops 3145216 | bytes 12288 | tf_op jit(solution)/shard_map/reduce_sum | solution.py:128
  7.9 1.0 %fusion = (f32[512,64]{1,0:T(8,128)S(1)}, f32[512,64]{1,0:T(8,128)S(1)}, f32[512,64]{1,0:T(8,128)S(1)}) fusion(f32[64]{0:T(128)S(1)} %multiply_power_fusion, f32[512]{0:T(512)S(1)} %add_convert_fusion), kind=kLoop, calls=%fused_computation.8 | loop fusion | flops 65536 | bytes 395520 | tf_op jit(solution)/shard_map/neg | solution.py:334
  10.0 1.2 %pad_add_fusion.5.refs_0_ = s32[7]{0:T(128)} fusion(s32[1]{0:T(128)} %bitcast.3, s32[6]{0:T(128)S(1)} %slice_bitcast_fusion.2), kind=kLoop, calls=%fused_computation.20 | loop fusion | flops 7 | bytes 56 | tf_op jit(solution)/shard_map/concatenate | solution.py:341
  13.8 1.8 %collective-permute-done.refs_7_ = bf16[32,4096]{1,0:T(8,128)(2,1)} collective-permute-done((bf16[32,4096]{1,0:T(8,128)(2,1)}, bf16[32,4096]{1,0:T(8,128)(2,1)}, u32[]{:S(2)}, u32[]{:S(2)}) %collective-permute-start) | collective-permute-done | bytes 262176 | tf_op jit(solution)/shard_map/ppermute | solution.py:278
  16.3 1.4 %broadcast_in_dim.9.refs_1_ = s32[256,128]{1,0:T(8,128)} broadcast(s32[256]{0:T(256)} %copy-done.9), dimensions={0} | broadcast | bytes 132096 | tf_op jit(solution)/shard_map/broadcast_in_dim | solution.py:129
  17.7 1.2 %collective-permute-start.3 = (bf16[32,4096]{1,0:T(8,128)(2,1)}, bf16[32,4096]{1,0:T(8,128)(2,1)}, u32[]{:S(2)}, u32[]{:S(2)}) collective-permute-start(bf16[32,4096]{1,0:T(8,128)(2,1)} %collective-permute-done.refs_7_), channel_id=1, source_target_pairs={{0,16},{1,17},{2,18},{3,19},{4,20},{5,21},{6,22},{7,23},{8,24},{9,... | collective-permute-start | bytes 786440 | tf_op jit(solution)/shard_map/ppermute | solution.py:278
  19.5 6.9 %collective-permute-done.2.refs_9_ = bf16[32,4096]{1,0:T(8,128)(2,1)} collective-permute-done((bf16[32,4096]{1,0:T(8,128)(2,1)}, bf16[32,4096]{1,0:T(8,128)(2,1)}, u32[]{:S(2)}, u32[]{:S(2)}) %collective-permute-start.2) | collective-permute-done | bytes 262176 | tf_op jit(solution)/shard_map/ppermute | solution.py:278
  26.4 1.4 %collective-permute-start.7 = (bf16[128,4096]{1,0:T(8,128)(2,1)S(1)}, bf16[128,4096]{1,0:T(8,128)(2,1)S(1)}, u32[]{:S(2)}, u32[]{:S(2)}) collective-permute-start(bf16[128,4096]{1,0:T(8,128)(2,1)S(1)} %copy-done), channel_id=1, source_target_pairs={{0,1},{1,0},{2,3},{3,2},{4,5},{5,4},{6,7},{7,6},{8,9},{9,8},{10,11... | collective-permute-start | bytes 3145736 | tf_op jit(solution)/shard_map/ppermute | solution.py:278
  27.9 1.1 %broadcast_select_fusion = bf16[64,4096]{1,0:T(8,128)(2,1)S(1)} fusion(bf16[64,4096]{1,0:T(8,128)(2,1)} %collective-permute-done.9.refs_8_, pred[]{:T(512)S(6)} %eq.7, bf16[4096,64]{0,1:T(8,128)(2,1)S(1)} %copy-done.1), kind=kLoop, calls=%fused_computation.2 | loop fusion | flops 262144 | bytes 1572865 | tf_op jit(solution)/shard_map/jit(_where)/select_n | solution.py:352
  29.1 1.3 %collective-permute-start.11 = (bf16[32,4096]{1,0:T(8,128)(2,1)}, bf16[32,4096]{1,0:T(8,128)(2,1)S(1)}, u32[]{:S(2)}, u32[]{:S(2)}) collective-permute-start(bf16[32,4096]{1,0:T(8,128)(2,1)} %collective-permute-done.2.refs_9_), channel_id=1, source_target_pairs={{0,16},{1,17},{2,18},{3,19},{4,20},{5,21},{6,22},{7,23},{8,24},{9,... | collective-permute-start | bytes 786440 | tf_op jit(solution)/shard_map/ppermute | solution.py:278
  30.4 1.2 %collective-permute-start.5 = (bf16[128,1024]{1,0:T(8,128)(2,1)S(1)}, bf16[128,1024]{1,0:T(8,128)(2,1)S(1)}, u32[]{:S(2)}, u32[]{:S(2)}) collective-permute-start(bf16[128,1024]{1,0:T(8,128)(2,1)S(1)} %copy-done.8), channel_id=1, source_target_pairs={{0,2},{1,3},{2,0},{3,1},{4,6},{5,7},{6,4},{7,5},{8,10},{9,11},{10,... | collective-permute-start | bytes 786440 | tf_op jit(solution)/shard_map/ppermute | solution.py:278
  32.3 1.5 %collective-permute-start.6 = (bf16[128,1024]{1,0:T(8,128)(2,1)S(1)}, bf16[128,1024]{1,0:T(8,128)(2,1)S(1)}, u32[]{:S(2)}, u32[]{:S(2)}) collective-permute-start(bf16[128,1024]{1,0:T(8,128)(2,1)S(1)} %copy-done.7), channel_id=1, source_target_pairs={{0,3},{1,2},{2,1},{3,0},{4,7},{5,6},{6,5},{7,4},{8,11},{9,10},{10,... | collective-permute-start | bytes 786440 | tf_op jit(solution)/shard_map/ppermute | solution.py:278
  33.8 2.3 %project.2.refs_4_ = bf16[512,128]{1,0:T(8,128)(2,1)S(1)} custom-call(s32[11]{0:T(128)S(1)} %copy-done.5, f32[512,128]{1,0:T(8,128)S(1)} %get-tuple-element.57.refs_1_, f32[512,128]{1,0:T(8,128)S(1)} %get-tuple-element.58.refs_2_, bf16[128,4096]{1,0:T(8,128)(2,1)S(1)} %copy-done, bf16[128,4096]{1,0:T(8,128)(2,1)S(1)} %collective-permute-done.7.refs_4_, ...), custom_call_target="tpu_custom_call" | custom-call | flops 67108864 | bytes 524288 | tf_op jit(solution)/shard_map/project/pallas_call | solution.py:203
  36.2 1.3 %collective-permute-start.12 = (bf16[512,128]{1,0:T(8,128)(2,1)S(1)}, bf16[512,128]{1,0:T(8,128)(2,1)S(1)}, u32[]{:S(2)}, u32[]{:S(2)}) collective-permute-start(bf16[512,128]{1,0:T(8,128)(2,1)S(1)} %project.2.refs_4_), channel_id=1, source_target_pairs={{0,8},{1,9},{2,10},{3,11},{4,12},{5,13},{6,14},{7,15},{16,24},{17,... | collective-permute-start | bytes 393224 | tf_op jit(solution)/shard_map/ppermute | solution.py:278
  37.5 3.1 %project.3.refs_5_ = bf16[512,128]{1,0:T(8,128)(2,1)S(1)} custom-call(s32[13]{0:T(128)S(1)} %copy-done.4, f32[512,128]{1,0:T(8,128)S(1)} %get-tuple-element.57.refs_1_, f32[512,128]{1,0:T(8,128)S(1)} %get-tuple-element.58.refs_2_, bf16[128,4096]{1,0:T(8,128)(2,1)S(1)} %copy-done, bf16[128,4096]{1,0:T(8,128)(2,1)S(1)} %collective-permute-done.7.refs_4_, ...), custom_call_target="tpu_custom_call" | custom-call | flops 67108864 | bytes 524288 | tf_op jit(solution)/shard_map/project/pallas_call | solution.py:203
  40.6 1.3 %collective-permute-start.14 = (bf16[512,128]{1,0:T(8,128)(2,1)S(1)}, bf16[512,128]{1,0:T(8,128)(2,1)S(1)}, u32[]{:S(2)}, u32[]{:S(2)}) collective-permute-start(bf16[512,128]{1,0:T(8,128)(2,1)S(1)} %project.3.refs_5_), channel_id=1, source_target_pairs={{0,8},{1,9},{2,10},{3,11},{4,12},{5,13},{6,14},{7,15},{16,24},{17,... | collective-permute-start | bytes 393224 | tf_op jit(solution)/shard_map/ppermute | solution.py:278
  41.9 1.3 %collective-permute-start.17 = (bf16[512,128]{1,0:T(8,128)(2,1)S(1)}, bf16[512,128]{1,0:T(8,128)(2,1)S(1)}, u32[]{:S(2)}, u32[]{:S(2)}) collective-permute-start(bf16[512,128]{1,0:T(8,128)(2,1)S(1)} %project.3.refs_5_), channel_id=1, source_target_pairs={{0,4},{1,5},{2,6},{3,7},{8,12},{9,13},{10,14},{11,15},{16,20},{17,... | collective-permute-start | bytes 393224 | tf_op jit(solution)/shard_map/ppermute | solution.py:278
  43.2 1.3 %collective-permute-start.16 = (bf16[512,128]{1,0:T(8,128)(2,1)S(1)}, bf16[512,128]{1,0:T(8,128)(2,1)S(1)}, u32[]{:S(2)}, u32[]{:S(2)}) collective-permute-start(bf16[512,128]{1,0:T(8,128)(2,1)S(1)} %project.2.refs_4_), channel_id=1, source_target_pairs={{0,4},{1,5},{2,6},{3,7},{8,12},{9,13},{10,14},{11,15},{16,20},{17,... | collective-permute-start | bytes 393224 | tf_op jit(solution)/shard_map/ppermute | solution.py:278
  44.5 2.6 %attend.4 = (f32[2048,128]{1,0:T(8,128)S(1)}, f32[2048,128]{1,0:T(8,128)S(1)}, f32[2048,128]{1,0:T(8,128)S(1)}) custom-call(s32[5]{0:T(128)S(1)} %pad_add_fusion.2.refs_0_, s32[256,128]{1,0:T(8,128)S(1)} %broadcast_in_dim.8.refs_1_, bf16[128,1024]{1,0:T(8,128)(2,1)S(1)} %collective-permute-done.5.refs_2_, ...), custom_call_target="tpu_custom_call" | custom-call | flops 67108864 | bytes 524288 | tf_op jit(solution)/shard_map/attend/pallas_call | solution.py:141
  47.2 2.4 %collective-permute-done.12.refs_6_.refs_8_ = bf16[512,128]{1,0:T(8,128)(2,1)S(1)} collective-permute-done((bf16[512,128]{1,0:T(8,128)(2,1)S(1)}, bf16[512,128]{1,0:T(8,128)(2,1)S(1)}, u32[]{:S(2)}, u32[]{:S(2)}) %collective-permute-start.12) | collective-permute-done | bytes 131104 | tf_op jit(solution)/shard_map/ppermute | solution.py:278
  49.6 1.9 %collective-permute-start.13 = (bf16[512,128]{1,0:T(8,128)(2,1)S(1)}, bf16[512,128]{1,0:T(8,128)(2,1)S(1)}, u32[]{:S(2)}, u32[]{:S(2)}) collective-permute-start(bf16[512,128]{1,0:T(8,128)(2,1)S(1)} %collective-permute-done.12.refs_6_.refs_8_), channel_id=1, source_target_pairs={{8,12},{9,13},{10,14},{11,15},{12,8},{13,9},{14,10},{15,11},{24,28... | collective-permute-start | bytes 393224 | tf_op jit(solution)/shard_map/ppermute | solution.py:278
  51.5 0.9 %collective-permute-done.14.refs_7_.refs_9_ = bf16[512,128]{1,0:T(8,128)(2,1)S(1)} collective-permute-done((bf16[512,128]{1,0:T(8,128)(2,1)S(1)}, bf16[512,128]{1,0:T(8,128)(2,1)S(1)}, u32[]{:S(2)}, u32[]{:S(2)}) %collective-permute-start.14) | collective-permute-done | bytes 131104 | tf_op jit(solution)/shard_map/ppermute | solution.py:278
  52.5 2.4 %collective-permute-start.15 = (bf16[512,128]{1,0:T(8,128)(2,1)S(1)}, bf16[512,128]{1,0:T(8,128)(2,1)S(1)}, u32[]{:S(2)}, u32[]{:S(2)}) collective-permute-start(bf16[512,128]{1,0:T(8,128)(2,1)S(1)} %collective-permute-done.14.refs_7_.refs_9_), channel_id=1, source_target_pairs={{8,12},{9,13},{10,14},{11,15},{12,8},{13,9},{14,10},{15,11},{24,28... | collective-permute-start | bytes 393224 | tf_op jit(solution)/shard_map/ppermute | solution.py:278
  55.8 1.4 %collective-permute-done.13.refs_4_.refs_10_ = bf16[512,128]{1,0:T(8,128)(2,1)S(1)} collective-permute-done((bf16[512,128]{1,0:T(8,128)(2,1)S(1)}, bf16[512,128]{1,0:T(8,128)(2,1)S(1)}, u32[]{:S(2)}, u32[]{:S(2)}) %collective-permute-start.13) | collective-permute-done | bytes 131104 | tf_op jit(solution)/shard_map/ppermute | solution.py:278
  57.3 2.8 %collective-permute-done.15.refs_5_.refs_11_ = bf16[512,128]{1,0:T(8,128)(2,1)S(1)} collective-permute-done((bf16[512,128]{1,0:T(8,128)(2,1)S(1)}, bf16[512,128]{1,0:T(8,128)(2,1)S(1)}, u32[]{:S(2)}, u32[]{:S(2)}) %collective-permute-start.15) | collective-permute-done | bytes 131104 | tf_op jit(solution)/shard_map/ppermute | solution.py:278
  60.1 1.4 %attend.6 = (bf16[128,1024]{1,0:T(8,128)(2,1)S(1)}, bf16[128,1024]{1,0:T(8,128)(2,1)S(1)}) custom-call(s32[5]{0:T(128)S(1)} %pad_add_fusion.3.refs_0_, s32[256,128]{1,0:T(8,128)S(1)} %broadcast_in_dim.8.refs_1_, bf16[128,1024]{1,0:T(8,128)(2,1)S(1)} %collective-permute-done.5.refs_2_, bf16[128,1024]{1,0:T(8,128)(2,1)S(1)} %collective-permute-done.6.refs_3_, ...), custom_call_target="tpu_custom_call" | custom-call | flops 67108864 | bytes 524288 | tf_op jit(solution)/shard_map/attend/pallas_call | solution.py:141
  61.9 3.0 %collective-permute-start.21 = (bf16[128,1024]{1,0:T(8,128)(2,1)S(1)}, bf16[128,1024]{1,0:T(8,128)(2,1)S(1)}, u32[]{:S(2)}, u32[]{:S(2)}) collective-permute-start(bf16[128,1024]{1,0:T(8,128)(2,1)S(1)} %get-tuple-element.77), channel_id=1, source_target_pairs={{0,3},{1,2},{2,1},{3,0},{4,7},{5,6},{6,5},{7,4},{8,11},{9,10},{10,... | collective-permute-start | bytes 786440 | tf_op jit(solution)/shard_map/ppermute | solution.py:278
  64.9 3.4 %attend.7 = (bf16[128,1024]{1,0:T(8,128)(2,1)S(1)}, bf16[128,1024]{1,0:T(8,128)(2,1)S(1)}) custom-call(s32[11]{0:T(128)S(1)} %pad_add_fusion.4.refs_0_, s32[256,128]{1,0:T(8,128)S(1)} %copy-done.2, bf16[128,1024]{1,0:T(8,128)(2,1)S(1)} %get-tuple-element.81.refs_2_, bf16[128,1024]{1,0:T(8,128)(2,1)} %collective-permute-done.4.refs_3_, ...), custom_call_target="tpu_custom_call" | custom-call | flops 67108864 | bytes 524288 | tf_op jit(solution)/shard_map/attend/pallas_call | solution.py:141
  69.9 5.3 %collective-permute-done.21.refs_4_ = bf16[128,1024]{1,0:T(8,128)(2,1)S(1)} collective-permute-done((bf16[128,1024]{1,0:T(8,128)(2,1)S(1)}, bf16[128,1024]{1,0:T(8,128)(2,1)S(1)}, u32[]{:S(2)}, u32[]{:S(2)}) %collective-permute-start.21) | collective-permute-done | bytes 262176 | tf_op jit(solution)/shard_map/ppermute | solution.py:278
  75.2 1.7 %join.1 = bf16[128,4096]{1,0:T(8,128)(2,1)} custom-call(s32[10]{0:T(128)S(1)} %get-tuple-element.45.place_ref, bf16[128,1024]{1,0:T(8,128)(2,1)S(1)} %get-tuple-element.83.refs_0_, bf16[64,1024]{1,0:T(8,128)(2,1)S(1)} %collective-permute-done.18.refs_1_, bf16[64,1024]{1,0:T(8,128)(2,1)S(1)} %collective-permute-done.19.refs_2_, ...), custom_call_target="tpu_custom_call" | custom-call | tf_op jit(solution)/shard_map/join/pallas_call | solution.py:247
  (66 shorter events, 12.8 us)
Async XLA Ops:
  1.7 13.9 %collective-permute-start = (bf16[32,4096]{1,0:T(8,128)(2,1)}, bf16[32,4096]{1,0:T(8,128)(2,1)}, u32[]{:S(2)}, u32[]{:S(2)}) collective-permute-start(bf16[32,4096]{1,0:T(8,128)(2,1)} %dynamic-slice_bitcast_fusion), channel_id=1, source_target_pairs={{0,8},{1,12},{2,10},{3,14},{4,13},{5,9},{6,15},{7,11},{8,0},{9,4},... | collective-permute-start | bytes 786440 | tf_op jit(solution)/shard_map/ppermute | solution.py:278
  1.7 26.1 %collective-permute-start.1 = (bf16[128,4096]{1,0:T(8,128)(2,1)}, bf16[128,4096]{1,0:T(8,128)(2,1)S(1)}, u32[]{:S(2)}, u32[]{:S(2)}) collective-permute-start(bf16[128,4096]{1,0:T(8,128)(2,1)} %refs_3_.3), channel_id=1, source_target_pairs={{0,2},{1,3},{2,0},{3,1},{4,6},{5,7},{6,4},{7,5},{8,10},{9,11},{10,... | collective-permute-start | bytes 3145736 | tf_op jit(solution)/shard_map/ppermute | solution.py:278
  1.9 26.0 %collective-permute-start.9 = (bf16[64,4096]{1,0:T(8,128)(2,1)}, bf16[64,4096]{1,0:T(8,128)(2,1)}, u32[]{:S(2)}, u32[]{:S(2)}) collective-permute-start(bf16[64,4096]{1,0:T(8,128)(2,1)} %bitcast.20), channel_id=1, source_target_pairs={{0,4},{1,5},{2,6},{3,7},{4,0},{5,1},{6,2},{7,3},{8,12},{9,13},{10,... | collective-permute-start | bytes 1572872 | tf_op jit(solution)/shard_map/ppermute | solution.py:278
  5.8 1.4 %copy-start.10 = (s32[256]{0:T(256)}, s32[256]{0:T(256)S(1)}, u32[]{:S(2)}) copy-start(s32[256]{0:T(256)S(1)} %get-tuple-element.86) | copy-start | bytes 3076
  5.8 5.4 %copy-start.9 = (s32[256]{0:T(256)}, s32[256]{0:T(256)S(1)}, u32[]{:S(2)}) copy-start(s32[256]{0:T(256)S(1)} %get-tuple-element.85) | copy-start | bytes 3076
  9.1 17.3 %copy-start = (bf16[128,4096]{1,0:T(8,128)(2,1)S(1)}, bf16[128,4096]{1,0:T(8,128)(2,1)}, u32[]{:S(2)}) copy-start(bf16[128,4096]{1,0:T(8,128)(2,1)} %refs_3_.3) | copy-start | bytes 3145732
  9.1 18.8 %copy-start.1 = (bf16[4096,64]{0,1:T(8,128)(2,1)S(1)}, bf16[4096,64]{0,1:T(8,128)(2,1)}, u32[]{:S(2)}) copy-start(bf16[4096,64]{0,1:T(8,128)(2,1)} %param.7) | copy-start | bytes 1572868
  17.7 8.7 %collective-permute-start.2 = (bf16[32,4096]{1,0:T(8,128)(2,1)}, bf16[32,4096]{1,0:T(8,128)(2,1)}, u32[]{:S(2)}, u32[]{:S(2)}) collective-permute-start(bf16[32,4096]{1,0:T(8,128)(2,1)} %collective-permute-done.refs_7_), channel_id=1, source_target_pairs={{0,4},{1,5},{2,6},{3,7},{4,0},{5,1},{6,2},{7,3},{8,12},{9,13},{10,... | collective-permute-start | bytes 786440 | tf_op jit(solution)/shard_map/ppermute | solution.py:278
  17.7 10.1 %collective-permute-start.3 = (bf16[32,4096]{1,0:T(8,128)(2,1)}, bf16[32,4096]{1,0:T(8,128)(2,1)}, u32[]{:S(2)}, u32[]{:S(2)}) collective-permute-start(bf16[32,4096]{1,0:T(8,128)(2,1)} %collective-permute-done.refs_7_), channel_id=1, source_target_pairs={{0,16},{1,17},{2,18},{3,19},{4,20},{5,21},{6,22},{7,23},{8,24},{9,... | collective-permute-start | bytes 786440 | tf_op jit(solution)/shard_map/ppermute | solution.py:278
  18.9 8.9 %collective-permute-start.4 = (bf16[128,1024]{1,0:T(8,128)(2,1)}, bf16[128,1024]{1,0:T(8,128)(2,1)}, u32[]{:S(2)}, u32[]{:S(2)}) collective-permute-start(bf16[128,1024]{1,0:T(8,128)(2,1)} %get-tuple-element.50), channel_id=1, source_target_pairs={{0,1},{1,0},{2,3},{3,2},{4,5},{5,4},{6,7},{7,6},{8,9},{9,8},{10,11... | collective-permute-start | bytes 786440 | tf_op jit(solution)/shard_map/ppermute | solution.py:278
  19.5 10.9 %copy-start.8 = (bf16[128,1024]{1,0:T(8,128)(2,1)S(1)}, bf16[128,1024]{1,0:T(8,128)(2,1)}, u32[]{:S(2)}) copy-start(bf16[128,1024]{1,0:T(8,128)(2,1)} %get-tuple-element.53) | copy-start | bytes 786436
  19.5 12.8 %copy-start.7 = (bf16[128,1024]{1,0:T(8,128)(2,1)S(1)}, bf16[128,1024]{1,0:T(8,128)(2,1)}, u32[]{:S(2)}) copy-start(bf16[128,1024]{1,0:T(8,128)(2,1)} %get-tuple-element.54) | copy-start | bytes 786436
  19.5 14.4 %copy-start.5 = (s32[11]{0:T(128)S(1)}, s32[11]{0:T(128)}, u32[]{:S(2)}) copy-start(s32[11]{0:T(128)} %slice_bitcast_fusion.6.refs_0_) | copy-start | bytes 136
  26.4 7.4 %collective-permute-start.7 = (bf16[128,4096]{1,0:T(8,128)(2,1)S(1)}, bf16[128,4096]{1,0:T(8,128)(2,1)S(1)}, u32[]{:S(2)}, u32[]{:S(2)}) collective-permute-start(bf16[128,4096]{1,0:T(8,128)(2,1)S(1)} %copy-done), channel_id=1, source_target_pairs={{0,1},{1,0},{2,3},{3,2},{4,5},{5,4},{6,7},{7,6},{8,9},{9,8},{10,11... | collective-permute-start | bytes 3145736 | tf_op jit(solution)/shard_map/ppermute | solution.py:278
  27.8 6.0 %collective-permute-start.8 = (bf16[128,4096]{1,0:T(8,128)(2,1)S(1)}, bf16[128,4096]{1,0:T(8,128)(2,1)S(1)}, u32[]{:S(2)}, u32[]{:S(2)}) collective-permute-start(bf16[128,4096]{1,0:T(8,128)(2,1)S(1)} %collective-permute-done.1.refs_5_), channel_id=1, source_target_pairs={{0,1},{1,0},{2,3},{3,2},{4,5},{5,4},{6,7},{7,6},{8,9},{9,8},{10,11... | collective-permute-start | bytes 3145736 | tf_op jit(solution)/shard_map/ppermute | solution.py:278
  29.0 8.5 %copy-start.4 = (s32[13]{0:T(128)S(1)}, s32[13]{0:T(128)}, u32[]{:S(2)}) copy-start(s32[13]{0:T(128)} %slice_bitcast_fusion.refs_0_) | copy-start | bytes 160
  29.0 3.3 %collective-permute-start.10 = (bf16[64,4096]{1,0:T(8,128)(2,1)S(1)}, bf16[64,4096]{1,0:T(8,128)(2,1)S(1)}, u32[]{:S(2)}, u32[]{:S(2)}) collective-permute-start(bf16[64,4096]{1,0:T(8,128)(2,1)S(1)} %broadcast_select_fusion), channel_id=1, source_target_pairs={{0,1},{1,0},{2,3},{3,2},{4,5},{5,4},{6,7},{7,6},{8,9},{9,8},{10,11... | collective-permute-start | bytes 1572872 | tf_op jit(solution)/shard_map/ppermute | solution.py:278
  29.1 8.4 %collective-permute-start.11 = (bf16[32,4096]{1,0:T(8,128)(2,1)}, bf16[32,4096]{1,0:T(8,128)(2,1)S(1)}, u32[]{:S(2)}, u32[]{:S(2)}) collective-permute-start(bf16[32,4096]{1,0:T(8,128)(2,1)} %collective-permute-done.2.refs_9_), channel_id=1, source_target_pairs={{0,16},{1,17},{2,18},{3,19},{4,20},{5,21},{6,22},{7,23},{8,24},{9,... | collective-permute-start | bytes 786440 | tf_op jit(solution)/shard_map/ppermute | solution.py:278
  30.4 12.8 %collective-permute-start.5 = (bf16[128,1024]{1,0:T(8,128)(2,1)S(1)}, bf16[128,1024]{1,0:T(8,128)(2,1)S(1)}, u32[]{:S(2)}, u32[]{:S(2)}) collective-permute-start(bf16[128,1024]{1,0:T(8,128)(2,1)S(1)} %copy-done.8), channel_id=1, source_target_pairs={{0,2},{1,3},{2,0},{3,1},{4,6},{5,7},{6,4},{7,5},{8,10},{9,11},{10,... | collective-permute-start | bytes 786440 | tf_op jit(solution)/shard_map/ppermute | solution.py:278
  32.3 12.2 %collective-permute-start.6 = (bf16[128,1024]{1,0:T(8,128)(2,1)S(1)}, bf16[128,1024]{1,0:T(8,128)(2,1)S(1)}, u32[]{:S(2)}, u32[]{:S(2)}) collective-permute-start(bf16[128,1024]{1,0:T(8,128)(2,1)S(1)} %copy-done.7), channel_id=1, source_target_pairs={{0,3},{1,2},{2,1},{3,0},{4,7},{5,6},{6,5},{7,4},{8,11},{9,10},{10,... | collective-permute-start | bytes 786440 | tf_op jit(solution)/shard_map/ppermute | solution.py:278
  36.2 18.7 %copy-start.3 = (s32[7]{0:T(128)S(1)}, s32[7]{0:T(128)}, u32[]{:S(2)}) copy-start(s32[7]{0:T(128)} %pad_add_fusion.5.refs_0_) | copy-start | bytes 88
  36.2 13.4 %collective-permute-start.12 = (bf16[512,128]{1,0:T(8,128)(2,1)S(1)}, bf16[512,128]{1,0:T(8,128)(2,1)S(1)}, u32[]{:S(2)}, u32[]{:S(2)}) collective-permute-start(bf16[512,128]{1,0:T(8,128)(2,1)S(1)} %project.2.refs_4_), channel_id=1, source_target_pairs={{0,8},{1,9},{2,10},{3,11},{4,12},{5,13},{6,14},{7,15},{16,24},{17,... | collective-permute-start | bytes 393224 | tf_op jit(solution)/shard_map/ppermute | solution.py:278
  40.6 11.9 %collective-permute-start.14 = (bf16[512,128]{1,0:T(8,128)(2,1)S(1)}, bf16[512,128]{1,0:T(8,128)(2,1)S(1)}, u32[]{:S(2)}, u32[]{:S(2)}) collective-permute-start(bf16[512,128]{1,0:T(8,128)(2,1)S(1)} %project.3.refs_5_), channel_id=1, source_target_pairs={{0,8},{1,9},{2,10},{3,11},{4,12},{5,13},{6,14},{7,15},{16,24},{17,... | collective-permute-start | bytes 393224 | tf_op jit(solution)/shard_map/ppermute | solution.py:278
  41.9 13.0 %collective-permute-start.17 = (bf16[512,128]{1,0:T(8,128)(2,1)S(1)}, bf16[512,128]{1,0:T(8,128)(2,1)S(1)}, u32[]{:S(2)}, u32[]{:S(2)}) collective-permute-start(bf16[512,128]{1,0:T(8,128)(2,1)S(1)} %project.3.refs_5_), channel_id=1, source_target_pairs={{0,4},{1,5},{2,6},{3,7},{8,12},{9,13},{10,14},{11,15},{16,20},{17,... | collective-permute-start | bytes 393224 | tf_op jit(solution)/shard_map/ppermute | solution.py:278
  43.2 11.7 %collective-permute-start.16 = (bf16[512,128]{1,0:T(8,128)(2,1)S(1)}, bf16[512,128]{1,0:T(8,128)(2,1)S(1)}, u32[]{:S(2)}, u32[]{:S(2)}) collective-permute-start(bf16[512,128]{1,0:T(8,128)(2,1)S(1)} %project.2.refs_4_), channel_id=1, source_target_pairs={{0,4},{1,5},{2,6},{3,7},{8,12},{9,13},{10,14},{11,15},{16,20},{17,... | collective-permute-start | bytes 393224 | tf_op jit(solution)/shard_map/ppermute | solution.py:278
  49.6 7.7 %collective-permute-start.13 = (bf16[512,128]{1,0:T(8,128)(2,1)S(1)}, bf16[512,128]{1,0:T(8,128)(2,1)S(1)}, u32[]{:S(2)}, u32[]{:S(2)}) collective-permute-start(bf16[512,128]{1,0:T(8,128)(2,1)S(1)} %collective-permute-done.12.refs_6_.refs_8_), channel_id=1, source_target_pairs={{8,12},{9,13},{10,14},{11,15},{12,8},{13,9},{14,10},{15,11},{24,28... | collective-permute-start | bytes 393224 | tf_op jit(solution)/shard_map/ppermute | solution.py:278
  52.5 7.6 %collective-permute-start.15 = (bf16[512,128]{1,0:T(8,128)(2,1)S(1)}, bf16[512,128]{1,0:T(8,128)(2,1)S(1)}, u32[]{:S(2)}, u32[]{:S(2)}) collective-permute-start(bf16[512,128]{1,0:T(8,128)(2,1)S(1)} %collective-permute-done.14.refs_7_.refs_9_), channel_id=1, source_target_pairs={{8,12},{9,13},{10,14},{11,15},{12,8},{13,9},{14,10},{15,11},{24,28... | collective-permute-start | bytes 393224 | tf_op jit(solution)/shard_map/ppermute | solution.py:278
  60.1 4.8 %copy-start.2 = (s32[256,128]{1,0:T(8,128)S(1)}, s32[256,128]{1,0:T(8,128)}, u32[]{:S(2)}) copy-start(s32[256,128]{1,0:T(8,128)} %broadcast_in_dim.9.refs_1_) | copy-start | bytes 393220
  61.5 8.4 %collective-permute-start.20 = (bf16[128,1024]{1,0:T(8,128)(2,1)S(1)}, bf16[128,1024]{1,0:T(8,128)(2,1)S(1)}, u32[]{:S(2)}, u32[]{:S(2)}) collective-permute-start(bf16[128,1024]{1,0:T(8,128)(2,1)S(1)} %get-tuple-element.76), channel_id=1, source_target_pairs={{0,2},{1,3},{2,0},{3,1},{4,6},{5,7},{6,4},{7,5},{8,10},{9,11},{10,... | collective-permute-start | bytes 786440 | tf_op jit(solution)/shard_map/ppermute | solution.py:278
  61.9 13.4 %collective-permute-start.21 = (bf16[128,1024]{1,0:T(8,128)(2,1)S(1)}, bf16[128,1024]{1,0:T(8,128)(2,1)S(1)}, u32[]{:S(2)}, u32[]{:S(2)}) collective-permute-start(bf16[128,1024]{1,0:T(8,128)(2,1)S(1)} %get-tuple-element.77), channel_id=1, source_target_pairs={{0,3},{1,2},{2,1},{3,0},{4,7},{5,6},{6,5},{7,4},{8,11},{9,10},{10,... | collective-permute-start | bytes 786440 | tf_op jit(solution)/shard_map/ppermute | solution.py:278
  68.3 1.4 %collective-permute-start.18 = (bf16[64,1024]{1,0:T(8,128)(2,1)S(1)}, bf16[64,1024]{1,0:T(8,128)(2,1)S(1)}, u32[]{:S(2)}, u32[]{:S(2)}) collective-permute-start(bf16[64,1024]{1,0:T(8,128)(2,1)S(1)} %get-tuple-element.92), channel_id=1, source_target_pairs={{0,1},{1,0},{2,3},{3,2},{4,5},{5,4},{6,7},{7,6},{8,9},{9,8},{10,11... | collective-permute-start | bytes 393224 | tf_op jit(solution)/shard_map/ppermute | solution.py:278
  68.3 1.5 %collective-permute-start.19 = (bf16[64,1024]{1,0:T(8,128)(2,1)S(1)}, bf16[64,1024]{1,0:T(8,128)(2,1)S(1)}, u32[]{:S(2)}, u32[]{:S(2)}) collective-permute-start(bf16[64,1024]{1,0:T(8,128)(2,1)S(1)} %get-tuple-element.91), channel_id=1, source_target_pairs={{0,1},{1,0},{2,3},{3,2},{4,5},{5,4},{6,7},{7,6},{8,9},{9,8},{10,11... | collective-permute-start | bytes 393224 | tf_op jit(solution)/shard_map/ppermute | solution.py:278
  (1 other events, 1.2 us)

commit v2 on v1

--- a/solution.py
+++ b/solution.py
@@ -60,32 +60,32 @@
         kv[i, kind] = arrays[2 * i][...]
         kv[i, 1 - kind] = arrays[2 * i + 1][...]
 
-    lanes = chunk // HD
-    starts = jnp.concatenate([starts_ref[...]] * lanes, axis=1)
-    q_pos = jnp.concatenate(
-        [
-            place_ref[i] + lax.broadcasted_iota(jnp.int32, (part_rows, chunk), 0)
-            for i in range(n_q)
-        ],
-        axis=0,
-    )
-    first_chunk = place_ref[n_q + 2 * n_kv] // chunk
+    first_key = place_ref[n_q + 2 * n_kv]
     last_row = place_ref[0]
     for i in range(1, n_q):
         last_row = jnp.maximum(last_row, place_ref[i])
-    end_chunk = (last_row + part_rows + chunk - 1) // chunk
-
-    def attend_chunk(i, j, t):
-        k_pos = t * chunk + lax.broadcasted_iota(jnp.int32, (rows, chunk), 1)
-        bias[...] = jnp.where((k_pos <= q_pos) & (k_pos >= starts), 0.0, MASKED)
-        here = pl.ds(pl.multiple_of(j * chunk, chunk), chunk)
+    end_key = last_row + part_rows
+
+    def attend_keys(i, at, begin, size):
+        lanes = size // HD
+        starts = jnp.concatenate([starts_ref[...]] * lanes, axis=1)
+        q_pos = jnp.concatenate(
+            [
+                place_ref[part] + lax.broadcasted_iota(jnp.int32, (part_rows, size), 0)
+                for part in range(n_q)
+            ],
+            axis=0,
+        )
+        k_pos = begin + lax.broadcasted_iota(jnp.int32, (rows, size), 1)
+        bias[:, :size] = jnp.where((k_pos <= q_pos) & (k_pos >= starts), 0.0, MASKED)
+        here = pl.ds(pl.multiple_of(at, size), size)
         score = lax.dot_general(
             stacked[...],
             kv[i, 0, here, :],
             (((1,), (1,)), ((), ())),
             preferred_element_type=jnp.float32,
         )
-        score = (score.reshape(QPK, rows, chunk) + bias[...][None]).reshape(QPK * rows, chunk)
+        score = (score.reshape(QPK, rows, size) + bias[:, :size][None]).reshape(QPK * rows, size)
         old = stat_m[...]
         top = jnp.maximum(old, jnp.max(score, axis=1, keepdims=True))
         expo = jnp.exp2((score - jnp.concatenate([top] * lanes, axis=1)) * EXP2_SCALE)
@@ -105,11 +105,19 @@
     @pl.loop(0, n_kv * chunks)
     def _(step):
         i, j = step // chunks, step % chunks
-        t = place_ref[n_q + i] * chunks + j
-
-        @pl.when((t >= first_chunk) & (t < end_chunk))
+        begin = (place_ref[n_q + i] * chunks + j) * chunk
+        middle = begin + chunk // 2
+        low = (begin >= 0) & (first_key < middle) & (end_key > begin)
+        high = (begin >= 0) & (first_key < begin + chunk) & (end_key > middle)
+
+        @pl.when(low & high)
         def _():
-            attend_chunk(i, j, t)
+            attend_keys(i, j * chunk, begin, chunk)
+
+        @pl.when(low != high)
+        def _():
+            half = jnp.where(high, chunk // 2, 0)
+            attend_keys(i, j * chunk + half, begin + half, chunk // 2)
 
     if not last:
         return
@@ -162,39 +170,27 @@
 def project_kernel(rows, n_hidden, n_pieces, place_ref, cos_ref, sin_ref, *refs):
     hidden = refs[:n_hidden]
     pieces = refs[n_hidden : n_hidden + n_pieces]
-    out_ref = refs[n_hidden + n_pieces]
-    hbuf, wbuf, hsem, wsem = refs[n_hidden + n_pieces + 1 :]
-
-    def w_copy(i):
+    out_ref, wbuf = refs[n_hidden + n_pieces :]
+
+    for i in range(n_pieces):
         size = pieces[i].shape[0]
-        at = pl.multiple_of(place_ref[2 + n_hidden + 2 * i], size)
-        return pltpu.make_async_copy(pieces[i], wbuf.at[pl.ds(at, size)], wsem.at[i])
-
-    def h_copy(i):
-        at = pl.multiple_of(place_ref[1 + i] * rows, rows)
-        return pltpu.make_async_copy(hidden[i], hbuf.at[pl.ds(at, rows)], hsem.at[i])
-
-    for i in range(n_pieces):
 
         @pl.when(place_ref[1 + n_hidden + 2 * i] == 1)
         def _():
-            w_copy(i).start()
-
+            at = pl.multiple_of(place_ref[2 + n_hidden + 2 * i], size)
+            wbuf[pl.ds(at, size), :] = pieces[i][...]
+
+    heads = lax.dot_general(
+        jnp.concatenate([block[...] for block in hidden], axis=0),
+        wbuf[...],
+        (((1,), (1,)), ((), ())),
+        preferred_element_type=jnp.float32,
+    )
     for i in range(n_hidden):
-        h_copy(i).start()
-    for i in range(n_pieces):
-
-        @pl.when(place_ref[1 + n_hidden + 2 * i] == 1)
-        def _():
-            w_copy(i).wait()
-
-    for i in range(n_hidden):
-        h_copy(i).wait()
-    head = lax.dot_general(
-        hbuf[...], wbuf[...], (((1,), (1,)), ((), ())), preferred_element_type=jnp.float32
-    )
-    turned = head * cos_ref[...] + pltpu.roll(head, HD // 2, 1) * sin_ref[...]
-    out_ref[...] = jnp.where(place_ref[0] == 1, turned, head).astype(jnp.bfloat16)
+        at = pl.ds(pl.multiple_of(place_ref[1 + i] * rows, rows), rows)
+        head = heads[i * rows : (i + 1) * rows]
+        turned = head * cos_ref[at, :] + pltpu.roll(head, HD // 2, 1) * sin_ref[at, :]
+        out_ref[at, :] = jnp.where(place_ref[0] == 1, turned, head).astype(jnp.bfloat16)
 
 
 def project(place, cos, sin, hidden, pieces):
@@ -203,14 +199,9 @@
     return pl.pallas_call(
         lambda *refs: project_kernel(rows, n, len(pieces), *refs),
         out_shape=jax.ShapeDtypeStruct((n * rows, HD), jnp.bfloat16),
-        in_specs=[IN_SMEM, IN_VMEM, IN_VMEM] + [ANY] * (n + len(pieces)),
+        in_specs=[IN_SMEM] + [IN_VMEM] * (2 + n + len(pieces)),
         out_specs=IN_VMEM,
-        scratch_shapes=[
-            pltpu.VMEM((n * rows, depth), jnp.bfloat16),
-            pltpu.VMEM((HD, depth), jnp.bfloat16),
-            pltpu.SemaphoreType.DMA((n,)),
-            pltpu.SemaphoreType.DMA((len(pieces),)),
-        ],
+        scratch_shapes=[pltpu.VMEM((HD, depth), jnp.bfloat16)],
         compiler_params=pltpu.CompilerParams(vmem_limit_bytes=VMEM_LIMIT),
         cost_estimate=pl.CostEstimate(
             flops=rows * depth * HD,
@@ -222,38 +213,20 @@
 
 
 def join_kernel(place_ref, *refs):
-    n = len(refs) - 4
-    out_ref, whole, sem, out_sem = refs[n:]
-    copies = []
-    for i in range(n):
-        height, width = refs[i].shape
+    *parts, out_ref = refs
+    for i, part in enumerate(parts):
+        height, width = part.shape
+        row = pl.multiple_of(place_ref[2 * i], height)
         at = pl.multiple_of(place_ref[2 * i + 1], width)
-        row = pl.multiple_of(place_ref[2 * i], height)
-        copies.append(
-            pltpu.make_async_copy(
-                refs[i], whole.at[pl.ds(row, height), pl.ds(at, width)], sem.at[i]
-            )
-        )
-    for c in copies:
-        c.start()
-    for c in copies:
-        c.wait()
-    copy = pltpu.make_async_copy(whole, out_ref, out_sem)
-    copy.start()
-    copy.wait()
+        out_ref[pl.ds(row, height), pl.ds(at, width)] = part[...]
 
 
 def join(place, parts, shape):
     return pl.pallas_call(
         join_kernel,
         out_shape=jax.ShapeDtypeStruct(shape, parts[0].dtype),
-        in_specs=[IN_SMEM] + [ANY] * len(parts),
-        out_specs=ANY,
-        scratch_shapes=[
-            pltpu.VMEM(shape, parts[0].dtype),
-            pltpu.SemaphoreType.DMA((len(parts),)),
-            pltpu.SemaphoreType.DMA,
-        ],
+        in_specs=[IN_SMEM] + [IN_VMEM] * len(parts),
+        out_specs=IN_VMEM,
         compiler_params=pltpu.CompilerParams(vmem_limit_bytes=VMEM_LIMIT),
         name="join",
     )(place, *parts)

time: 78.4 us -> 78.6 us (level)
  Pallas kernels: 15.4 us -> 22.8 us
  waiting for transfers between devices: 23.5 us -> 17.1 us
    pallas_call x4, Pallas kernels: 8.31 us -> 16.2 us  [attend(): pl.pallas_call(lambda *refs: attend_kernel(rows, chunk, n_q, n_kv, bool(s...]
    ppermute x22, waiting for transfers between devices: 23.5 us -> 17.1 us  [hop(): return lambda v: lax.ppermute(v, AXES, pairs)]
  transfers between devices with their start and end apart: 22 -> 22, of which waited for: 10 -> 10; matrix products, arithmetic and copies ran while one was open for 18% -> 18% of each run, Pallas kernels for 16% -> 24%
where the time goes in v2:
time: 78.6 us; the launch traced here: 77.7 us
  Pallas kernels  22.8 us (29%)
  starting transfers between devices  21.7 us (28%)
  waiting for transfers between devices  17.1 us (22%)
  other arithmetic  8.16 us (10%)
  local copies, waits for them, and re-layouts  7.7 us (10%)
    ppermute x22, starting transfers between devices, hop(): return lambda v: lax.ppermute(v, AXES, pairs)  21.7 us
    ppermute x22, waiting for transfers between devices, hop(): return lambda v: lax.ppermute(v, AXES, pairs)  17.1 us
    pallas_call x4, Pallas kernels, attend(): pl.pallas_call(lambda *refs: attend_kernel(rows, chunk, n_q, n_kv, bool(s...  16.2 us
    pallas_call x2, Pallas kernels, project(): pl.pallas_call(lambda *refs: project_kernel(rows, n, len(pieces), *refs),...  5.04 us
    concatenate x4, other arithmetic, by_planes(): places[at] = jnp.concatenate([places[at], lowest[low]])  3.3 us
    broadcast_in_dim x2, local copies, waits for them, and re-layouts, attend_starts(): jnp.broadcast_to(starts[:, None], (starts.shape[0], HD))  2.12 us
    dynamic_slice x1, local copies, waits for them, and re-layouts, by_planes(): far_0 = far(lax.dynamic_slice_in_dim(weight, x * part, part, 0))  1.66 us
    pallas_call x1, Pallas kernels, join(): pl.pallas_call(join_kernel, out_shape=jax.ShapeDtypeStruct(shape, parts[0...  1.58 us
  transfers between devices with their start and end apart: 22, of which 10 were waited for; matrix products, arithmetic and copies ran while one was open for 18% of the time, Pallas kernels for 24%

profile of v2, /device:TPU:29, one launch (start us, length us, event | category | flops | bytes accessed | tf_op | source)
XLA Modules:
  0.0 77.7 jit_solution(15751499128735459191)
XLA Ops:
  0.0 1.7 %dynamic-slice_bitcast_fusion = bf16[32,4096]{1,0:T(8,128)(2,1)} fusion(bf16[4096,64]{0,1:T(8,128)(2,1)} %param.7, s32[]{:T(128)S(6)} %select_n.60), kind=kLoop, calls=%fused_computation.7 | loop fusion | bytes 524292 | tf_op jit(solution)/shard_map/dynamic_slice | solution.py:299
  3.6 0.9 %fusion.2 = (s32[128]{0:T(128)S(1)}, s32[128]{0:T(128)S(1)}, s32[128]{0:T(128)S(1)}, s32[128]{0:T(128)S(1)}) fusion(s32[2048]{0:T(1024)} %param.8, s32[]{:T(128)S(6)} %select_n.65, s32[]{:T(128)S(6)} %select_n.66, s32[]{:T(128)S(6)} %select_n.68, s32[]{:T(128)S(6)} %select_n.67), kind=kLoop, calls=%fused_computation.30 | loop fusion | bytes 4112 | tf_op jit(solution)/shard_map/dynamic_slice | solution.py:134
  4.6 1.2 %convert_reduce_fusion = (s32[256]{0:T(256)S(1)}, s32[256]{0:T(256)S(1)}) fusion(s32[2048]{0:T(1024)} %param.8, s32[256]{0:T(256)S(1)} %get-tuple-element.105, s32[256]{0:T(256)S(1)} %get-tuple-element.104), kind=kLoop, calls=%fused_computation | loop fusion | flops 3145216 | bytes 12288 | tf_op jit(solution)/shard_map/reduce_sum | solution.py:136
  7.9 1.0 %fusion = (f32[512,64]{1,0:T(8,128)S(1)}, f32[512,64]{1,0:T(8,128)S(1)}, f32[512,64]{1,0:T(8,128)S(1)}) fusion(f32[64]{0:T(128)S(1)} %multiply_power_fusion, f32[512]{0:T(512)S(1)} %add_convert_fusion), kind=kLoop, calls=%fused_computation.8 | loop fusion | flops 65536 | bytes 395520 | tf_op jit(solution)/shard_map/neg | solution.py:307
  10.0 1.2 %pad_add_fusion.5.refs_0_ = s32[7]{0:T(128)} fusion(s32[1]{0:T(128)} %bitcast.3, s32[6]{0:T(128)S(1)} %slice_bitcast_fusion.2), kind=kLoop, calls=%fused_computation.20 | loop fusion | flops 7 | bytes 56 | tf_op jit(solution)/shard_map/concatenate | solution.py:314
  13.8 1.8 %collective-permute-done.refs_7_ = bf16[32,4096]{1,0:T(8,128)(2,1)} collective-permute-done((bf16[32,4096]{1,0:T(8,128)(2,1)}, bf16[32,4096]{1,0:T(8,128)(2,1)}, u32[]{:S(2)}, u32[]{:S(2)}) %collective-permute-start) | collective-permute-done | bytes 262176 | tf_op jit(solution)/shard_map/ppermute | solution.py:251
  16.3 1.4 %broadcast_in_dim.9.refs_1_ = s32[256,128]{1,0:T(8,128)} broadcast(s32[256]{0:T(256)} %copy-done.9), dimensions={0} | broadcast | bytes 132096 | tf_op jit(solution)/shard_map/broadcast_in_dim | solution.py:137
  17.7 1.2 %collective-permute-start.3 = (bf16[32,4096]{1,0:T(8,128)(2,1)}, bf16[32,4096]{1,0:T(8,128)(2,1)}, u32[]{:S(2)}, u32[]{:S(2)}) collective-permute-start(bf16[32,4096]{1,0:T(8,128)(2,1)} %collective-permute-done.refs_7_), channel_id=1, source_target_pairs={{0,16},{1,17},{2,18},{3,19},{4,20},{5,21},{6,22},{7,23},{8,24},{9,... | collective-permute-start | bytes 786440 | tf_op jit(solution)/shard_map/ppermute | solution.py:251
  19.5 6.9 %collective-permute-done.2.refs_9_ = bf16[32,4096]{1,0:T(8,128)(2,1)} collective-permute-done((bf16[32,4096]{1,0:T(8,128)(2,1)}, bf16[32,4096]{1,0:T(8,128)(2,1)}, u32[]{:S(2)}, u32[]{:S(2)}) %collective-permute-start.2) | collective-permute-done | bytes 262176 | tf_op jit(solution)/shard_map/ppermute | solution.py:251
  26.4 1.4 %collective-permute-start.7 = (bf16[128,4096]{1,0:T(8,128)(2,1)S(1)}, bf16[128,4096]{1,0:T(8,128)(2,1)S(1)}, u32[]{:S(2)}, u32[]{:S(2)}) collective-permute-start(bf16[128,4096]{1,0:T(8,128)(2,1)S(1)} %copy-done), channel_id=1, source_target_pairs={{0,1},{1,0},{2,3},{3,2},{4,5},{5,4},{6,7},{7,6},{8,9},{9,8},{10,11... | collective-permute-start | bytes 3145736 | tf_op jit(solution)/shard_map/ppermute | solution.py:251
  27.9 1.1 %broadcast_select_fusion = bf16[64,4096]{1,0:T(8,128)(2,1)S(1)} fusion(bf16[64,4096]{1,0:T(8,128)(2,1)} %collective-permute-done.9.refs_8_, pred[]{:T(512)S(6)} %eq.7, bf16[4096,64]{0,1:T(8,128)(2,1)S(1)} %copy-done.1), kind=kLoop, calls=%fused_computation.2 | loop fusion | flops 262144 | bytes 1572865 | tf_op jit(solution)/shard_map/jit(_where)/select_n | solution.py:325
  29.1 1.3 %collective-permute-start.11 = (bf16[32,4096]{1,0:T(8,128)(2,1)}, bf16[32,4096]{1,0:T(8,128)(2,1)S(1)}, u32[]{:S(2)}, u32[]{:S(2)}) collective-permute-start(bf16[32,4096]{1,0:T(8,128)(2,1)} %collective-permute-done.2.refs_9_), channel_id=1, source_target_pairs={{0,16},{1,17},{2,18},{3,19},{4,20},{5,21},{6,22},{7,23},{8,24},{9,... | collective-permute-start | bytes 786440 | tf_op jit(solution)/shard_map/ppermute | solution.py:251
  30.4 1.2 %collective-permute-start.5 = (bf16[128,1024]{1,0:T(8,128)(2,1)S(1)}, bf16[128,1024]{1,0:T(8,128)(2,1)S(1)}, u32[]{:S(2)}, u32[]{:S(2)}) collective-permute-start(bf16[128,1024]{1,0:T(8,128)(2,1)S(1)} %copy-done.8), channel_id=1, source_target_pairs={{0,2},{1,3},{2,0},{3,1},{4,6},{5,7},{6,4},{7,5},{8,10},{9,11},{10,... | collective-permute-start | bytes 786440 | tf_op jit(solution)/shard_map/ppermute | solution.py:251
  32.3 1.5 %collective-permute-start.6 = (bf16[128,1024]{1,0:T(8,128)(2,1)S(1)}, bf16[128,1024]{1,0:T(8,128)(2,1)S(1)}, u32[]{:S(2)}, u32[]{:S(2)}) collective-permute-start(bf16[128,1024]{1,0:T(8,128)(2,1)S(1)} %copy-done.7), channel_id=1, source_target_pairs={{0,3},{1,2},{2,1},{3,0},{4,7},{5,6},{6,5},{7,4},{8,11},{9,10},{10,... | collective-permute-start | bytes 786440 | tf_op jit(solution)/shard_map/ppermute | solution.py:251
  33.8 2.5 %project.2.refs_4_ = bf16[512,128]{1,0:T(8,128)(2,1)S(1)} custom-call(s32[11]{0:T(128)S(1)} %copy-done.5, f32[512,128]{1,0:T(8,128)S(1)} %get-tuple-element.57.refs_1_, f32[512,128]{1,0:T(8,128)S(1)} %get-tuple-element.58.refs_2_, bf16[128,4096]{1,0:T(8,128)(2,1)S(1)} %copy-done, bf16[128,4096]{1,0:T(8,128)(2,1)S(1)} %collective-permute-done.7.refs_4_, ...), custom_call_target="tpu_custom_call" | custom-call | flops 67108864 | bytes 524288 | tf_op jit(solution)/shard_map/project/pallas_call | solution.py:199
  36.3 1.3 %collective-permute-start.12 = (bf16[512,128]{1,0:T(8,128)(2,1)S(1)}, bf16[512,128]{1,0:T(8,128)(2,1)S(1)}, u32[]{:S(2)}, u32[]{:S(2)}) collective-permute-start(bf16[512,128]{1,0:T(8,128)(2,1)S(1)} %project.2.refs_4_), channel_id=1, source_target_pairs={{0,8},{1,9},{2,10},{3,11},{4,12},{5,13},{6,14},{7,15},{16,24},{17,... | collective-permute-start | bytes 393224 | tf_op jit(solution)/shard_map/ppermute | solution.py:251
  37.7 2.6 %project.3.refs_5_ = bf16[512,128]{1,0:T(8,128)(2,1)S(1)} custom-call(s32[13]{0:T(128)S(1)} %copy-done.4, f32[512,128]{1,0:T(8,128)S(1)} %get-tuple-element.57.refs_1_, f32[512,128]{1,0:T(8,128)S(1)} %get-tuple-element.58.refs_2_, bf16[128,4096]{1,0:T(8,128)(2,1)S(1)} %copy-done, bf16[128,4096]{1,0:T(8,128)(2,1)S(1)} %collective-permute-done.7.refs_4_, ...), custom_call_target="tpu_custom_call" | custom-call | flops 67108864 | bytes 524288 | tf_op jit(solution)/shard_map/project/pallas_call | solution.py:199
  40.2 1.3 %collective-permute-start.14 = (bf16[512,128]{1,0:T(8,128)(2,1)S(1)}, bf16[512,128]{1,0:T(8,128)(2,1)S(1)}, u32[]{:S(2)}, u32[]{:S(2)}) collective-permute-start(bf16[512,128]{1,0:T(8,128)(2,1)S(1)} %project.3.refs_5_), channel_id=1, source_target_pairs={{0,8},{1,9},{2,10},{3,11},{4,12},{5,13},{6,14},{7,15},{16,24},{17,... | collective-permute-start | bytes 393224 | tf_op jit(solution)/shard_map/ppermute | solution.py:251
  41.5 1.3 %collective-permute-start.17 = (bf16[512,128]{1,0:T(8,128)(2,1)S(1)}, bf16[512,128]{1,0:T(8,128)(2,1)S(1)}, u32[]{:S(2)}, u32[]{:S(2)}) collective-permute-start(bf16[512,128]{1,0:T(8,128)(2,1)S(1)} %project.3.refs_5_), channel_id=1, source_target_pairs={{0,4},{1,5},{2,6},{3,7},{8,12},{9,13},{10,14},{11,15},{16,20},{17,... | collective-permute-start | bytes 393224 | tf_op jit(solution)/shard_map/ppermute | solution.py:251
  42.8 1.3 %collective-permute-start.16 = (bf16[512,128]{1,0:T(8,128)(2,1)S(1)}, bf16[512,128]{1,0:T(8,128)(2,1)S(1)}, u32[]{:S(2)}, u32[]{:S(2)}) collective-permute-start(bf16[512,128]{1,0:T(8,128)(2,1)S(1)} %project.2.refs_4_), channel_id=1, source_target_pairs={{0,4},{1,5},{2,6},{3,7},{8,12},{9,13},{10,14},{11,15},{16,20},{17,... | collective-permute-start | bytes 393224 | tf_op jit(solution)/shard_map/ppermute | solution.py:251
  44.3 1.9 %attend.4 = (f32[2048,128]{1,0:T(8,128)S(1)}, f32[2048,128]{1,0:T(8,128)S(1)}, f32[2048,128]{1,0:T(8,128)S(1)}) custom-call(s32[5]{0:T(128)S(1)} %pad_add_fusion.2.refs_0_, s32[256,128]{1,0:T(8,128)S(1)} %broadcast_in_dim.8.refs_1_, bf16[128,1024]{1,0:T(8,128)(2,1)S(1)} %collective-permute-done.5.refs_2_, ...), custom_call_target="tpu_custom_call" | custom-call | flops 67108864 | bytes 524288 | tf_op jit(solution)/shard_map/attend/pallas_call | solution.py:149
  46.3 2.9 %collective-permute-done.12.refs_6_.refs_8_ = bf16[512,128]{1,0:T(8,128)(2,1)S(1)} collective-permute-done((bf16[512,128]{1,0:T(8,128)(2,1)S(1)}, bf16[512,128]{1,0:T(8,128)(2,1)S(1)}, u32[]{:S(2)}, u32[]{:S(2)}) %collective-permute-start.12) | collective-permute-done | bytes 131104 | tf_op jit(solution)/shard_map/ppermute | solution.py:251
  49.2 1.9 %collective-permute-start.13 = (bf16[512,128]{1,0:T(8,128)(2,1)S(1)}, bf16[512,128]{1,0:T(8,128)(2,1)S(1)}, u32[]{:S(2)}, u32[]{:S(2)}) collective-permute-start(bf16[512,128]{1,0:T(8,128)(2,1)S(1)} %collective-permute-done.12.refs_6_.refs_8_), channel_id=1, source_target_pairs={{8,12},{9,13},{10,14},{11,15},{12,8},{13,9},{14,10},{15,11},{24,28... | collective-permute-start | bytes 393224 | tf_op jit(solution)/shard_map/ppermute | solution.py:251
  51.1 0.9 %collective-permute-done.14.refs_7_.refs_9_ = bf16[512,128]{1,0:T(8,128)(2,1)S(1)} collective-permute-done((bf16[512,128]{1,0:T(8,128)(2,1)S(1)}, bf16[512,128]{1,0:T(8,128)(2,1)S(1)}, u32[]{:S(2)}, u32[]{:S(2)}) %collective-permute-start.14) | collective-permute-done | bytes 131104 | tf_op jit(solution)/shard_map/ppermute | solution.py:251
  52.0 2.6 %collective-permute-start.15 = (bf16[512,128]{1,0:T(8,128)(2,1)S(1)}, bf16[512,128]{1,0:T(8,128)(2,1)S(1)}, u32[]{:S(2)}, u32[]{:S(2)}) collective-permute-start(bf16[512,128]{1,0:T(8,128)(2,1)S(1)} %collective-permute-done.14.refs_7_.refs_9_), channel_id=1, source_target_pairs={{8,12},{9,13},{10,14},{11,15},{12,8},{13,9},{14,10},{15,11},{24,28... | collective-permute-start | bytes 393224 | tf_op jit(solution)/shard_map/ppermute | solution.py:251
  54.7 4.4 %attend.5 = (f32[2048,128]{1,0:T(8,128)S(1)}, f32[2048,128]{1,0:T(8,128)S(1)}, f32[2048,128]{1,0:T(8,128)S(1)}) custom-call(s32[7]{0:T(128)S(1)} %copy-done.3, s32[256,128]{1,0:T(8,128)S(1)} %broadcast_in_dim.8.refs_1_, bf16[128,1024]{1,0:T(8,128)(2,1)S(1)} %collective-permute-done.5.refs_2_, bf16[128,1024]{1,0:T(8,128)(2,1)S(1)} %collective-permute-done.6.refs_3_, ...), custom_call_target="tpu_custom_call" | custom-call | flops 67108864 | bytes 524288 | tf_op jit(solution)/shard_map/attend/pallas_call | solution.py:149
  59.1 1.0 %collective-permute-done.15.refs_5_.refs_11_ = bf16[512,128]{1,0:T(8,128)(2,1)S(1)} collective-permute-done((bf16[512,128]{1,0:T(8,128)(2,1)S(1)}, bf16[512,128]{1,0:T(8,128)(2,1)S(1)}, u32[]{:S(2)}, u32[]{:S(2)}) %collective-permute-start.15) | collective-permute-done | bytes 131104 | tf_op jit(solution)/shard_map/ppermute | solution.py:251
  60.2 2.2 %attend.6 = (bf16[128,1024]{1,0:T(8,128)(2,1)S(1)}, bf16[128,1024]{1,0:T(8,128)(2,1)S(1)}) custom-call(s32[5]{0:T(128)S(1)} %pad_add_fusion.3.refs_0_, s32[256,128]{1,0:T(8,128)S(1)} %broadcast_in_dim.8.refs_1_, bf16[128,1024]{1,0:T(8,128)(2,1)S(1)} %collective-permute-done.5.refs_2_, bf16[128,1024]{1,0:T(8,128)(2,1)S(1)} %collective-permute-done.6.refs_3_, ...), custom_call_target="tpu_custom_call" | custom-call | flops 67108864 | bytes 524288 | tf_op jit(solution)/shard_map/attend/pallas_call | solution.py:149
  62.6 2.8 %collective-permute-start.21 = (bf16[128,1024]{1,0:T(8,128)(2,1)S(1)}, bf16[128,1024]{1,0:T(8,128)(2,1)S(1)}, u32[]{:S(2)}, u32[]{:S(2)}) collective-permute-start(bf16[128,1024]{1,0:T(8,128)(2,1)S(1)} %get-tuple-element.77), channel_id=1, source_target_pairs={{0,3},{1,2},{2,1},{3,0},{4,7},{5,6},{6,5},{7,4},{8,11},{9,10},{10,... | collective-permute-start | bytes 786440 | tf_op jit(solution)/shard_map/ppermute | solution.py:251
  65.4 7.6 %attend.7 = (bf16[128,1024]{1,0:T(8,128)(2,1)S(1)}, bf16[128,1024]{1,0:T(8,128)(2,1)S(1)}) custom-call(s32[11]{0:T(128)S(1)} %pad_add_fusion.4.refs_0_, s32[256,128]{1,0:T(8,128)S(1)} %copy-done.2, bf16[128,1024]{1,0:T(8,128)(2,1)S(1)} %get-tuple-element.81.refs_2_, bf16[128,1024]{1,0:T(8,128)(2,1)} %collective-permute-done.4.refs_3_, ...), custom_call_target="tpu_custom_call" | custom-call | flops 67108864 | bytes 524288 | tf_op jit(solution)/shard_map/attend/pallas_call | solution.py:149
  74.6 1.5 %collective-permute-done.21.refs_4_ = bf16[128,1024]{1,0:T(8,128)(2,1)S(1)} collective-permute-done((bf16[128,1024]{1,0:T(8,128)(2,1)S(1)}, bf16[128,1024]{1,0:T(8,128)(2,1)S(1)}, u32[]{:S(2)}, u32[]{:S(2)}) %collective-permute-start.21) | collective-permute-done | bytes 262176 | tf_op jit(solution)/shard_map/ppermute | solution.py:251
  76.1 1.6 %join.1 = bf16[128,4096]{1,0:T(8,128)(2,1)} custom-call(s32[10]{0:T(128)S(1)} %get-tuple-element.45.place_ref, bf16[128,1024]{1,0:T(8,128)(2,1)S(1)} %get-tuple-element.83.refs_0_, bf16[64,1024]{1,0:T(8,128)(2,1)S(1)} %collective-permute-done.18.refs_1_, bf16[64,1024]{1,0:T(8,128)(2,1)S(1)} %collective-permute-done.19.refs_2_, ...), custom_call_target="tpu_custom_call" | custom-call | tf_op jit(solution)/shard_map/join/pallas_call | solution.py:225
  (66 shorter events, 11.9 us)
Async XLA Ops:
  1.7 13.9 %collective-permute-start = (bf16[32,4096]{1,0:T(8,128)(2,1)}, bf16[32,4096]{1,0:T(8,128)(2,1)}, u32[]{:S(2)}, u32[]{:S(2)}) collective-permute-start(bf16[32,4096]{1,0:T(8,128)(2,1)} %dynamic-slice_bitcast_fusion), channel_id=1, source_target_pairs={{0,8},{1,12},{2,10},{3,14},{4,13},{5,9},{6,15},{7,11},{8,0},{9,4},... | collective-permute-start | bytes 786440 | tf_op jit(solution)/shard_map/ppermute | solution.py:251
  1.7 26.1 %collective-permute-start.1 = (bf16[128,4096]{1,0:T(8,128)(2,1)}, bf16[128,4096]{1,0:T(8,128)(2,1)S(1)}, u32[]{:S(2)}, u32[]{:S(2)}) collective-permute-start(bf16[128,4096]{1,0:T(8,128)(2,1)} %refs_3_.3), channel_id=1, source_target_pairs={{0,2},{1,3},{2,0},{3,1},{4,6},{5,7},{6,4},{7,5},{8,10},{9,11},{10,... | collective-permute-start | bytes 3145736 | tf_op jit(solution)/shard_map/ppermute | solution.py:251
  1.9 26.0 %collective-permute-start.9 = (bf16[64,4096]{1,0:T(8,128)(2,1)}, bf16[64,4096]{1,0:T(8,128)(2,1)}, u32[]{:S(2)}, u32[]{:S(2)}) collective-permute-start(bf16[64,4096]{1,0:T(8,128)(2,1)} %bitcast.20), channel_id=1, source_target_pairs={{0,4},{1,5},{2,6},{3,7},{4,0},{5,1},{6,2},{7,3},{8,12},{9,13},{10,... | collective-permute-start | bytes 1572872 | tf_op jit(solution)/shard_map/ppermute | solution.py:251
  5.8 1.4 %copy-start.10 = (s32[256]{0:T(256)}, s32[256]{0:T(256)S(1)}, u32[]{:S(2)}) copy-start(s32[256]{0:T(256)S(1)} %get-tuple-element.86) | copy-start | bytes 3076
  5.8 5.4 %copy-start.9 = (s32[256]{0:T(256)}, s32[256]{0:T(256)S(1)}, u32[]{:S(2)}) copy-start(s32[256]{0:T(256)S(1)} %get-tuple-element.85) | copy-start | bytes 3076
  9.1 17.3 %copy-start = (bf16[128,4096]{1,0:T(8,128)(2,1)S(1)}, bf16[128,4096]{1,0:T(8,128)(2,1)}, u32[]{:S(2)}) copy-start(bf16[128,4096]{1,0:T(8,128)(2,1)} %refs_3_.3) | copy-start | bytes 3145732
  9.1 18.8 %copy-start.1 = (bf16[4096,64]{0,1:T(8,128)(2,1)S(1)}, bf16[4096,64]{0,1:T(8,128)(2,1)}, u32[]{:S(2)}) copy-start(bf16[4096,64]{0,1:T(8,128)(2,1)} %param.7) | copy-start | bytes 1572868
  17.7 8.7 %collective-permute-start.2 = (bf16[32,4096]{1,0:T(8,128)(2,1)}, bf16[32,4096]{1,0:T(8,128)(2,1)}, u32[]{:S(2)}, u32[]{:S(2)}) collective-permute-start(bf16[32,4096]{1,0:T(8,128)(2,1)} %collective-permute-done.refs_7_), channel_id=1, source_target_pairs={{0,4},{1,5},{2,6},{3,7},{4,0},{5,1},{6,2},{7,3},{8,12},{9,13},{10,... | collective-permute-start | bytes 786440 | tf_op jit(solution)/shard_map/ppermute | solution.py:251
  17.7 10.1 %collective-permute-start.3 = (bf16[32,4096]{1,0:T(8,128)(2,1)}, bf16[32,4096]{1,0:T(8,128)(2,1)}, u32[]{:S(2)}, u32[]{:S(2)}) collective-permute-start(bf16[32,4096]{1,0:T(8,128)(2,1)} %collective-permute-done.refs_7_), channel_id=1, source_target_pairs={{0,16},{1,17},{2,18},{3,19},{4,20},{5,21},{6,22},{7,23},{8,24},{9,... | collective-permute-start | bytes 786440 | tf_op jit(solution)/shard_map/ppermute | solution.py:251
  18.9 8.9 %collective-permute-start.4 = (bf16[128,1024]{1,0:T(8,128)(2,1)}, bf16[128,1024]{1,0:T(8,128)(2,1)}, u32[]{:S(2)}, u32[]{:S(2)}) collective-permute-start(bf16[128,1024]{1,0:T(8,128)(2,1)} %get-tuple-element.50), channel_id=1, source_target_pairs={{0,1},{1,0},{2,3},{3,2},{4,5},{5,4},{6,7},{7,6},{8,9},{9,8},{10,11... | collective-permute-start | bytes 786440 | tf_op jit(solution)/shard_map/ppermute | solution.py:251
  19.5 10.9 %copy-start.8 = (bf16[128,1024]{1,0:T(8,128)(2,1)S(1)}, bf16[128,1024]{1,0:T(8,128)(2,1)}, u32[]{:S(2)}) copy-start(bf16[128,1024]{1,0:T(8,128)(2,1)} %get-tuple-element.53) | copy-start | bytes 786436
  19.5 12.8 %copy-start.7 = (bf16[128,1024]{1,0:T(8,128)(2,1)S(1)}, bf16[128,1024]{1,0:T(8,128)(2,1)}, u32[]{:S(2)}) copy-start(bf16[128,1024]{1,0:T(8,128)(2,1)} %get-tuple-element.54) | copy-start | bytes 786436
  19.5 14.4 %copy-start.5 = (s32[11]{0:T(128)S(1)}, s32[11]{0:T(128)}, u32[]{:S(2)}) copy-start(s32[11]{0:T(128)} %slice_bitcast_fusion.6.refs_0_) | copy-start | bytes 136
  26.4 7.4 %collective-permute-start.7 = (bf16[128,4096]{1,0:T(8,128)(2,1)S(1)}, bf16[128,4096]{1,0:T(8,128)(2,1)S(1)}, u32[]{:S(2)}, u32[]{:S(2)}) collective-permute-start(bf16[128,4096]{1,0:T(8,128)(2,1)S(1)} %copy-done), channel_id=1, source_target_pairs={{0,1},{1,0},{2,3},{3,2},{4,5},{5,4},{6,7},{7,6},{8,9},{9,8},{10,11... | collective-permute-start | bytes 3145736 | tf_op jit(solution)/shard_map/ppermute | solution.py:251
  27.8 6.0 %collective-permute-start.8 = (bf16[128,4096]{1,0:T(8,128)(2,1)S(1)}, bf16[128,4096]{1,0:T(8,128)(2,1)S(1)}, u32[]{:S(2)}, u32[]{:S(2)}) collective-permute-start(bf16[128,4096]{1,0:T(8,128)(2,1)S(1)} %collective-permute-done.1.refs_5_), channel_id=1, source_target_pairs={{0,1},{1,0},{2,3},{3,2},{4,5},{5,4},{6,7},{7,6},{8,9},{9,8},{10,11... | collective-permute-start | bytes 3145736 | tf_op jit(solution)/shard_map/ppermute | solution.py:251
  29.0 8.6 %copy-start.4 = (s32[13]{0:T(128)S(1)}, s32[13]{0:T(128)}, u32[]{:S(2)}) copy-start(s32[13]{0:T(128)} %slice_bitcast_fusion.refs_0_) | copy-start | bytes 160
  29.0 3.3 %collective-permute-start.10 = (bf16[64,4096]{1,0:T(8,128)(2,1)S(1)}, bf16[64,4096]{1,0:T(8,128)(2,1)S(1)}, u32[]{:S(2)}, u32[]{:S(2)}) collective-permute-start(bf16[64,4096]{1,0:T(8,128)(2,1)S(1)} %broadcast_select_fusion), channel_id=1, source_target_pairs={{0,1},{1,0},{2,3},{3,2},{4,5},{5,4},{6,7},{7,6},{8,9},{9,8},{10,11... | collective-permute-start | bytes 1572872 | tf_op jit(solution)/shard_map/ppermute | solution.py:251
  29.1 8.5 %collective-permute-start.11 = (bf16[32,4096]{1,0:T(8,128)(2,1)}, bf16[32,4096]{1,0:T(8,128)(2,1)S(1)}, u32[]{:S(2)}, u32[]{:S(2)}) collective-permute-start(bf16[32,4096]{1,0:T(8,128)(2,1)} %collective-permute-done.2.refs_9_), channel_id=1, source_target_pairs={{0,16},{1,17},{2,18},{3,19},{4,20},{5,21},{6,22},{7,23},{8,24},{9,... | collective-permute-start | bytes 786440 | tf_op jit(solution)/shard_map/ppermute | solution.py:251
  30.4 12.4 %collective-permute-start.5 = (bf16[128,1024]{1,0:T(8,128)(2,1)S(1)}, bf16[128,1024]{1,0:T(8,128)(2,1)S(1)}, u32[]{:S(2)}, u32[]{:S(2)}) collective-permute-start(bf16[128,1024]{1,0:T(8,128)(2,1)S(1)} %copy-done.8), channel_id=1, source_target_pairs={{0,2},{1,3},{2,0},{3,1},{4,6},{5,7},{6,4},{7,5},{8,10},{9,11},{10,... | collective-permute-start | bytes 786440 | tf_op jit(solution)/shard_map/ppermute | solution.py:251
  32.3 12.0 %collective-permute-start.6 = (bf16[128,1024]{1,0:T(8,128)(2,1)S(1)}, bf16[128,1024]{1,0:T(8,128)(2,1)S(1)}, u32[]{:S(2)}, u32[]{:S(2)}) collective-permute-start(bf16[128,1024]{1,0:T(8,128)(2,1)S(1)} %copy-done.7), channel_id=1, source_target_pairs={{0,3},{1,2},{2,1},{3,0},{4,7},{5,6},{6,5},{7,4},{8,11},{9,10},{10,... | collective-permute-start | bytes 786440 | tf_op jit(solution)/shard_map/ppermute | solution.py:251
  36.3 18.4 %copy-start.3 = (s32[7]{0:T(128)S(1)}, s32[7]{0:T(128)}, u32[]{:S(2)}) copy-start(s32[7]{0:T(128)} %pad_add_fusion.5.refs_0_) | copy-start | bytes 88
  36.3 12.9 %collective-permute-start.12 = (bf16[512,128]{1,0:T(8,128)(2,1)S(1)}, bf16[512,128]{1,0:T(8,128)(2,1)S(1)}, u32[]{:S(2)}, u32[]{:S(2)}) collective-permute-start(bf16[512,128]{1,0:T(8,128)(2,1)S(1)} %project.2.refs_4_), channel_id=1, source_target_pairs={{0,8},{1,9},{2,10},{3,11},{4,12},{5,13},{6,14},{7,15},{16,24},{17,... | collective-permute-start | bytes 393224 | tf_op jit(solution)/shard_map/ppermute | solution.py:251
  40.2 11.8 %collective-permute-start.14 = (bf16[512,128]{1,0:T(8,128)(2,1)S(1)}, bf16[512,128]{1,0:T(8,128)(2,1)S(1)}, u32[]{:S(2)}, u32[]{:S(2)}) collective-permute-start(bf16[512,128]{1,0:T(8,128)(2,1)S(1)} %project.3.refs_5_), channel_id=1, source_target_pairs={{0,8},{1,9},{2,10},{3,11},{4,12},{5,13},{6,14},{7,15},{16,24},{17,... | collective-permute-start | bytes 393224 | tf_op jit(solution)/shard_map/ppermute | solution.py:251
  41.5 13.2 %collective-permute-start.17 = (bf16[512,128]{1,0:T(8,128)(2,1)S(1)}, bf16[512,128]{1,0:T(8,128)(2,1)S(1)}, u32[]{:S(2)}, u32[]{:S(2)}) collective-permute-start(bf16[512,128]{1,0:T(8,128)(2,1)S(1)} %project.3.refs_5_), channel_id=1, source_target_pairs={{0,4},{1,5},{2,6},{3,7},{8,12},{9,13},{10,14},{11,15},{16,20},{17,... | collective-permute-start | bytes 393224 | tf_op jit(solution)/shard_map/ppermute | solution.py:251
  42.8 11.9 %collective-permute-start.16 = (bf16[512,128]{1,0:T(8,128)(2,1)S(1)}, bf16[512,128]{1,0:T(8,128)(2,1)S(1)}, u32[]{:S(2)}, u32[]{:S(2)}) collective-permute-start(bf16[512,128]{1,0:T(8,128)(2,1)S(1)} %project.2.refs_4_), channel_id=1, source_target_pairs={{0,4},{1,5},{2,6},{3,7},{8,12},{9,13},{10,14},{11,15},{16,20},{17,... | collective-permute-start | bytes 393224 | tf_op jit(solution)/shard_map/ppermute | solution.py:251
  49.2 10.0 %collective-permute-start.13 = (bf16[512,128]{1,0:T(8,128)(2,1)S(1)}, bf16[512,128]{1,0:T(8,128)(2,1)S(1)}, u32[]{:S(2)}, u32[]{:S(2)}) collective-permute-start(bf16[512,128]{1,0:T(8,128)(2,1)S(1)} %collective-permute-done.12.refs_6_.refs_8_), channel_id=1, source_target_pairs={{8,12},{9,13},{10,14},{11,15},{12,8},{13,9},{14,10},{15,11},{24,28... | collective-permute-start | bytes 393224 | tf_op jit(solution)/shard_map/ppermute | solution.py:251
  52.0 8.1 %collective-permute-start.15 = (bf16[512,128]{1,0:T(8,128)(2,1)S(1)}, bf16[512,128]{1,0:T(8,128)(2,1)S(1)}, u32[]{:S(2)}, u32[]{:S(2)}) collective-permute-start(bf16[512,128]{1,0:T(8,128)(2,1)S(1)} %collective-permute-done.14.refs_7_.refs_9_), channel_id=1, source_target_pairs={{8,12},{9,13},{10,14},{11,15},{12,8},{13,9},{14,10},{15,11},{24,28... | collective-permute-start | bytes 393224 | tf_op jit(solution)/shard_map/ppermute | solution.py:251
  60.2 5.2 %copy-start.2 = (s32[256,128]{1,0:T(8,128)S(1)}, s32[256,128]{1,0:T(8,128)}, u32[]{:S(2)}) copy-start(s32[256,128]{1,0:T(8,128)} %broadcast_in_dim.9.refs_1_) | copy-start | bytes 393220
  62.4 12.2 %collective-permute-start.20 = (bf16[128,1024]{1,0:T(8,128)(2,1)S(1)}, bf16[128,1024]{1,0:T(8,128)(2,1)S(1)}, u32[]{:S(2)}, u32[]{:S(2)}) collective-permute-start(bf16[128,1024]{1,0:T(8,128)(2,1)S(1)} %get-tuple-element.76), channel_id=1, source_target_pairs={{0,2},{1,3},{2,0},{3,1},{4,6},{5,7},{6,4},{7,5},{8,10},{9,11},{10,... | collective-permute-start | bytes 786440 | tf_op jit(solution)/shard_map/ppermute | solution.py:251
  62.6 13.5 %collective-permute-start.21 = (bf16[128,1024]{1,0:T(8,128)(2,1)S(1)}, bf16[128,1024]{1,0:T(8,128)(2,1)S(1)}, u32[]{:S(2)}, u32[]{:S(2)}) collective-permute-start(bf16[128,1024]{1,0:T(8,128)(2,1)S(1)} %get-tuple-element.77), channel_id=1, source_target_pairs={{0,3},{1,2},{2,1},{3,0},{4,7},{5,6},{6,5},{7,4},{8,11},{9,10},{10,... | collective-permute-start | bytes 786440 | tf_op jit(solution)/shard_map/ppermute | solution.py:251
  73.0 1.4 %collective-permute-start.18 = (bf16[64,1024]{1,0:T(8,128)(2,1)S(1)}, bf16[64,1024]{1,0:T(8,128)(2,1)S(1)}, u32[]{:S(2)}, u32[]{:S(2)}) collective-permute-start(bf16[64,1024]{1,0:T(8,128)(2,1)S(1)} %get-tuple-element.92), channel_id=1, source_target_pairs={{0,1},{1,0},{2,3},{3,2},{4,5},{5,4},{6,7},{7,6},{8,9},{9,8},{10,11... | collective-permute-start | bytes 393224 | tf_op jit(solution)/shard_map/ppermute | solution.py:251
  73.1 1.5 %collective-permute-start.19 = (bf16[64,1024]{1,0:T(8,128)(2,1)S(1)}, bf16[64,1024]{1,0:T(8,128)(2,1)S(1)}, u32[]{:S(2)}, u32[]{:S(2)}) collective-permute-start(bf16[64,1024]{1,0:T(8,128)(2,1)S(1)} %get-tuple-element.91), channel_id=1, source_target_pairs={{0,1},{1,0},{2,3},{3,2},{4,5},{5,4},{6,7},{7,6},{8,9},{9,8},{10,11... | collective-permute-start | bytes 393224 | tf_op jit(solution)/shard_map/ppermute | solution.py:251
  (1 other events, 1.2 us)

commit v3 on v2

--- a/solution.py
+++ b/solution.py
@@ -212,26 +212,6 @@
     )(place, cos, sin, *hidden, *pieces)
 
 
-def join_kernel(place_ref, *refs):
-    *parts, out_ref = refs
-    for i, part in enumerate(parts):
-        height, width = part.shape
-        row = pl.multiple_of(place_ref[2 * i], height)
-        at = pl.multiple_of(place_ref[2 * i + 1], width)
-        out_ref[pl.ds(row, height), pl.ds(at, width)] = part[...]
-
-
-def join(place, parts, shape):
-    return pl.pallas_call(
-        join_kernel,
-        out_shape=jax.ShapeDtypeStruct(shape, parts[0].dtype),
-        in_specs=[IN_SMEM] + [IN_VMEM] * len(parts),
-        out_specs=IN_VMEM,
-        compiler_params=pltpu.CompilerParams(vmem_limit_bytes=VMEM_LIMIT),
-        name="join",
-    )(place, *parts)
-
-
 def by_planes(hidden, queries, kv_weight, doc_ids):
     rows = hidden.shape[0]
     tokens = doc_ids.shape[0]
@@ -261,7 +241,7 @@
     swap_high = hop(lambda x, z, y, c: (x, z ^ 1, y, c) if z >= 2 else None)
 
     chunk = math.gcd(tokens, 512)
-    tables = [[] for _ in range(7)]
+    tables = [[] for _ in range(6)]
     for i in range(32):
         ix, iz, iy, ic = i // 16, (i // 4) % 4, (i // 2) % 2, i % 2
         blocks = [2 * iy + ic, 2 * iy + 1 - ic, 2 * (1 - iy) + ic, 2 * (1 - iy) + 1 - ic]
@@ -271,7 +251,7 @@
             + [own, ic * width, 1 - own, ic * width, 1, (1 - ic) * width]
         )
         side = (1 - own) * width
-        tables[6].append(
+        tables[5].append(
             [int(iz >= 2), *blocks]
             + [1, side + ix * part, 1, side + (1 - ix) * part]
             + [1, width - side + ix * part, 1, width - side + (1 - ix) * part]
@@ -283,10 +263,6 @@
             first = [(4 * iz + 2 * iy_rows + core) * rows for core in (ic, 1 - ic)]
             kinds = [max(plane, 0) // 2 for plane in some]
             tables[at].append(first + some + kinds)
-        heads = [iy + 2 * ic, iy + 2 * (1 - ic), iy + 2 * (1 - ic)]
-        heads += [1 - iy + 2 * ic, 1 - iy + 2 * (1 - ic)]
-        tops = [0, 0, rows // 2, 0, 0]
-        tables[5].append([v for top, h in zip(tops, heads) for v in (top, h * columns)])
     widths = [len(t[0]) for t in tables]
     whole = np.concatenate([np.asarray(t, np.int32) for t in tables], axis=1)
     place = lax.dynamic_slice_in_dim(jnp.asarray(whole), x * 16 + node, 1, 0)[0]
@@ -330,8 +306,8 @@
 
     plane_hidden = [hidden, hidden_c, hidden_y, hidden_yc]
     kv_a = project(places[0], cos, sin, plane_hidden, [weight, near_0, near_c])
-    kv_a, places[6] = lax.optimization_barrier((kv_a, places[6]))
-    kv_b = project(places[6], cos, sin, plane_hidden, [far_0, far_0x, far_1, far_1x])
+    kv_a, places[5] = lax.optimization_barrier((kv_a, places[5]))
+    kv_b = project(places[5], cos, sin, plane_hidden, [far_0, far_0x, far_1, far_1x])
 
     a_near, a_far = up_near(kv_a), up_far(kv_a)
     b_near, b_far = up_near(kv_b), up_far(kv_b)
@@ -347,8 +323,15 @@
     stored = own + below + other
     across, places[3] = lax.optimization_barrier((across, places[3]))
     here, beside = attend(places[3], starts[1], [q_own, q_core], stored, tokens, chunk)
-    parts = [here, to_core(beside[: rows // 2]), to_core(beside[rows // 2 :])] + back
-    return join(places[5], parts, queries.shape)
+    halves = [to_core(beside[: rows // 2]), to_core(beside[rows // 2 :])]
+    here, halves, back = lax.optimization_barrier((here, halves, back))
+    same_y = [here, jnp.concatenate(halves, axis=0)]
+    heads = []
+    for h in range(KVH):
+        mine = jnp.where(h // 2 == c, same_y[0], same_y[1])
+        other_y = jnp.where(h // 2 == c, back[0], back[1])
+        heads.append(jnp.where(h % 2 == y, mine, other_y))
+    return jnp.concatenate(heads, axis=1)
 
 
 def by_gathers(hidden, queries, kv_weight, doc_ids):

time: 78.6 us -> 77.5 us (0.986)
  Pallas kernels: 22.8 us -> 18.8 us
  local copies, waits for them, and re-layouts: 7.7 us -> 9.15 us
    pallas_call x4, Pallas kernels: 16.2 us -> 13.8 us  [attend(): pl.pallas_call(lambda *refs: attend_kernel(rows, chunk, n_q, n_kv, bool(s...]
    pallas_call x1 -> x0, Pallas kernels: 1.58 us -> none  [join(): pl.pallas_call(join_kernel, out_shape=jax.ShapeDtypeStruct(shape, parts[0...]
    dynamic_slice x1, local copies, waits for them, and re-layouts: 0.91 us -> 2.21 us  [by_planes(): lax.dynamic_slice_in_dim(queries, h * columns, columns, 1)]
    concatenate x0 -> x1, other arithmetic: none -> 1.04 us  [by_planes(): return jnp.concatenate(heads, axis=1)]
    concatenate x4, other arithmetic: 3.3 us -> 2.47 us  [by_planes(): places[at] = jnp.concatenate([places[at], lowest[low]])]
  transfers between devices with their start and end apart: 22 -> 22, of which waited for: 10 -> 10; matrix products, arithmetic and copies ran while one was open for 18% -> 19% of each run, Pallas kernels for 24% -> 23%
where the time goes in v3:
time: 77.5 us; the launch traced here: 76.2 us
  starting transfers between devices  22.1 us (29%)
  Pallas kernels  18.8 us (24%)
  waiting for transfers between devices  17.5 us (23%)
  local copies, waits for them, and re-layouts  9.15 us (12%)
  other arithmetic  8.39 us (11%)
    ppermute x22, starting transfers between devices, hop(): return lambda v: lax.ppermute(v, AXES, pairs)  22.1 us
    ppermute x22, waiting for transfers between devices, hop(): return lambda v: lax.ppermute(v, AXES, pairs)  17.5 us
    pallas_call x4, Pallas kernels, attend(): pl.pallas_call(lambda *refs: attend_kernel(rows, chunk, n_q, n_kv, bool(s...  13.8 us
    pallas_call x2, Pallas kernels, project(): pl.pallas_call(lambda *refs: project_kernel(rows, n, len(pieces), *refs),...  5.01 us
    concatenate x4, other arithmetic, by_planes(): places[at] = jnp.concatenate([places[at], lowest[low]])  2.47 us
    dynamic_slice x1, local copies, waits for them, and re-layouts, by_planes(): lax.dynamic_slice_in_dim(queries, h * columns, columns, 1)  2.21 us
    broadcast_in_dim x2, local copies, waits for them, and re-layouts, attend_starts(): jnp.broadcast_to(starts[:, None], (starts.shape[0], HD))  2.19 us
    dynamic_slice x1, local copies, waits for them, and re-layouts, by_planes(): far_0 = far(lax.dynamic_slice_in_dim(weight, x * part, part, 0))  1.67 us
  transfers between devices with their start and end apart: 22, of which 10 were waited for; matrix products, arithmetic and copies ran while one was open for 19% of the time, Pallas kernels for 23%

profile of v3, /device:TPU:29, one launch (start us, length us, event | category | flops | bytes accessed | tf_op | source)
XLA Modules:
  0.0 76.2 jit_solution(12057047991186278591)
XLA Ops:
  0.0 1.7 %dynamic-slice_bitcast_fusion = bf16[32,4096]{1,0:T(8,128)(2,1)} fusion(bf16[4096,64]{0,1:T(8,128)(2,1)} %param.7, s32[]{:T(128)S(6)} %select_n.115), kind=kLoop, calls=%fused_computation.8 | loop fusion | bytes 524292 | tf_op jit(solution)/shard_map/dynamic_slice | solution.py:275
  4.6 1.2 %convert_reduce_fusion = (s32[256]{0:T(256)S(1)}, s32[256]{0:T(256)S(1)}) fusion(s32[2048]{0:T(1024)} %param.8, s32[256]{0:T(256)S(1)} %get-tuple-element.115, s32[256]{0:T(256)S(1)} %get-tuple-element.114), kind=kLoop, calls=%fused_computation | loop fusion | flops 3145216 | bytes 12288 | tf_op jit(solution)/shard_map/reduce_sum | solution.py:136
  7.7 1.0 %fusion = (f32[512,64]{1,0:T(8,128)S(1)}, f32[512,64]{1,0:T(8,128)S(1)}, f32[512,64]{1,0:T(8,128)S(1)}) fusion(f32[64]{0:T(128)S(1)} %multiply_power_fusion, f32[512]{0:T(512)S(1)} %add_convert_fusion), kind=kLoop, calls=%fused_computation.17 | loop fusion | flops 65536 | bytes 395520 | tf_op jit(solution)/shard_map/neg | solution.py:283
  8.9 2.2 %constant_dynamic-slice_fusion = (bf16[128,1024]{1,0:T(8,128)(2,1)}, bf16[128,1024]{1,0:T(8,128)(2,1)}, bf16[128,1024]{1,0:T(8,128)(2,1)S(1)}, bf16[128,1024]{1,0:T(8,128)(2,1)}) fusion(bf16[128,4096]{1,0:T(8,128)(2,1)} %param.6, s32[]{:T(128)S(6)} %select_n.125, s32[]{:T(128)S(6)} %select_n.123, s32[]{:T(128)S(6)} %select_n.122, s32[]{:T(128)S(6)} %select_n.124), kind=kLoop, calls=%fused_computation.21 | loop fusion | bytes 2097168 | tf_op jit(solution)/shard_map/dynamic_slice | solution.py:292
  14.3 1.3 %collective-permute-done.refs_7_ = bf16[32,4096]{1,0:T(8,128)(2,1)} collective-permute-done((bf16[32,4096]{1,0:T(8,128)(2,1)}, bf16[32,4096]{1,0:T(8,128)(2,1)}, u32[]{:S(2)}, u32[]{:S(2)}) %collective-permute-start) | collective-permute-done | bytes 262176 | tf_op jit(solution)/shard_map/ppermute | solution.py:231
  16.4 1.4 %broadcast_in_dim.9.refs_1_ = s32[256,128]{1,0:T(8,128)} broadcast(s32[256]{0:T(256)} %copy-done.7), dimensions={0} | broadcast | bytes 132096 | tf_op jit(solution)/shard_map/broadcast_in_dim | solution.py:137
  17.8 1.2 %collective-permute-start.3 = (bf16[32,4096]{1,0:T(8,128)(2,1)}, bf16[32,4096]{1,0:T(8,128)(2,1)}, u32[]{:S(2)}, u32[]{:S(2)}) collective-permute-start(bf16[32,4096]{1,0:T(8,128)(2,1)} %collective-permute-done.refs_7_), channel_id=1, source_target_pairs={{0,16},{1,17},{2,18},{3,19},{4,20},{5,21},{6,22},{7,23},{8,24},{9,... | collective-permute-start | bytes 786440 | tf_op jit(solution)/shard_map/ppermute | solution.py:231
  19.0 1.0 %collective-permute-start.4 = (bf16[128,1024]{1,0:T(8,128)(2,1)}, bf16[128,1024]{1,0:T(8,128)(2,1)}, u32[]{:S(2)}, u32[]{:S(2)}) collective-permute-start(bf16[128,1024]{1,0:T(8,128)(2,1)} %get-tuple-element.53), channel_id=1, source_target_pairs={{0,1},{1,0},{2,3},{3,2},{4,5},{5,4},{6,7},{7,6},{8,9},{9,8},{10,11... | collective-permute-start | bytes 786440 | tf_op jit(solution)/shard_map/ppermute | solution.py:231
  20.0 6.4 %collective-permute-done.2.refs_9_ = bf16[32,4096]{1,0:T(8,128)(2,1)} collective-permute-done((bf16[32,4096]{1,0:T(8,128)(2,1)}, bf16[32,4096]{1,0:T(8,128)(2,1)}, u32[]{:S(2)}, u32[]{:S(2)}) %collective-permute-start.2) | collective-permute-done | bytes 262176 | tf_op jit(solution)/shard_map/ppermute | solution.py:231
  26.5 1.3 %collective-permute-start.7 = (bf16[128,4096]{1,0:T(8,128)(2,1)S(1)}, bf16[128,4096]{1,0:T(8,128)(2,1)S(1)}, u32[]{:S(2)}, u32[]{:S(2)}) collective-permute-start(bf16[128,4096]{1,0:T(8,128)(2,1)S(1)} %copy-done), channel_id=1, source_target_pairs={{0,1},{1,0},{2,3},{3,2},{4,5},{5,4},{6,7},{7,6},{8,9},{9,8},{10,11... | collective-permute-start | bytes 3145736 | tf_op jit(solution)/shard_map/ppermute | solution.py:231
  27.9 1.1 %broadcast_select_fusion = bf16[64,4096]{1,0:T(8,128)(2,1)S(1)} fusion(bf16[64,4096]{1,0:T(8,128)(2,1)} %collective-permute-done.9.refs_8_, pred[]{:T(512)S(6)} %eq.29, bf16[4096,64]{0,1:T(8,128)(2,1)S(1)} %copy-done.1), kind=kLoop, calls=%fused_computation.3 | loop fusion | flops 262144 | bytes 1572865 | tf_op jit(solution)/shard_map/jit(_where)/select_n | solution.py:301
  29.1 1.3 %collective-permute-start.11 = (bf16[32,4096]{1,0:T(8,128)(2,1)}, bf16[32,4096]{1,0:T(8,128)(2,1)S(1)}, u32[]{:S(2)}, u32[]{:S(2)}) collective-permute-start(bf16[32,4096]{1,0:T(8,128)(2,1)} %collective-permute-done.2.refs_9_), channel_id=1, source_target_pairs={{0,16},{1,17},{2,18},{3,19},{4,20},{5,21},{6,22},{7,23},{8,24},{9,... | collective-permute-start | bytes 786440 | tf_op jit(solution)/shard_map/ppermute | solution.py:231
  30.4 1.2 %collective-permute-start.5 = (bf16[128,1024]{1,0:T(8,128)(2,1)S(1)}, bf16[128,1024]{1,0:T(8,128)(2,1)S(1)}, u32[]{:S(2)}, u32[]{:S(2)}) collective-permute-start(bf16[128,1024]{1,0:T(8,128)(2,1)S(1)} %copy-done.6), channel_id=1, source_target_pairs={{0,2},{1,3},{2,0},{3,1},{4,6},{5,7},{6,4},{7,5},{8,10},{9,11},{10,... | collective-permute-start | bytes 786440 | tf_op jit(solution)/shard_map/ppermute | solution.py:231
  32.3 1.5 %collective-permute-start.6 = (bf16[128,1024]{1,0:T(8,128)(2,1)S(1)}, bf16[128,1024]{1,0:T(8,128)(2,1)S(1)}, u32[]{:S(2)}, u32[]{:S(2)}) collective-permute-start(bf16[128,1024]{1,0:T(8,128)(2,1)S(1)} %copy-done.5), channel_id=1, source_target_pairs={{0,3},{1,2},{2,1},{3,0},{4,7},{5,6},{6,5},{7,4},{8,11},{9,10},{10,... | collective-permute-start | bytes 786440 | tf_op jit(solution)/shard_map/ppermute | solution.py:231
  33.8 2.5 %project.2.refs_4_ = bf16[512,128]{1,0:T(8,128)(2,1)S(1)} custom-call(s32[11]{0:T(128)S(1)} %copy-done.4, f32[512,128]{1,0:T(8,128)S(1)} %get-tuple-element.60.refs_1_, f32[512,128]{1,0:T(8,128)S(1)} %get-tuple-element.61.refs_2_, bf16[128,4096]{1,0:T(8,128)(2,1)S(1)} %copy-done, bf16[128,4096]{1,0:T(8,128)(2,1)S(1)} %collective-permute-done.7.refs_4_, ...), custom_call_target="tpu_custom_call" | custom-call | flops 67108864 | bytes 524288 | tf_op jit(solution)/shard_map/project/pallas_call | solution.py:199
  36.3 1.3 %collective-permute-start.12 = (bf16[512,128]{1,0:T(8,128)(2,1)S(1)}, bf16[512,128]{1,0:T(8,128)(2,1)S(1)}, u32[]{:S(2)}, u32[]{:S(2)}) collective-permute-start(bf16[512,128]{1,0:T(8,128)(2,1)S(1)} %project.2.refs_4_), channel_id=1, source_target_pairs={{0,8},{1,9},{2,10},{3,11},{4,12},{5,13},{6,14},{7,15},{16,24},{17,... | collective-permute-start | bytes 393224 | tf_op jit(solution)/shard_map/ppermute | solution.py:231
  37.6 2.5 %project.3.refs_5_ = bf16[512,128]{1,0:T(8,128)(2,1)S(1)} custom-call(s32[13]{0:T(128)S(1)} %copy-done.3, f32[512,128]{1,0:T(8,128)S(1)} %get-tuple-element.60.refs_1_, f32[512,128]{1,0:T(8,128)S(1)} %get-tuple-element.61.refs_2_, bf16[128,4096]{1,0:T(8,128)(2,1)S(1)} %copy-done, bf16[128,4096]{1,0:T(8,128)(2,1)S(1)} %collective-permute-done.7.refs_4_, ...), custom_call_target="tpu_custom_call" | custom-call | flops 67108864 | bytes 524288 | tf_op jit(solution)/shard_map/project/pallas_call | solution.py:199
  40.2 1.3 %collective-permute-start.14 = (bf16[512,128]{1,0:T(8,128)(2,1)S(1)}, bf16[512,128]{1,0:T(8,128)(2,1)S(1)}, u32[]{:S(2)}, u32[]{:S(2)}) collective-permute-start(bf16[512,128]{1,0:T(8,128)(2,1)S(1)} %project.3.refs_5_), channel_id=1, source_target_pairs={{0,8},{1,9},{2,10},{3,11},{4,12},{5,13},{6,14},{7,15},{16,24},{17,... | collective-permute-start | bytes 393224 | tf_op jit(solution)/shard_map/ppermute | solution.py:231
  41.5 1.3 %collective-permute-start.17 = (bf16[512,128]{1,0:T(8,128)(2,1)S(1)}, bf16[512,128]{1,0:T(8,128)(2,1)S(1)}, u32[]{:S(2)}, u32[]{:S(2)}) collective-permute-start(bf16[512,128]{1,0:T(8,128)(2,1)S(1)} %project.3.refs_5_), channel_id=1, source_target_pairs={{0,4},{1,5},{2,6},{3,7},{8,12},{9,13},{10,14},{11,15},{16,20},{17,... | collective-permute-start | bytes 393224 | tf_op jit(solution)/shard_map/ppermute | solution.py:231
  42.8 1.3 %collective-permute-start.16 = (bf16[512,128]{1,0:T(8,128)(2,1)S(1)}, bf16[512,128]{1,0:T(8,128)(2,1)S(1)}, u32[]{:S(2)}, u32[]{:S(2)}) collective-permute-start(bf16[512,128]{1,0:T(8,128)(2,1)S(1)} %project.2.refs_4_), channel_id=1, source_target_pairs={{0,4},{1,5},{2,6},{3,7},{8,12},{9,13},{10,14},{11,15},{16,20},{17,... | collective-permute-start | bytes 393224 | tf_op jit(solution)/shard_map/ppermute | solution.py:231
  44.3 1.9 %attend.4 = (f32[2048,128]{1,0:T(8,128)S(1)}, f32[2048,128]{1,0:T(8,128)S(1)}, f32[2048,128]{1,0:T(8,128)S(1)}) custom-call(s32[5]{0:T(128)S(1)} %pad_add_fusion.2.refs_0_, s32[256,128]{1,0:T(8,128)S(1)} %broadcast_in_dim.8.refs_1_, bf16[128,1024]{1,0:T(8,128)(2,1)S(1)} %collective-permute-done.5.refs_2_, ...), custom_call_target="tpu_custom_call" | custom-call | flops 67108864 | bytes 524288 | tf_op jit(solution)/shard_map/attend/pallas_call | solution.py:149
  46.2 3.0 %collective-permute-done.12.refs_6_.refs_8_ = bf16[512,128]{1,0:T(8,128)(2,1)S(1)} collective-permute-done((bf16[512,128]{1,0:T(8,128)(2,1)S(1)}, bf16[512,128]{1,0:T(8,128)(2,1)S(1)}, u32[]{:S(2)}, u32[]{:S(2)}) %collective-permute-start.12) | collective-permute-done | bytes 131104 | tf_op jit(solution)/shard_map/ppermute | solution.py:231
  49.2 1.9 %collective-permute-start.13 = (bf16[512,128]{1,0:T(8,128)(2,1)S(1)}, bf16[512,128]{1,0:T(8,128)(2,1)S(1)}, u32[]{:S(2)}, u32[]{:S(2)}) collective-permute-start(bf16[512,128]{1,0:T(8,128)(2,1)S(1)} %collective-permute-done.12.refs_6_.refs_8_), channel_id=1, source_target_pairs={{8,12},{9,13},{10,14},{11,15},{12,8},{13,9},{14,10},{15,11},{24,28... | collective-permute-start | bytes 393224 | tf_op jit(solution)/shard_map/ppermute | solution.py:231
  51.1 0.9 %collective-permute-done.14.refs_7_.refs_9_ = bf16[512,128]{1,0:T(8,128)(2,1)S(1)} collective-permute-done((bf16[512,128]{1,0:T(8,128)(2,1)S(1)}, bf16[512,128]{1,0:T(8,128)(2,1)S(1)}, u32[]{:S(2)}, u32[]{:S(2)}) %collective-permute-start.14) | collective-permute-done | bytes 131104 | tf_op jit(solution)/shard_map/ppermute | solution.py:231
  52.0 2.6 %collective-permute-start.15 = (bf16[512,128]{1,0:T(8,128)(2,1)S(1)}, bf16[512,128]{1,0:T(8,128)(2,1)S(1)}, u32[]{:S(2)}, u32[]{:S(2)}) collective-permute-start(bf16[512,128]{1,0:T(8,128)(2,1)S(1)} %collective-permute-done.14.refs_7_.refs_9_), channel_id=1, source_target_pairs={{8,12},{9,13},{10,14},{11,15},{12,8},{13,9},{14,10},{15,11},{24,28... | collective-permute-start | bytes 393224 | tf_op jit(solution)/shard_map/ppermute | solution.py:231
  54.7 4.1 %attend.5 = (f32[2048,128]{1,0:T(8,128)S(1)}, f32[2048,128]{1,0:T(8,128)S(1)}, f32[2048,128]{1,0:T(8,128)S(1)}) custom-call(s32[7]{0:T(128)S(1)} %pad_add_fusion.5.refs_0_, s32[256,128]{1,0:T(8,128)S(1)} %broadcast_in_dim.8.refs_1_, bf16[128,1024]{1,0:T(8,128)(2,1)S(1)} %collective-permute-done.5.refs_2_, ...), custom_call_target="tpu_custom_call" | custom-call | flops 67108864 | bytes 524288 | tf_op jit(solution)/shard_map/attend/pallas_call | solution.py:149
  58.8 1.3 %collective-permute-done.15.refs_5_.refs_11_ = bf16[512,128]{1,0:T(8,128)(2,1)S(1)} collective-permute-done((bf16[512,128]{1,0:T(8,128)(2,1)S(1)}, bf16[512,128]{1,0:T(8,128)(2,1)S(1)}, u32[]{:S(2)}, u32[]{:S(2)}) %collective-permute-start.15) | collective-permute-done | bytes 131104 | tf_op jit(solution)/shard_map/ppermute | solution.py:231
  60.1 1.2 %attend.6 = (bf16[128,1024]{1,0:T(8,128)(2,1)S(1)}, bf16[128,1024]{1,0:T(8,128)(2,1)S(1)}) custom-call(s32[5]{0:T(128)S(1)} %pad_add_fusion.3.refs_0_, s32[256,128]{1,0:T(8,128)S(1)} %broadcast_in_dim.8.refs_1_, bf16[128,1024]{1,0:T(8,128)(2,1)S(1)} %collective-permute-done.5.refs_2_, bf16[128,1024]{1,0:T(8,128)(2,1)S(1)} %collective-permute-done.6.refs_3_, ...), custom_call_target="tpu_custom_call" | custom-call | flops 67108864 | bytes 524288 | tf_op jit(solution)/shard_map/attend/pallas_call | solution.py:149
  61.5 2.8 %collective-permute-start.21 = (bf16[128,1024]{1,0:T(8,128)(2,1)S(1)}, bf16[128,1024]{1,0:T(8,128)(2,1)S(1)}, u32[]{:S(2)}, u32[]{:S(2)}) collective-permute-start(bf16[128,1024]{1,0:T(8,128)(2,1)S(1)} %get-tuple-element.80), channel_id=1, source_target_pairs={{0,3},{1,2},{2,1},{3,0},{4,7},{5,6},{6,5},{7,4},{8,11},{9,10},{10,... | collective-permute-start | bytes 786440 | tf_op jit(solution)/shard_map/ppermute | solution.py:231
  64.3 6.6 %attend.7 = (bf16[128,1024]{1,0:T(8,128)(2,1)S(1)}, bf16[128,1024]{1,0:T(8,128)(2,1)S(1)}) custom-call(s32[11]{0:T(128)S(1)} %pad_add_fusion.4.refs_0_, s32[256,128]{1,0:T(8,128)S(1)} %copy-done.2, bf16[128,1024]{1,0:T(8,128)(2,1)S(1)} %get-tuple-element.84.refs_2_, bf16[128,1024]{1,0:T(8,128)(2,1)} %collective-permute-done.4.refs_3_, ...), custom_call_target="tpu_custom_call" | custom-call | flops 67108864 | bytes 524288 | tf_op jit(solution)/shard_map/attend/pallas_call | solution.py:149
  72.5 2.5 %collective-permute-done.21 = bf16[128,1024]{1,0:T(8,128)(2,1)S(1)} collective-permute-done((bf16[128,1024]{1,0:T(8,128)(2,1)S(1)}, bf16[128,1024]{1,0:T(8,128)(2,1)S(1)}, u32[]{:S(2)}, u32[]{:S(2)}) %collective-permute-start.21) | collective-permute-done | bytes 262176 | tf_op jit(solution)/shard_map/ppermute | solution.py:231
  75.2 1.0 %pad_maximum_fusion = bf16[128,4096]{1,0:T(8,128)(2,1)} fusion(bf16[128,1024]{1,0:T(8,128)(2,1)S(1)} %get-tuple-element.96, bf16[128,1024]{1,0:T(8,128)(2,1)S(1)} %get-tuple-element.98, bf16[128,1024]{1,0:T(8,128)(2,1)S(1)} %get-tuple-element.97, bf16[128,1024]{1,0:T(8,128)(2,1)S(1)} %get-tuple-element.95), kind=kLoop, calls=%fused_computation.2 | loop fusion | flops 4194304 | bytes 2097152 | tf_op jit(solution)/shard_map/concatenate | solution.py:334
  (65 shorter events, 11.9 us)
Async XLA Ops:
  1.7 13.9 %collective-permute-start = (bf16[32,4096]{1,0:T(8,128)(2,1)}, bf16[32,4096]{1,0:T(8,128)(2,1)}, u32[]{:S(2)}, u32[]{:S(2)}) collective-permute-start(bf16[32,4096]{1,0:T(8,128)(2,1)} %dynamic-slice_bitcast_fusion), channel_id=1, source_target_pairs={{0,8},{1,12},{2,10},{3,14},{4,13},{5,9},{6,15},{7,11},{8,0},{9,4},... | collective-permute-start | bytes 786440 | tf_op jit(solution)/shard_map/ppermute | solution.py:231
  1.7 26.1 %collective-permute-start.1 = (bf16[128,4096]{1,0:T(8,128)(2,1)}, bf16[128,4096]{1,0:T(8,128)(2,1)S(1)}, u32[]{:S(2)}, u32[]{:S(2)}) collective-permute-start(bf16[128,4096]{1,0:T(8,128)(2,1)} %refs_3_.3), channel_id=1, source_target_pairs={{0,2},{1,3},{2,0},{3,1},{4,6},{5,7},{6,4},{7,5},{8,10},{9,11},{10,... | collective-permute-start | bytes 3145736 | tf_op jit(solution)/shard_map/ppermute | solution.py:231
  1.9 26.0 %collective-permute-start.9 = (bf16[64,4096]{1,0:T(8,128)(2,1)}, bf16[64,4096]{1,0:T(8,128)(2,1)}, u32[]{:S(2)}, u32[]{:S(2)}) collective-permute-start(bf16[64,4096]{1,0:T(8,128)(2,1)} %bitcast.18), channel_id=1, source_target_pairs={{0,4},{1,5},{2,6},{3,7},{4,0},{5,1},{6,2},{7,3},{8,12},{9,13},{10,... | collective-permute-start | bytes 1572872 | tf_op jit(solution)/shard_map/ppermute | solution.py:231
  5.8 1.2 %copy-start.8 = (s32[256]{0:T(256)}, s32[256]{0:T(256)S(1)}, u32[]{:S(2)}) copy-start(s32[256]{0:T(256)S(1)} %get-tuple-element.94) | copy-start | bytes 3076
  5.8 5.9 %copy-start.7 = (s32[256]{0:T(256)}, s32[256]{0:T(256)S(1)}, u32[]{:S(2)}) copy-start(s32[256]{0:T(256)S(1)} %get-tuple-element.93) | copy-start | bytes 3076
  8.9 17.6 %copy-start = (bf16[128,4096]{1,0:T(8,128)(2,1)S(1)}, bf16[128,4096]{1,0:T(8,128)(2,1)}, u32[]{:S(2)}) copy-start(bf16[128,4096]{1,0:T(8,128)(2,1)} %refs_3_.3) | copy-start | bytes 3145732
  8.9 19.0 %copy-start.1 = (bf16[4096,64]{0,1:T(8,128)(2,1)S(1)}, bf16[4096,64]{0,1:T(8,128)(2,1)}, u32[]{:S(2)}) copy-start(bf16[4096,64]{0,1:T(8,128)(2,1)} %param.7) | copy-start | bytes 1572868
  17.8 8.7 %collective-permute-start.2 = (bf16[32,4096]{1,0:T(8,128)(2,1)}, bf16[32,4096]{1,0:T(8,128)(2,1)}, u32[]{:S(2)}, u32[]{:S(2)}) collective-permute-start(bf16[32,4096]{1,0:T(8,128)(2,1)} %collective-permute-done.refs_7_), channel_id=1, source_target_pairs={{0,4},{1,5},{2,6},{3,7},{4,0},{5,1},{6,2},{7,3},{8,12},{9,13},{10,... | collective-permute-start | bytes 786440 | tf_op jit(solution)/shard_map/ppermute | solution.py:231
  17.8 10.0 %collective-permute-start.3 = (bf16[32,4096]{1,0:T(8,128)(2,1)}, bf16[32,4096]{1,0:T(8,128)(2,1)}, u32[]{:S(2)}, u32[]{:S(2)}) collective-permute-start(bf16[32,4096]{1,0:T(8,128)(2,1)} %collective-permute-done.refs_7_), channel_id=1, source_target_pairs={{0,16},{1,17},{2,18},{3,19},{4,20},{5,21},{6,22},{7,23},{8,24},{9,... | collective-permute-start | bytes 786440 | tf_op jit(solution)/shard_map/ppermute | solution.py:231
  19.0 8.8 %collective-permute-start.4 = (bf16[128,1024]{1,0:T(8,128)(2,1)}, bf16[128,1024]{1,0:T(8,128)(2,1)}, u32[]{:S(2)}, u32[]{:S(2)}) collective-permute-start(bf16[128,1024]{1,0:T(8,128)(2,1)} %get-tuple-element.53), channel_id=1, source_target_pairs={{0,1},{1,0},{2,3},{3,2},{4,5},{5,4},{6,7},{7,6},{8,9},{9,8},{10,11... | collective-permute-start | bytes 786440 | tf_op jit(solution)/shard_map/ppermute | solution.py:231
  20.0 10.4 %copy-start.6 = (bf16[128,1024]{1,0:T(8,128)(2,1)S(1)}, bf16[128,1024]{1,0:T(8,128)(2,1)}, u32[]{:S(2)}) copy-start(bf16[128,1024]{1,0:T(8,128)(2,1)} %get-tuple-element.56) | copy-start | bytes 786436
  20.0 12.3 %copy-start.5 = (bf16[128,1024]{1,0:T(8,128)(2,1)S(1)}, bf16[128,1024]{1,0:T(8,128)(2,1)}, u32[]{:S(2)}) copy-start(bf16[128,1024]{1,0:T(8,128)(2,1)} %get-tuple-element.57) | copy-start | bytes 786436
  20.0 13.8 %copy-start.4 = (s32[11]{0:T(128)S(1)}, s32[11]{0:T(128)}, u32[]{:S(2)}) copy-start(s32[11]{0:T(128)} %slice_bitcast_fusion.5.refs_0_) | copy-start | bytes 136
  26.5 7.4 %collective-permute-start.7 = (bf16[128,4096]{1,0:T(8,128)(2,1)S(1)}, bf16[128,4096]{1,0:T(8,128)(2,1)S(1)}, u32[]{:S(2)}, u32[]{:S(2)}) collective-permute-start(bf16[128,4096]{1,0:T(8,128)(2,1)S(1)} %copy-done), channel_id=1, source_target_pairs={{0,1},{1,0},{2,3},{3,2},{4,5},{5,4},{6,7},{7,6},{8,9},{9,8},{10,11... | collective-permute-start | bytes 3145736 | tf_op jit(solution)/shard_map/ppermute | solution.py:231
  27.8 6.0 %collective-permute-start.8 = (bf16[128,4096]{1,0:T(8,128)(2,1)S(1)}, bf16[128,4096]{1,0:T(8,128)(2,1)S(1)}, u32[]{:S(2)}, u32[]{:S(2)}) collective-permute-start(bf16[128,4096]{1,0:T(8,128)(2,1)S(1)} %collective-permute-done.1.refs_5_), channel_id=1, source_target_pairs={{0,1},{1,0},{2,3},{3,2},{4,5},{5,4},{6,7},{7,6},{8,9},{9,8},{10,11... | collective-permute-start | bytes 3145736 | tf_op jit(solution)/shard_map/ppermute | solution.py:231
  29.0 8.6 %copy-start.3 = (s32[13]{0:T(128)S(1)}, s32[13]{0:T(128)}, u32[]{:S(2)}) copy-start(s32[13]{0:T(128)} %slice_bitcast_fusion.refs_0_) | copy-start | bytes 160
  29.0 3.3 %collective-permute-start.10 = (bf16[64,4096]{1,0:T(8,128)(2,1)S(1)}, bf16[64,4096]{1,0:T(8,128)(2,1)S(1)}, u32[]{:S(2)}, u32[]{:S(2)}) collective-permute-start(bf16[64,4096]{1,0:T(8,128)(2,1)S(1)} %broadcast_select_fusion), channel_id=1, source_target_pairs={{0,1},{1,0},{2,3},{3,2},{4,5},{5,4},{6,7},{7,6},{8,9},{9,8},{10,11... | collective-permute-start | bytes 1572872 | tf_op jit(solution)/shard_map/ppermute | solution.py:231
  29.1 8.5 %collective-permute-start.11 = (bf16[32,4096]{1,0:T(8,128)(2,1)}, bf16[32,4096]{1,0:T(8,128)(2,1)S(1)}, u32[]{:S(2)}, u32[]{:S(2)}) collective-permute-start(bf16[32,4096]{1,0:T(8,128)(2,1)} %collective-permute-done.2.refs_9_), channel_id=1, source_target_pairs={{0,16},{1,17},{2,18},{3,19},{4,20},{5,21},{6,22},{7,23},{8,24},{9,... | collective-permute-start | bytes 786440 | tf_op jit(solution)/shard_map/ppermute | solution.py:231
  30.4 12.4 %collective-permute-start.5 = (bf16[128,1024]{1,0:T(8,128)(2,1)S(1)}, bf16[128,1024]{1,0:T(8,128)(2,1)S(1)}, u32[]{:S(2)}, u32[]{:S(2)}) collective-permute-start(bf16[128,1024]{1,0:T(8,128)(2,1)S(1)} %copy-done.6), channel_id=1, source_target_pairs={{0,2},{1,3},{2,0},{3,1},{4,6},{5,7},{6,4},{7,5},{8,10},{9,11},{10,... | collective-permute-start | bytes 786440 | tf_op jit(solution)/shard_map/ppermute | solution.py:231
  32.3 12.0 %collective-permute-start.6 = (bf16[128,1024]{1,0:T(8,128)(2,1)S(1)}, bf16[128,1024]{1,0:T(8,128)(2,1)S(1)}, u32[]{:S(2)}, u32[]{:S(2)}) collective-permute-start(bf16[128,1024]{1,0:T(8,128)(2,1)S(1)} %copy-done.5), channel_id=1, source_target_pairs={{0,3},{1,2},{2,1},{3,0},{4,7},{5,6},{6,5},{7,4},{8,11},{9,10},{10,... | collective-permute-start | bytes 786440 | tf_op jit(solution)/shard_map/ppermute | solution.py:231
  36.3 12.8 %collective-permute-start.12 = (bf16[512,128]{1,0:T(8,128)(2,1)S(1)}, bf16[512,128]{1,0:T(8,128)(2,1)S(1)}, u32[]{:S(2)}, u32[]{:S(2)}) collective-permute-start(bf16[512,128]{1,0:T(8,128)(2,1)S(1)} %project.2.refs_4_), channel_id=1, source_target_pairs={{0,8},{1,9},{2,10},{3,11},{4,12},{5,13},{6,14},{7,15},{16,24},{17,... | collective-permute-start | bytes 393224 | tf_op jit(solution)/shard_map/ppermute | solution.py:231
  40.2 11.8 %collective-permute-start.14 = (bf16[512,128]{1,0:T(8,128)(2,1)S(1)}, bf16[512,128]{1,0:T(8,128)(2,1)S(1)}, u32[]{:S(2)}, u32[]{:S(2)}) collective-permute-start(bf16[512,128]{1,0:T(8,128)(2,1)S(1)} %project.3.refs_5_), channel_id=1, source_target_pairs={{0,8},{1,9},{2,10},{3,11},{4,12},{5,13},{6,14},{7,15},{16,24},{17,... | collective-permute-start | bytes 393224 | tf_op jit(solution)/shard_map/ppermute | solution.py:231
  41.5 13.2 %collective-permute-start.17 = (bf16[512,128]{1,0:T(8,128)(2,1)S(1)}, bf16[512,128]{1,0:T(8,128)(2,1)S(1)}, u32[]{:S(2)}, u32[]{:S(2)}) collective-permute-start(bf16[512,128]{1,0:T(8,128)(2,1)S(1)} %project.3.refs_5_), channel_id=1, source_target_pairs={{0,4},{1,5},{2,6},{3,7},{8,12},{9,13},{10,14},{11,15},{16,20},{17,... | collective-permute-start | bytes 393224 | tf_op jit(solution)/shard_map/ppermute | solution.py:231
  42.8 11.9 %collective-permute-start.16 = (bf16[512,128]{1,0:T(8,128)(2,1)S(1)}, bf16[512,128]{1,0:T(8,128)(2,1)S(1)}, u32[]{:S(2)}, u32[]{:S(2)}) collective-permute-start(bf16[512,128]{1,0:T(8,128)(2,1)S(1)} %project.2.refs_4_), channel_id=1, source_target_pairs={{0,4},{1,5},{2,6},{3,7},{8,12},{9,13},{10,14},{11,15},{16,20},{17,... | collective-permute-start | bytes 393224 | tf_op jit(solution)/shard_map/ppermute | solution.py:231
  49.2 9.6 %collective-permute-start.13 = (bf16[512,128]{1,0:T(8,128)(2,1)S(1)}, bf16[512,128]{1,0:T(8,128)(2,1)S(1)}, u32[]{:S(2)}, u32[]{:S(2)}) collective-permute-start(bf16[512,128]{1,0:T(8,128)(2,1)S(1)} %collective-permute-done.12.refs_6_.refs_8_), channel_id=1, source_target_pairs={{8,12},{9,13},{10,14},{11,15},{12,8},{13,9},{14,10},{15,11},{24,28... | collective-permute-start | bytes 393224 | tf_op jit(solution)/shard_map/ppermute | solution.py:231
  52.0 8.1 %collective-permute-start.15 = (bf16[512,128]{1,0:T(8,128)(2,1)S(1)}, bf16[512,128]{1,0:T(8,128)(2,1)S(1)}, u32[]{:S(2)}, u32[]{:S(2)}) collective-permute-start(bf16[512,128]{1,0:T(8,128)(2,1)S(1)} %collective-permute-done.14.refs_7_.refs_9_), channel_id=1, source_target_pairs={{8,12},{9,13},{10,14},{11,15},{12,8},{13,9},{14,10},{15,11},{24,28... | collective-permute-start | bytes 393224 | tf_op jit(solution)/shard_map/ppermute | solution.py:231
  60.1 4.2 %copy-start.2 = (s32[256,128]{1,0:T(8,128)S(1)}, s32[256,128]{1,0:T(8,128)}, u32[]{:S(2)}) copy-start(s32[256,128]{1,0:T(8,128)} %broadcast_in_dim.9.refs_1_) | copy-start | bytes 393220
  61.3 11.2 %collective-permute-start.20 = (bf16[128,1024]{1,0:T(8,128)(2,1)S(1)}, bf16[128,1024]{1,0:T(8,128)(2,1)S(1)}, u32[]{:S(2)}, u32[]{:S(2)}) collective-permute-start(bf16[128,1024]{1,0:T(8,128)(2,1)S(1)} %get-tuple-element.79), channel_id=1, source_target_pairs={{0,2},{1,3},{2,0},{3,1},{4,6},{5,7},{6,4},{7,5},{8,10},{9,11},{10,... | collective-permute-start | bytes 786440 | tf_op jit(solution)/shard_map/ppermute | solution.py:231
  61.5 13.5 %collective-permute-start.21 = (bf16[128,1024]{1,0:T(8,128)(2,1)S(1)}, bf16[128,1024]{1,0:T(8,128)(2,1)S(1)}, u32[]{:S(2)}, u32[]{:S(2)}) collective-permute-start(bf16[128,1024]{1,0:T(8,128)(2,1)S(1)} %get-tuple-element.80), channel_id=1, source_target_pairs={{0,3},{1,2},{2,1},{3,0},{4,7},{5,6},{6,5},{7,4},{8,11},{9,10},{10,... | collective-permute-start | bytes 786440 | tf_op jit(solution)/shard_map/ppermute | solution.py:231
  70.9 1.4 %collective-permute-start.18 = (bf16[64,1024]{1,0:T(8,128)(2,1)S(1)}, bf16[64,1024]{1,0:T(8,128)(2,1)S(1)}, u32[]{:S(2)}, u32[]{:S(2)}) collective-permute-start(bf16[64,1024]{1,0:T(8,128)(2,1)S(1)} %get-tuple-element.104), channel_id=1, source_target_pairs={{0,1},{1,0},{2,3},{3,2},{4,5},{5,4},{6,7},{7,6},{8,9},{9,8},{10,11... | collective-permute-start | bytes 393224 | tf_op jit(solution)/shard_map/ppermute | solution.py:231
  71.0 1.5 %collective-permute-start.19 = (bf16[64,1024]{1,0:T(8,128)(2,1)S(1)}, bf16[64,1024]{1,0:T(8,128)(2,1)S(1)}, u32[]{:S(2)}, u32[]{:S(2)}) collective-permute-start(bf16[64,1024]{1,0:T(8,128)(2,1)S(1)} %get-tuple-element.103), channel_id=1, source_target_pairs={{0,1},{1,0},{2,3},{3,2},{4,5},{5,4},{6,7},{7,6},{8,9},{9,8},{10,11... | collective-permute-start | bytes 393224 | tf_op jit(solution)/shard_map/ppermute | solution.py:231

commit v4 on v3

--- a/solution.py
+++ b/solution.py
@@ -241,7 +241,7 @@
     swap_high = hop(lambda x, z, y, c: (x, z ^ 1, y, c) if z >= 2 else None)
 
     chunk = math.gcd(tokens, 512)
-    tables = [[] for _ in range(6)]
+    tables = [[] for _ in range(7)]
     for i in range(32):
         ix, iz, iy, ic = i // 16, (i // 4) % 4, (i // 2) % 2, i % 2
         blocks = [2 * iy + ic, 2 * iy + 1 - ic, 2 * (1 - iy) + ic, 2 * (1 - iy) + 1 - ic]
@@ -258,9 +258,10 @@
         )
         planes = [iz, iz - 1 if iz % 2 else -1, iz - 2, (iz ^ 1) - 2 if iz >= 2 else -1]
         calls = [(1, 1 - iy, planes[:1]), (2, 1 - iy, planes[3:])]
-        calls += [(3, iy, planes), (4, 1 - iy, planes[1:3])]
+        calls += [(3, iy, planes), (4, 1 - iy, planes[1:3]), (6, iy, planes)]
         for at, iy_rows, some in calls:
-            first = [(4 * iz + 2 * iy_rows + core) * rows for core in (ic, 1 - ic)]
+            cores = {3: [1 - ic], 6: [ic]}.get(at, [ic, 1 - ic])
+            first = [(4 * iz + 2 * iy_rows + core) * rows for core in cores]
             kinds = [max(plane, 0) // 2 for plane in some]
             tables[at].append(first + some + kinds)
     widths = [len(t[0]) for t in tables]
@@ -286,7 +287,8 @@
         [(4 * z + 2 * y + c) * rows, (4 * z + 2 * y + 1 - c) * rows],
     ]
     starts, lowest = zip(*[attend_starts(doc_ids, first, rows) for first in firsts])
-    for at, low in ((1, 0), (2, 0), (3, 1), (4, 0)):
+    starts = [starts[0], starts[1][:rows], starts[1][rows:]]
+    for at, low in ((1, 0), (2, 0), (3, 1), (4, 0), (6, 1)):
         places[at] = jnp.concatenate([places[at], lowest[low]])
     q_own, *q_away = [
         lax.dynamic_slice_in_dim(queries, h * columns, columns, 1)
@@ -322,7 +324,9 @@
     back = [to_y(across[0]), to_both(across[1])]
     stored = own + below + other
     across, places[3] = lax.optimization_barrier((across, places[3]))
-    here, beside = attend(places[3], starts[1], [q_own, q_core], stored, tokens, chunk)
+    (beside,) = attend(places[3], starts[2], [q_core], stored, tokens, chunk)
+    beside, places[6] = lax.optimization_barrier((beside, places[6]))
+    (here,) = attend(places[6], starts[1], [q_own], stored, tokens, chunk)
     halves = [to_core(beside[: rows // 2]), to_core(beside[rows // 2 :])]
     here, halves, back = lax.optimization_barrier((here, halves, back))
     same_y = [here, jnp.concatenate(halves, axis=0)]

time: 77.5 us -> 78.4 us (1.012)
  waiting for transfers between devices: 17.5 us -> 11.8 us
  Pallas kernels: 18.8 us -> 23 us
  other arithmetic: 8.39 us -> 10.4 us
  starting transfers between devices: 22.1 us -> 23.6 us
    ppermute x22, waiting for transfers between devices: 17.5 us -> 11.8 us  [hop(): return lambda v: lax.ppermute(v, AXES, pairs)]
    pallas_call x4 -> x5, Pallas kernels: 13.8 us -> 18 us  [attend(): pl.pallas_call(lambda *refs: attend_kernel(rows, chunk, n_q, n_kv, bool(s...]
    concatenate x4 -> x5, other arithmetic: 2.47 us -> 4.26 us  [by_planes(): places[at] = jnp.concatenate([places[at], lowest[low]])]
    ppermute x22, starting transfers between devices: 22.1 us -> 23.6 us  [hop(): return lambda v: lax.ppermute(v, AXES, pairs)]
    broadcast_in_dim x2 -> x3, local copies, waits for them, and re-layouts: 2.19 us -> 1.51 us  [attend_starts(): jnp.broadcast_to(starts[:, None], (starts.shape[0], HD))]
  transfers between devices with their start and end apart: 22 -> 22, of which waited for: 10 -> 7; matrix products, arithmetic and copies ran while one was open for 19% -> 21% of each run, Pallas kernels for 23% -> 27%
where the time goes in v4:
time: 78.4 us; the launch traced here: 77.6 us
  starting transfers between devices  23.6 us (30%)
  Pallas kernels  23 us (29%)
  waiting for transfers between devices  11.8 us (15%)
  other arithmetic  10.4 us (13%)
  local copies, waits for them, and re-layouts  8.47 us (11%)
    ppermute x22, starting transfers between devices, hop(): return lambda v: lax.ppermute(v, AXES, pairs)  23.6 us
    pallas_call x5, Pallas kernels, attend(): pl.pallas_call(lambda *refs: attend_kernel(rows, chunk, n_q, n_kv, bool(s...  18 us
    ppermute x22, waiting for transfers between devices, hop(): return lambda v: lax.ppermute(v, AXES, pairs)  11.8 us
    pallas_call x2, Pallas kernels, project(): pl.pallas_call(lambda *refs: project_kernel(rows, n, len(pieces), *refs),...  5 us
    concatenate x5, other arithmetic, by_planes(): places[at] = jnp.concatenate([places[at], lowest[low]])  4.26 us
    dynamic_slice x1, local copies, waits for them, and re-layouts, by_planes(): lax.dynamic_slice_in_dim(queries, h * columns, columns, 1)  2.28 us
    dynamic_slice x1, local copies, waits for them, and re-layouts, by_planes(): far_0 = far(lax.dynamic_slice_in_dim(weight, x * part, part, 0))  1.67 us
  transfers between devices with their start and end apart: 22, of which 7 were waited for; matrix products, arithmetic and copies ran while one was open for 21% of the time, Pallas kernels for 27%

profile of v4, /device:TPU:29, one launch (start us, length us, event | category | flops | bytes accessed | tf_op | source)
XLA Modules:
  0.0 77.6 jit_solution(11526544064459814666)
XLA Ops:
  0.0 1.7 %dynamic-slice_bitcast_fusion = bf16[32,4096]{1,0:T(8,128)(2,1)} fusion(bf16[4096,64]{0,1:T(8,128)(2,1)} %param.7, s32[]{:T(128)S(6)} %select_n.115), kind=kLoop, calls=%fused_computation.8 | loop fusion | bytes 524292 | tf_op jit(solution)/shard_map/dynamic_slice | solution.py:276
  1.9 0.9 %collective-permute-start.9 = (bf16[64,4096]{1,0:T(8,128)(2,1)}, bf16[64,4096]{1,0:T(8,128)(2,1)}, u32[]{:S(2)}, u32[]{:S(2)}) collective-permute-start(bf16[64,4096]{1,0:T(8,128)(2,1)} %bitcast.20), channel_id=1, source_target_pairs={{0,4},{1,5},{2,6},{3,7},{4,0},{5,1},{6,2},{7,3},{8,12},{9,13},{10,... | collective-permute-start | bytes 1572872 | tf_op jit(solution)/shard_map/ppermute | solution.py:231
  3.7 0.9 %fusion.2 = (s32[128]{0:T(128)S(1)}, s32[128]{0:T(128)S(1)}, s32[128]{0:T(128)S(1)}, s32[128]{0:T(128)S(1)}) fusion(s32[2048]{0:T(1024)} %param.8, s32[]{:T(128)S(6)} %select_n.117, s32[]{:T(128)S(6)} %select_n.118, s32[]{:T(128)S(6)} %select_n.120, s32[]{:T(128)S(6)} %select_n.119), kind=kLoop, calls=%fused_computation.42 | loop fusion | bytes 4112 | tf_op jit(solution)/shard_map/dynamic_slice | solution.py:134
  4.6 1.2 %convert_reduce_fusion = (s32[256]{0:T(256)S(1)}, s32[256]{0:T(256)S(1)}) fusion(s32[2048]{0:T(1024)} %param.8, s32[256]{0:T(256)S(1)} %get-tuple-element.123, s32[256]{0:T(256)S(1)} %get-tuple-element.122), kind=kLoop, calls=%fused_computation | loop fusion | flops 3145216 | bytes 12288 | tf_op jit(solution)/shard_map/reduce_sum | solution.py:136
  9.5 1.0 %fusion = (f32[512,64]{1,0:T(8,128)S(1)}, f32[512,64]{1,0:T(8,128)S(1)}, f32[512,64]{1,0:T(8,128)S(1)}) fusion(f32[64]{0:T(128)S(1)} %multiply_power_fusion, f32[512]{0:T(512)S(1)} %add_convert_fusion), kind=kLoop, calls=%fused_computation.17 | loop fusion | flops 65536 | bytes 395520 | tf_op jit(solution)/shard_map/neg | solution.py:284
  10.8 2.3 %constant_dynamic-slice_fusion = (bf16[128,1024]{1,0:T(8,128)(2,1)}, bf16[128,1024]{1,0:T(8,128)(2,1)}, bf16[128,1024]{1,0:T(8,128)(2,1)}, bf16[128,1024]{1,0:T(8,128)(2,1)}) fusion(bf16[128,4096]{1,0:T(8,128)(2,1)} %param.6, s32[]{:T(128)S(6)} %select_n.125, s32[]{:T(128)S(6)} %select_n.123, s32[]{:T(128)S(6)} %select_n.122, s32[]{:T(128)S(6)} %select_n.124), kind=kLoop, calls=%fused_computation.21 | loop fusion | bytes 2097168 | tf_op jit(solution)/shard_map/dynamic_slice | solution.py:294
  14.8 1.3 %pad_add_fusion.5.refs_0_ = s32[7]{0:T(128)} fusion(s32[1]{0:T(128)} %bitcast.3, s32[6]{0:T(128)S(1)} %slice_bitcast_fusion.2), kind=kLoop, calls=%fused_computation.31 | loop fusion | flops 7 | bytes 56 | tf_op jit(solution)/shard_map/concatenate | solution.py:292
  18.3 1.2 %collective-permute-start.3 = (bf16[32,4096]{1,0:T(8,128)(2,1)S(1)}, bf16[32,4096]{1,0:T(8,128)(2,1)}, u32[]{:S(2)}, u32[]{:S(2)}) collective-permute-start(bf16[32,4096]{1,0:T(8,128)(2,1)S(1)} %collective-permute-done.refs_7_), channel_id=1, source_target_pairs={{0,16},{1,17},{2,18},{3,19},{4,20},{5,21},{6,22},{7,23},{8,24},{9,... | collective-permute-start | bytes 786440 | tf_op jit(solution)/shard_map/ppermute | solution.py:231
  19.5 1.8 %collective-permute-start.4 = (bf16[128,1024]{1,0:T(8,128)(2,1)}, bf16[128,1024]{1,0:T(8,128)(2,1)}, u32[]{:S(2)}, u32[]{:S(2)}) collective-permute-start(bf16[128,1024]{1,0:T(8,128)(2,1)} %get-tuple-element.55), channel_id=1, source_target_pairs={{0,1},{1,0},{2,3},{3,2},{4,5},{5,4},{6,7},{7,6},{8,9},{9,8},{10,11... | collective-permute-start | bytes 786440 | tf_op jit(solution)/shard_map/ppermute | solution.py:231
  21.3 4.9 %collective-permute-done.2.refs_9_ = bf16[32,4096]{1,0:T(8,128)(2,1)} collective-permute-done((bf16[32,4096]{1,0:T(8,128)(2,1)S(1)}, bf16[32,4096]{1,0:T(8,128)(2,1)}, u32[]{:S(2)}, u32[]{:S(2)}) %collective-permute-start.2) | collective-permute-done | bytes 262176 | tf_op jit(solution)/shard_map/ppermute | solution.py:231
  26.2 1.6 %collective-permute-start.7 = (bf16[128,4096]{1,0:T(8,128)(2,1)S(1)}, bf16[128,4096]{1,0:T(8,128)(2,1)S(1)}, u32[]{:S(2)}, u32[]{:S(2)}) collective-permute-start(bf16[128,4096]{1,0:T(8,128)(2,1)S(1)} %copy-done), channel_id=1, source_target_pairs={{0,1},{1,0},{2,3},{3,2},{4,5},{5,4},{6,7},{7,6},{8,9},{9,8},{10,11... | collective-permute-start | bytes 3145736 | tf_op jit(solution)/shard_map/ppermute | solution.py:231
  27.9 1.1 %broadcast_select_fusion = bf16[64,4096]{1,0:T(8,128)(2,1)S(1)} fusion(bf16[64,4096]{1,0:T(8,128)(2,1)} %collective-permute-done.9.refs_8_, pred[]{:T(512)S(6)} %eq.29, bf16[4096,64]{0,1:T(8,128)(2,1)S(1)} %copy-done.1), kind=kLoop, calls=%fused_computation.3 | loop fusion | flops 262144 | bytes 1572865 | tf_op jit(solution)/shard_map/jit(_where)/select_n | solution.py:303
  29.1 1.3 %collective-permute-start.11 = (bf16[32,4096]{1,0:T(8,128)(2,1)}, bf16[32,4096]{1,0:T(8,128)(2,1)S(1)}, u32[]{:S(2)}, u32[]{:S(2)}) collective-permute-start(bf16[32,4096]{1,0:T(8,128)(2,1)} %collective-permute-done.2.refs_9_), channel_id=1, source_target_pairs={{0,16},{1,17},{2,18},{3,19},{4,20},{5,21},{6,22},{7,23},{8,24},{9,... | collective-permute-start | bytes 786440 | tf_op jit(solution)/shard_map/ppermute | solution.py:231
  30.4 1.2 %collective-permute-start.5 = (bf16[128,1024]{1,0:T(8,128)(2,1)S(1)}, bf16[128,1024]{1,0:T(8,128)(2,1)S(1)}, u32[]{:S(2)}, u32[]{:S(2)}) collective-permute-start(bf16[128,1024]{1,0:T(8,128)(2,1)S(1)} %copy-done.11), channel_id=1, source_target_pairs={{0,2},{1,3},{2,0},{3,1},{4,6},{5,7},{6,4},{7,5},{8,10},{9,11},{10,... | collective-permute-start | bytes 786440 | tf_op jit(solution)/shard_map/ppermute | solution.py:231
  32.3 1.5 %collective-permute-start.6 = (bf16[128,1024]{1,0:T(8,128)(2,1)S(1)}, bf16[128,1024]{1,0:T(8,128)(2,1)S(1)}, u32[]{:S(2)}, u32[]{:S(2)}) collective-permute-start(bf16[128,1024]{1,0:T(8,128)(2,1)S(1)} %copy-done.10), channel_id=1, source_target_pairs={{0,3},{1,2},{2,1},{3,0},{4,7},{5,6},{6,5},{7,4},{8,11},{9,10},{10,... | collective-permute-start | bytes 786440 | tf_op jit(solution)/shard_map/ppermute | solution.py:231
  33.9 2.5 %project.2.refs_4_.refs_3_ = bf16[512,128]{1,0:T(8,128)(2,1)S(1)} custom-call(s32[11]{0:T(128)S(1)} %copy-done.9, f32[512,128]{1,0:T(8,128)S(1)} %get-tuple-element.62.refs_1_, f32[512,128]{1,0:T(8,128)S(1)} %get-tuple-element.63.refs_2_, bf16[128,4096]{1,0:T(8,128)(2,1)S(1)} %copy-done, bf16[128,4096]{1,0:T(8,128)(2,1)S(1)} %collective-permute-done.7.refs_4_, ...), custom_call_target="tpu_custom_call" | custom-call | flops 67108864 | bytes 524288 | tf_op jit(solution)/shard_map/project/pallas_call | solution.py:199
  36.4 1.3 %collective-permute-start.12 = (bf16[512,128]{1,0:T(8,128)(2,1)S(1)}, bf16[512,128]{1,0:T(8,128)(2,1)S(1)}, u32[]{:S(2)}, u32[]{:S(2)}) collective-permute-start(bf16[512,128]{1,0:T(8,128)(2,1)S(1)} %project.2.refs_4_.refs_3_), channel_id=1, source_target_pairs={{0,8},{1,9},{2,10},{3,11},{4,12},{5,13},{6,14},{7,15},{16,24},{17,... | collective-permute-start | bytes 393224 | tf_op jit(solution)/shard_map/ppermute | solution.py:231
  37.7 2.5 %project.3.refs_5_.refs_4_ = bf16[512,128]{1,0:T(8,128)(2,1)S(1)} custom-call(s32[13]{0:T(128)S(1)} %copy-done.8, f32[512,128]{1,0:T(8,128)S(1)} %get-tuple-element.62.refs_1_, f32[512,128]{1,0:T(8,128)S(1)} %get-tuple-element.63.refs_2_, bf16[128,4096]{1,0:T(8,128)(2,1)S(1)} %copy-done, bf16[128,4096]{1,0:T(8,128)(2,1)S(1)} %collective-permute-done.7.refs_4_, ...), custom_call_target="tpu_custom_call" | custom-call | flops 67108864 | bytes 524288 | tf_op jit(solution)/shard_map/project/pallas_call | solution.py:199
  40.2 1.3 %collective-permute-start.14 = (bf16[512,128]{1,0:T(8,128)(2,1)S(1)}, bf16[512,128]{1,0:T(8,128)(2,1)S(1)}, u32[]{:S(2)}, u32[]{:S(2)}) collective-permute-start(bf16[512,128]{1,0:T(8,128)(2,1)S(1)} %project.3.refs_5_.refs_4_), channel_id=1, source_target_pairs={{0,8},{1,9},{2,10},{3,11},{4,12},{5,13},{6,14},{7,15},{16,24},{17,... | collective-permute-start | bytes 393224 | tf_op jit(solution)/shard_map/ppermute | solution.py:231
  41.5 1.3 %collective-permute-start.17 = (bf16[512,128]{1,0:T(8,128)(2,1)S(1)}, bf16[512,128]{1,0:T(8,128)(2,1)S(1)}, u32[]{:S(2)}, u32[]{:S(2)}) collective-permute-start(bf16[512,128]{1,0:T(8,128)(2,1)S(1)} %project.3.refs_5_.refs_4_), channel_id=1, source_target_pairs={{0,4},{1,5},{2,6},{3,7},{8,12},{9,13},{10,14},{11,15},{16,20},{17,... | collective-permute-start | bytes 393224 | tf_op jit(solution)/shard_map/ppermute | solution.py:231
  42.8 1.3 %collective-permute-start.16 = (bf16[512,128]{1,0:T(8,128)(2,1)S(1)}, bf16[512,128]{1,0:T(8,128)(2,1)S(1)}, u32[]{:S(2)}, u32[]{:S(2)}) collective-permute-start(bf16[512,128]{1,0:T(8,128)(2,1)S(1)} %project.2.refs_4_.refs_3_), channel_id=1, source_target_pairs={{0,4},{1,5},{2,6},{3,7},{8,12},{9,13},{10,14},{11,15},{16,20},{17,... | collective-permute-start | bytes 393224 | tf_op jit(solution)/shard_map/ppermute | solution.py:231
  44.3 1.9 %attend.5 = (f32[2048,128]{1,0:T(8,128)S(1)}, f32[2048,128]{1,0:T(8,128)S(1)}, f32[2048,128]{1,0:T(8,128)S(1)}) custom-call(s32[5]{0:T(128)S(1)} %pad_add_fusion.2.refs_0_, s32[256,128]{1,0:T(8,128)S(1)} %broadcast_in_dim.10.refs_1_, bf16[128,1024]{1,0:T(8,128)(2,1)S(1)} %collective-permute-done.5.refs_2_, ...), custom_call_target="tpu_custom_call" | custom-call | flops 67108864 | bytes 524288 | tf_op jit(solution)/shard_map/attend/pallas_call | solution.py:149
  46.3 3.1 %collective-permute-done.12.refs_6_.refs_7_ = bf16[512,128]{1,0:T(8,128)(2,1)S(1)} collective-permute-done((bf16[512,128]{1,0:T(8,128)(2,1)S(1)}, bf16[512,128]{1,0:T(8,128)(2,1)S(1)}, u32[]{:S(2)}, u32[]{:S(2)}) %collective-permute-start.12) | collective-permute-done | bytes 131104 | tf_op jit(solution)/shard_map/ppermute | solution.py:231
  49.4 1.9 %collective-permute-start.13 = (bf16[512,128]{1,0:T(8,128)(2,1)S(1)}, bf16[512,128]{1,0:T(8,128)(2,1)S(1)}, u32[]{:S(2)}, u32[]{:S(2)}) collective-permute-start(bf16[512,128]{1,0:T(8,128)(2,1)S(1)} %collective-permute-done.12.refs_6_.refs_7_), channel_id=1, source_target_pairs={{8,12},{9,13},{10,14},{11,15},{12,8},{13,9},{14,10},{15,11},{24,28... | collective-permute-start | bytes 393224 | tf_op jit(solution)/shard_map/ppermute | solution.py:231
  52.2 2.7 %collective-permute-start.15 = (bf16[512,128]{1,0:T(8,128)(2,1)S(1)}, bf16[512,128]{1,0:T(8,128)(2,1)S(1)}, u32[]{:S(2)}, u32[]{:S(2)}) collective-permute-start(bf16[512,128]{1,0:T(8,128)(2,1)S(1)} %collective-permute-done.14.refs_7_.refs_8_), channel_id=1, source_target_pairs={{8,12},{9,13},{10,14},{11,15},{12,8},{13,9},{14,10},{15,11},{24,28... | collective-permute-start | bytes 393224 | tf_op jit(solution)/shard_map/ppermute | solution.py:231
  54.9 4.4 %attend.6 = (f32[2048,128]{1,0:T(8,128)S(1)}, f32[2048,128]{1,0:T(8,128)S(1)}, f32[2048,128]{1,0:T(8,128)S(1)}) custom-call(s32[7]{0:T(128)S(1)} %copy-done.7, s32[256,128]{1,0:T(8,128)S(1)} %broadcast_in_dim.10.refs_1_, bf16[128,1024]{1,0:T(8,128)(2,1)S(1)} %collective-permute-done.5.refs_2_, bf16[128,1024]{1,0:T(8,128)(2,1)S(1)} %collective-permute-done.6.refs_3_, ...), custom_call_target="tpu_custom_call" | custom-call | flops 67108864 | bytes 524288 | tf_op jit(solution)/shard_map/attend/pallas_call | solution.py:149
  59.3 1.1 %collective-permute-done.15.refs_5_.refs_10_ = bf16[512,128]{1,0:T(8,128)(2,1)S(1)} collective-permute-done((bf16[512,128]{1,0:T(8,128)(2,1)S(1)}, bf16[512,128]{1,0:T(8,128)(2,1)S(1)}, u32[]{:S(2)}, u32[]{:S(2)}) %collective-permute-start.15) | collective-permute-done | bytes 131104 | tf_op jit(solution)/shard_map/ppermute | solution.py:231
  60.5 2.2 %attend.7 = (bf16[128,1024]{1,0:T(8,128)(2,1)S(1)}, bf16[128,1024]{1,0:T(8,128)(2,1)S(1)}) custom-call(s32[5]{0:T(128)S(1)} %pad_add_fusion.3.refs_0_, s32[256,128]{1,0:T(8,128)S(1)} %broadcast_in_dim.10.refs_1_, bf16[128,1024]{1,0:T(8,128)(2,1)S(1)} %collective-permute-done.5.refs_2_, bf16[128,1024]{1,0:T(8,128)(2,1)S(1)} %collective-permute-done.6.refs_3_, ...), custom_call_target="tpu_custom_call" | custom-call | flops 67108864 | bytes 524288 | tf_op jit(solution)/shard_map/attend/pallas_call | solution.py:149
  62.8 2.8 %collective-permute-start.21 = (bf16[128,1024]{1,0:T(8,128)(2,1)S(1)}, bf16[128,1024]{1,0:T(8,128)(2,1)S(1)}, u32[]{:S(2)}, u32[]{:S(2)}) collective-permute-start(bf16[128,1024]{1,0:T(8,128)(2,1)S(1)} %get-tuple-element.82), channel_id=1, source_target_pairs={{0,3},{1,2},{2,1},{3,0},{4,7},{5,6},{6,5},{7,4},{8,11},{9,10},{10,... | collective-permute-start | bytes 786440 | tf_op jit(solution)/shard_map/ppermute | solution.py:231
  65.6 4.9 %attend.8 = bf16[128,1024]{1,0:T(8,128)(2,1)S(1)} custom-call(s32[10]{0:T(128)S(1)} %pad_add_fusion.4.refs_0_, s32[128,128]{1,0:T(8,128)S(1)} %copy-done.6, bf16[128,1024]{1,0:T(8,128)(2,1)} %collective-permute-done.4.refs_2_, bf16[512,128]{1,0:T(8,128)(2,1)S(1)} %project.2.refs_4_.refs_3_, bf16[512,128]{1,0:T(8,128)(2,1)S(1)} %project.3.refs_5_.refs_4_, ...), custom_call_target="tpu_custom_call" | custom-call | flops 33554432 | bytes 262144 | tf_op jit(solution)/shard_map/attend/pallas_call | solution.py:149
  71.1 4.5 %attend.9 = bf16[128,1024]{1,0:T(8,128)(2,1)S(1)} custom-call(s32[10]{0:T(128)S(1)} %pad_add_fusion.6.refs_0_, s32[128,128]{1,0:T(8,128)S(1)} %copy-done.5, bf16[128,1024]{1,0:T(8,128)(2,1)S(1)} %copy-done.2, bf16[512,128]{1,0:T(8,128)(2,1)S(1)} %project.2.refs_4_.refs_3_, bf16[512,128]{1,0:T(8,128)(2,1)S(1)} %project.3.refs_5_.refs_4_, ...), custom_call_target="tpu_custom_call" | custom-call | flops 33554432 | bytes 262144 | tf_op jit(solution)/shard_map/attend/pallas_call | solution.py:149
  76.5 1.0 %pad_maximum_fusion = bf16[128,4096]{1,0:T(8,128)(2,1)} fusion(bf16[128,1024]{1,0:T(8,128)(2,1)S(1)} %get-tuple-element.100, bf16[128,1024]{1,0:T(8,128)(2,1)S(1)} %get-tuple-element.102, bf16[128,1024]{1,0:T(8,128)(2,1)S(1)} %get-tuple-element.101, bf16[128,1024]{1,0:T(8,128)(2,1)S(1)} %get-tuple-element.99), kind=kLoop, calls=%fused_computation.2 | loop fusion | flops 4194304 | bytes 2097152 | tf_op jit(solution)/shard_map/concatenate | solution.py:338
  (79 shorter events, 12.4 us)
Async XLA Ops:
  1.7 14.5 %collective-permute-start = (bf16[32,4096]{1,0:T(8,128)(2,1)}, bf16[32,4096]{1,0:T(8,128)(2,1)S(1)}, u32[]{:S(2)}, u32[]{:S(2)}) collective-permute-start(bf16[32,4096]{1,0:T(8,128)(2,1)} %dynamic-slice_bitcast_fusion), channel_id=1, source_target_pairs={{0,8},{1,12},{2,10},{3,14},{4,13},{5,9},{6,15},{7,11},{8,0},{9,4},... | collective-permute-start | bytes 786440 | tf_op jit(solution)/shard_map/ppermute | solution.py:231
  1.7 26.1 %collective-permute-start.1 = (bf16[128,4096]{1,0:T(8,128)(2,1)}, bf16[128,4096]{1,0:T(8,128)(2,1)S(1)}, u32[]{:S(2)}, u32[]{:S(2)}) collective-permute-start(bf16[128,4096]{1,0:T(8,128)(2,1)} %refs_3_.3), channel_id=1, source_target_pairs={{0,2},{1,3},{2,0},{3,1},{4,6},{5,7},{6,4},{7,5},{8,10},{9,11},{10,... | collective-permute-start | bytes 3145736 | tf_op jit(solution)/shard_map/ppermute | solution.py:231
  1.9 26.0 %collective-permute-start.9 = (bf16[64,4096]{1,0:T(8,128)(2,1)}, bf16[64,4096]{1,0:T(8,128)(2,1)}, u32[]{:S(2)}, u32[]{:S(2)}) collective-permute-start(bf16[64,4096]{1,0:T(8,128)(2,1)} %bitcast.20), channel_id=1, source_target_pairs={{0,4},{1,5},{2,6},{3,7},{4,0},{5,1},{6,2},{7,3},{8,12},{9,13},{10,... | collective-permute-start | bytes 1572872 | tf_op jit(solution)/shard_map/ppermute | solution.py:231
  10.8 15.5 %copy-start = (bf16[128,4096]{1,0:T(8,128)(2,1)S(1)}, bf16[128,4096]{1,0:T(8,128)(2,1)}, u32[]{:S(2)}) copy-start(bf16[128,4096]{1,0:T(8,128)(2,1)} %refs_3_.3) | copy-start | bytes 3145732
  10.8 17.1 %copy-start.1 = (bf16[4096,64]{0,1:T(8,128)(2,1)S(1)}, bf16[4096,64]{0,1:T(8,128)(2,1)}, u32[]{:S(2)}) copy-start(bf16[4096,64]{0,1:T(8,128)(2,1)} %param.7) | copy-start | bytes 1572868
  16.2 17.6 %copy-start.3 = (bf16[32,4096]{1,0:T(8,128)(2,1)}, bf16[32,4096]{1,0:T(8,128)(2,1)S(1)}, u32[]{:S(2)}) copy-start(bf16[32,4096]{1,0:T(8,128)(2,1)S(1)} %collective-permute-done.refs_7_) | copy-start | bytes 786436
  17.7 8.5 %collective-permute-start.2 = (bf16[32,4096]{1,0:T(8,128)(2,1)S(1)}, bf16[32,4096]{1,0:T(8,128)(2,1)}, u32[]{:S(2)}, u32[]{:S(2)}) collective-permute-start(bf16[32,4096]{1,0:T(8,128)(2,1)S(1)} %collective-permute-done.refs_7_), channel_id=1, source_target_pairs={{0,4},{1,5},{2,6},{3,7},{4,0},{5,1},{6,2},{7,3},{8,12},{9,13},{10,... | collective-permute-start | bytes 786440 | tf_op jit(solution)/shard_map/ppermute | solution.py:231
  18.3 9.5 %collective-permute-start.3 = (bf16[32,4096]{1,0:T(8,128)(2,1)S(1)}, bf16[32,4096]{1,0:T(8,128)(2,1)}, u32[]{:S(2)}, u32[]{:S(2)}) collective-permute-start(bf16[32,4096]{1,0:T(8,128)(2,1)S(1)} %collective-permute-done.refs_7_), channel_id=1, source_target_pairs={{0,16},{1,17},{2,18},{3,19},{4,20},{5,21},{6,22},{7,23},{8,24},{9,... | collective-permute-start | bytes 786440 | tf_op jit(solution)/shard_map/ppermute | solution.py:231
  19.5 8.3 %collective-permute-start.4 = (bf16[128,1024]{1,0:T(8,128)(2,1)}, bf16[128,1024]{1,0:T(8,128)(2,1)}, u32[]{:S(2)}, u32[]{:S(2)}) collective-permute-start(bf16[128,1024]{1,0:T(8,128)(2,1)} %get-tuple-element.55), channel_id=1, source_target_pairs={{0,1},{1,0},{2,3},{3,2},{4,5},{5,4},{6,7},{7,6},{8,9},{9,8},{10,11... | collective-permute-start | bytes 786440 | tf_op jit(solution)/shard_map/ppermute | solution.py:231
  21.3 9.1 %copy-start.11 = (bf16[128,1024]{1,0:T(8,128)(2,1)S(1)}, bf16[128,1024]{1,0:T(8,128)(2,1)}, u32[]{:S(2)}) copy-start(bf16[128,1024]{1,0:T(8,128)(2,1)} %get-tuple-element.58) | copy-start | bytes 786436
  21.3 11.0 %copy-start.10 = (bf16[128,1024]{1,0:T(8,128)(2,1)S(1)}, bf16[128,1024]{1,0:T(8,128)(2,1)}, u32[]{:S(2)}) copy-start(bf16[128,1024]{1,0:T(8,128)(2,1)} %get-tuple-element.59) | copy-start | bytes 786436
  21.3 12.5 %copy-start.9 = (s32[11]{0:T(128)S(1)}, s32[11]{0:T(128)}, u32[]{:S(2)}) copy-start(s32[11]{0:T(128)} %slice_bitcast_fusion.6.refs_0_) | copy-start | bytes 136
  26.2 7.6 %collective-permute-start.7 = (bf16[128,4096]{1,0:T(8,128)(2,1)S(1)}, bf16[128,4096]{1,0:T(8,128)(2,1)S(1)}, u32[]{:S(2)}, u32[]{:S(2)}) collective-permute-start(bf16[128,4096]{1,0:T(8,128)(2,1)S(1)} %copy-done), channel_id=1, source_target_pairs={{0,1},{1,0},{2,3},{3,2},{4,5},{5,4},{6,7},{7,6},{8,9},{9,8},{10,11... | collective-permute-start | bytes 3145736 | tf_op jit(solution)/shard_map/ppermute | solution.py:231
  27.8 6.0 %collective-permute-start.8 = (bf16[128,4096]{1,0:T(8,128)(2,1)S(1)}, bf16[128,4096]{1,0:T(8,128)(2,1)S(1)}, u32[]{:S(2)}, u32[]{:S(2)}) collective-permute-start(bf16[128,4096]{1,0:T(8,128)(2,1)S(1)} %collective-permute-done.1.refs_5_), channel_id=1, source_target_pairs={{0,1},{1,0},{2,3},{3,2},{4,5},{5,4},{6,7},{7,6},{8,9},{9,8},{10,11... | collective-permute-start | bytes 3145736 | tf_op jit(solution)/shard_map/ppermute | solution.py:231
  29.0 8.7 %copy-start.8 = (s32[13]{0:T(128)S(1)}, s32[13]{0:T(128)}, u32[]{:S(2)}) copy-start(s32[13]{0:T(128)} %slice_bitcast_fusion.1.refs_0_) | copy-start | bytes 160
  29.0 3.3 %collective-permute-start.10 = (bf16[64,4096]{1,0:T(8,128)(2,1)S(1)}, bf16[64,4096]{1,0:T(8,128)(2,1)S(1)}, u32[]{:S(2)}, u32[]{:S(2)}) collective-permute-start(bf16[64,4096]{1,0:T(8,128)(2,1)S(1)} %broadcast_select_fusion), channel_id=1, source_target_pairs={{0,1},{1,0},{2,3},{3,2},{4,5},{5,4},{6,7},{7,6},{8,9},{9,8},{10,11... | collective-permute-start | bytes 1572872 | tf_op jit(solution)/shard_map/ppermute | solution.py:231
  29.1 8.6 %collective-permute-start.11 = (bf16[32,4096]{1,0:T(8,128)(2,1)}, bf16[32,4096]{1,0:T(8,128)(2,1)S(1)}, u32[]{:S(2)}, u32[]{:S(2)}) collective-permute-start(bf16[32,4096]{1,0:T(8,128)(2,1)} %collective-permute-done.2.refs_9_), channel_id=1, source_target_pairs={{0,16},{1,17},{2,18},{3,19},{4,20},{5,21},{6,22},{7,23},{8,24},{9,... | collective-permute-start | bytes 786440 | tf_op jit(solution)/shard_map/ppermute | solution.py:231
  30.4 12.4 %collective-permute-start.5 = (bf16[128,1024]{1,0:T(8,128)(2,1)S(1)}, bf16[128,1024]{1,0:T(8,128)(2,1)S(1)}, u32[]{:S(2)}, u32[]{:S(2)}) collective-permute-start(bf16[128,1024]{1,0:T(8,128)(2,1)S(1)} %copy-done.11), channel_id=1, source_target_pairs={{0,2},{1,3},{2,0},{3,1},{4,6},{5,7},{6,4},{7,5},{8,10},{9,11},{10,... | collective-permute-start | bytes 786440 | tf_op jit(solution)/shard_map/ppermute | solution.py:231
  32.3 12.0 %collective-permute-start.6 = (bf16[128,1024]{1,0:T(8,128)(2,1)S(1)}, bf16[128,1024]{1,0:T(8,128)(2,1)S(1)}, u32[]{:S(2)}, u32[]{:S(2)}) collective-permute-start(bf16[128,1024]{1,0:T(8,128)(2,1)S(1)} %copy-done.10), channel_id=1, source_target_pairs={{0,3},{1,2},{2,1},{3,0},{4,7},{5,6},{6,5},{7,4},{8,11},{9,10},{10,... | collective-permute-start | bytes 786440 | tf_op jit(solution)/shard_map/ppermute | solution.py:231
  36.4 18.5 %copy-start.7 = (s32[7]{0:T(128)S(1)}, s32[7]{0:T(128)}, u32[]{:S(2)}) copy-start(s32[7]{0:T(128)} %pad_add_fusion.5.refs_0_) | copy-start | bytes 88
  36.4 13.0 %collective-permute-start.12 = (bf16[512,128]{1,0:T(8,128)(2,1)S(1)}, bf16[512,128]{1,0:T(8,128)(2,1)S(1)}, u32[]{:S(2)}, u32[]{:S(2)}) collective-permute-start(bf16[512,128]{1,0:T(8,128)(2,1)S(1)} %project.2.refs_4_.refs_3_), channel_id=1, source_target_pairs={{0,8},{1,9},{2,10},{3,11},{4,12},{5,13},{6,14},{7,15},{16,24},{17,... | collective-permute-start | bytes 393224 | tf_op jit(solution)/shard_map/ppermute | solution.py:231
  40.2 12.0 %collective-permute-start.14 = (bf16[512,128]{1,0:T(8,128)(2,1)S(1)}, bf16[512,128]{1,0:T(8,128)(2,1)S(1)}, u32[]{:S(2)}, u32[]{:S(2)}) collective-permute-start(bf16[512,128]{1,0:T(8,128)(2,1)S(1)} %project.3.refs_5_.refs_4_), channel_id=1, source_target_pairs={{0,8},{1,9},{2,10},{3,11},{4,12},{5,13},{6,14},{7,15},{16,24},{17,... | collective-permute-start | bytes 393224 | tf_op jit(solution)/shard_map/ppermute | solution.py:231
  41.5 13.3 %collective-permute-start.17 = (bf16[512,128]{1,0:T(8,128)(2,1)S(1)}, bf16[512,128]{1,0:T(8,128)(2,1)S(1)}, u32[]{:S(2)}, u32[]{:S(2)}) collective-permute-start(bf16[512,128]{1,0:T(8,128)(2,1)S(1)} %project.3.refs_5_.refs_4_), channel_id=1, source_target_pairs={{0,4},{1,5},{2,6},{3,7},{8,12},{9,13},{10,14},{11,15},{16,20},{17,... | collective-permute-start | bytes 393224 | tf_op jit(solution)/shard_map/ppermute | solution.py:231
  42.8 12.0 %collective-permute-start.16 = (bf16[512,128]{1,0:T(8,128)(2,1)S(1)}, bf16[512,128]{1,0:T(8,128)(2,1)S(1)}, u32[]{:S(2)}, u32[]{:S(2)}) collective-permute-start(bf16[512,128]{1,0:T(8,128)(2,1)S(1)} %project.2.refs_4_.refs_3_), channel_id=1, source_target_pairs={{0,4},{1,5},{2,6},{3,7},{8,12},{9,13},{10,14},{11,15},{16,20},{17,... | collective-permute-start | bytes 393224 | tf_op jit(solution)/shard_map/ppermute | solution.py:231
  49.4 10.0 %collective-permute-start.13 = (bf16[512,128]{1,0:T(8,128)(2,1)S(1)}, bf16[512,128]{1,0:T(8,128)(2,1)S(1)}, u32[]{:S(2)}, u32[]{:S(2)}) collective-permute-start(bf16[512,128]{1,0:T(8,128)(2,1)S(1)} %collective-permute-done.12.refs_6_.refs_7_), channel_id=1, source_target_pairs={{8,12},{9,13},{10,14},{11,15},{12,8},{13,9},{14,10},{15,11},{24,28... | collective-permute-start | bytes 393224 | tf_op jit(solution)/shard_map/ppermute | solution.py:231
  52.2 8.3 %collective-permute-start.15 = (bf16[512,128]{1,0:T(8,128)(2,1)S(1)}, bf16[512,128]{1,0:T(8,128)(2,1)S(1)}, u32[]{:S(2)}, u32[]{:S(2)}) collective-permute-start(bf16[512,128]{1,0:T(8,128)(2,1)S(1)} %collective-permute-done.14.refs_7_.refs_8_), channel_id=1, source_target_pairs={{8,12},{9,13},{10,14},{11,15},{12,8},{13,9},{14,10},{15,11},{24,28... | collective-permute-start | bytes 393224 | tf_op jit(solution)/shard_map/ppermute | solution.py:231
  62.7 12.9 %collective-permute-start.20 = (bf16[128,1024]{1,0:T(8,128)(2,1)S(1)}, bf16[128,1024]{1,0:T(8,128)(2,1)S(1)}, u32[]{:S(2)}, u32[]{:S(2)}) collective-permute-start(bf16[128,1024]{1,0:T(8,128)(2,1)S(1)} %get-tuple-element.81), channel_id=1, source_target_pairs={{0,2},{1,3},{2,0},{3,1},{4,6},{5,7},{6,4},{7,5},{8,10},{9,11},{10,... | collective-permute-start | bytes 786440 | tf_op jit(solution)/shard_map/ppermute | solution.py:231
  62.8 8.3 %copy-start.2 = (bf16[128,1024]{1,0:T(8,128)(2,1)S(1)}, bf16[128,1024]{1,0:T(8,128)(2,1)}, u32[]{:S(2)}) copy-start(bf16[128,1024]{1,0:T(8,128)(2,1)} %get-tuple-element.90.refs_2_) | copy-start | bytes 786436
  62.8 8.3 %copy-start.5 = (s32[128,128]{1,0:T(8,128)S(1)}, s32[128,128]{1,0:T(8,128)}, u32[]{:S(2)}) copy-start(s32[128,128]{1,0:T(8,128)} %broadcast_in_dim.11.refs_1_) | copy-start | bytes 196612
  62.8 13.6 %collective-permute-start.21 = (bf16[128,1024]{1,0:T(8,128)(2,1)S(1)}, bf16[128,1024]{1,0:T(8,128)(2,1)S(1)}, u32[]{:S(2)}, u32[]{:S(2)}) collective-permute-start(bf16[128,1024]{1,0:T(8,128)(2,1)S(1)} %get-tuple-element.82), channel_id=1, source_target_pairs={{0,3},{1,2},{2,1},{3,0},{4,7},{5,6},{6,5},{7,4},{8,11},{9,10},{10,... | collective-permute-start | bytes 786440 | tf_op jit(solution)/shard_map/ppermute | solution.py:231
  70.5 5.1 %collective-permute-start.18 = (bf16[64,1024]{1,0:T(8,128)(2,1)S(1)}, bf16[64,1024]{1,0:T(8,128)(2,1)S(1)}, u32[]{:S(2)}, u32[]{:S(2)}) collective-permute-start(bf16[64,1024]{1,0:T(8,128)(2,1)S(1)} %get-tuple-element.108), channel_id=1, source_target_pairs={{0,1},{1,0},{2,3},{3,2},{4,5},{5,4},{6,7},{7,6},{8,9},{9,8},{10,11... | collective-permute-start | bytes 393224 | tf_op jit(solution)/shard_map/ppermute | solution.py:231
  70.6 5.0 %collective-permute-start.19 = (bf16[64,1024]{1,0:T(8,128)(2,1)S(1)}, bf16[64,1024]{1,0:T(8,128)(2,1)S(1)}, u32[]{:S(2)}, u32[]{:S(2)}) collective-permute-start(bf16[64,1024]{1,0:T(8,128)(2,1)S(1)} %get-tuple-element.107), channel_id=1, source_target_pairs={{0,1},{1,0},{2,3},{3,2},{4,5},{5,4},{6,7},{7,6},{8,9},{9,8},{10,11... | collective-permute-start | bytes 393224 | tf_op jit(solution)/shard_map/ppermute | solution.py:231
  (4 other events, 15.9 us)
